TPU v7x, 128 devices: a whole 4x4x4 slice. The times are simulated.
128 devices in a mesh: gx: 8 (over z, core), gy: 16 (over y, x).
Axes of the slice: x: 4, y: 4, z: 4, core: 2. Of those that a mesh axis runs over, the one named last changes fastest.
Arguments:
- features: bfloat16 [512, 512, 256], P(('gx', 'gy')), may hold values from -6 to 6
- occupancy: int32 [512, 512], P(('gx', 'gy')), may hold values 0 or 1
- routes: int32 [512, 1], P(('gx', 'gy')), may hold values from 0 to 7; in each aligned block of 4 rows (0 to 3, 4 to 7, ...) no two rows name the same one
- neighbours: int32 [512, 6], P(('gx', 'gy')), may hold values from 0 to 8, as said below
- weight: bfloat16 [27, 256, 256], replicated, may hold values from -0.078125 to 0.078125
- cotangent: bfloat16 [1024, 512, 256], P(('gx', 'gy')), may hold values from -6 to 6
Outputs:
- owned_out: bfloat16 [1024, 512, 256], P(('gx', 'gy'))
- input_grad: bfloat16 [512, 512, 256], P(('gx', 'gy'))
- weight_grad: float32 [27, 256, 256], replicated
Inputs may be any that keep to these rules, and one draw needn't show every extreme that they name: `routes`: at most 1 bricks of one device have the same owner, and some device gives exactly 1 to some owner. `neighbours`: values of the -z and +z columns are under 4 or exactly 8.
All inputs are finite; a program needn't handle non-finite values. No bound on the sum of `occupancy` on one device may be relied on, other than what follows from the above.
Results may differ from a plain program's by a relative error of at most 0.0029.
Values may be sent and summed in bfloat16 or wider, within the bound.
No kernel may reach another device: no remote copies, remote signals or barrier semaphores. Data moves between devices by JAX's collectives and lax.ppermute only.
A program may use at most 192 MiB of HBM per device.

v0:
```python
import jax
import jax.numpy as jnp
import numpy as np
from jax import lax
from jax.sharding import PartitionSpec as P

EDGE = 8
TAPS = 27
V = 512
FACE = 64
PACKED = 896


norm_eps = 1e-06


def from_behind(block, axis, distance):
    devices = range(lax.axis_size(axis))
    route = [(i - distance, i) for i in devices if i - distance in devices]
    return lax.ppermute(block, axis, route)


def shortened(x):
    return jax.tree.map(lambda a: a.astype(jnp.bfloat16) if a.dtype == jnp.float32 else a, x)


def hidden_of(values, occupancy):
    scale = lax.rsqrt(jnp.mean(values * values, axis=-1, keepdims=True) + norm_eps)
    return occupancy[..., None].astype(jnp.float32) * jax.nn.silu(values * scale)


def layer_of(cube, layer_id):
    edge_cells = cube.shape[1]
    side_pos = 0 if layer_id % 2 == 0 else edge_cells - 1
    if layer_id < 2:
        return cube[:, side_pos]
    if layer_id < 4:
        return cube[:, :, side_pos]
    return cube[:, :, :, side_pos]


def add_layer(cube, layer_id, addend):
    edge_cells = cube.shape[1]
    side_pos = 0 if layer_id % 2 == 0 else edge_cells - 1
    if layer_id < 2:
        return cube.at[:, side_pos].add(addend)
    if layer_id < 4:
        return cube.at[:, :, side_pos].add(addend)
    return cube.at[:, :, :, side_pos].add(addend)


def padded_of(cube, faces):
    edge_cells = cube.shape[1]
    inside = slice(1, edge_cells + 1)
    padded = jnp.pad(cube, ((0, 0), (1, 1), (1, 1), (1, 1), (0, 0)))
    padded = padded.at[:, 0, inside, inside].set(faces[0])
    padded = padded.at[:, edge_cells + 1, inside, inside].set(faces[1])
    padded = padded.at[:, inside, 0, inside].set(faces[2])
    padded = padded.at[:, inside, edge_cells + 1, inside].set(faces[3])
    padded = padded.at[:, inside, inside, 0].set(faces[4])
    padded = padded.at[:, inside, inside, edge_cells + 1].set(faces[5])
    return padded


def face_taps(face_id):
    axis_id = face_id // 2
    fixed_tap = 0 if face_id % 2 == 0 else 2
    listing = []
    for tap_a in range(3):
        for tap_b in range(3):
            coords = [tap_a, tap_b]
            coords.insert(axis_id, fixed_tap)
            listing.append((coords[0] * 9 + coords[1] * 3 + coords[2], tap_a, tap_b))
    return listing


def face_slab(grad_grid, face_id, tap_a, tap_b, edge_cells):
    axis_id = face_id // 2
    fixed_pos = 2 if face_id % 2 == 0 else edge_cells + 1
    first_cut = slice(3 - tap_a, 3 - tap_a + edge_cells)
    second_cut = slice(3 - tap_b, 3 - tap_b + edge_cells)
    if axis_id == 0:
        return grad_grid[:, fixed_pos, first_cut, second_cut]
    if axis_id == 1:
        return grad_grid[:, first_cut, fixed_pos, second_cut]
    return grad_grid[:, first_cut, second_cut, fixed_pos]


def tap_triples():
    listing = []
    for tap_x in range(3):
        for tap_y in range(3):
            for tap_z in range(3):
                listing.append((tap_x, tap_y, tap_z))
    return listing


def block_work(packs, dmixed, weight):
    count = packs.shape[0]
    width = packs.shape[2]
    group = min(2, count)
    turns = count // group
    weight_flat = weight.reshape(-1, width)
    turned = jnp.transpose(weight, (0, 2, 1))
    turned_flat = turned.reshape(-1, width)
    face_weights = [
        turned[np.array([entry[0] for entry in face_taps(face_id)])].reshape(-1, width)
        for face_id in range(6)
    ]

    def one_group(kernel_acc, pieces):
        pack_rows, grad_rows = pieces
        cube = pack_rows[:, :V].reshape(group, EDGE, EDGE, EDGE, width)
        faces = [
            pack_rows[:, V + face_id * FACE : V + (face_id + 1) * FACE].reshape(
                group, EDGE, EDGE, width
            )
            for face_id in range(6)
        ]
        padded = padded_of(cube, faces)
        columns = jnp.concatenate(
            [
                padded[:, tap_x : tap_x + EDGE, tap_y : tap_y + EDGE, tap_z : tap_z + EDGE]
                for tap_x, tap_y, tap_z in tap_triples()
            ],
            axis=-1,
        ).reshape(group * V, -1)
        mixed = jnp.dot(columns, weight_flat, preferred_element_type=jnp.float32)
        grad_flat = grad_rows.reshape(group * V, width)
        kernel_acc = kernel_acc + lax.dot_general(
            columns, grad_flat, (((0,), (0,)), ((), ())), preferred_element_type=jnp.float32
        )
        grad_grid = jnp.pad(
            grad_rows.reshape(group, EDGE, EDGE, EDGE, width),
            ((0, 0), (2, 2), (2, 2), (2, 2), (0, 0)),
        )
        spread = jnp.concatenate(
            [
                grad_grid[
                    :,
                    3 - tap_x : 3 - tap_x + EDGE,
                    3 - tap_y : 3 - tap_y + EDGE,
                    3 - tap_z : 3 - tap_z + EDGE,
                ]
                for tap_x, tap_y, tap_z in tap_triples()
            ],
            axis=-1,
        ).reshape(group * V, -1)
        pieces_out = [
            jnp.dot(spread, turned_flat, preferred_element_type=jnp.float32).reshape(
                group, V, width
            )
        ]
        for face_id in range(6):
            slabs = jnp.concatenate(
                [
                    face_slab(grad_grid, face_id, tap_a, tap_b, EDGE)
                    for _, tap_a, tap_b in face_taps(face_id)
                ],
                axis=-1,
            ).reshape(group * FACE, -1)
            pieces_out.append(
                jnp.dot(slabs, face_weights[face_id], preferred_element_type=jnp.float32).reshape(
                    group, FACE, width
                )
            )
        return (kernel_acc, (mixed.reshape(group, V, width), jnp.concatenate(pieces_out, axis=1)))

    start_acc = jnp.zeros((TAPS * width, width), jnp.float32)
    kernel_acc, (mixed, dpacked) = lax.scan(
        one_group,
        start_acc,
        (packs.reshape(turns, group, PACKED, width), dmixed.reshape(turns, group, V, width)),
    )
    return (
        mixed.reshape(count, V, width),
        dpacked.reshape(count, PACKED, width),
        kernel_acc.reshape(TAPS, width, width),
    )


def row_faces(table, by_step):
    return from_behind(table, "gx", by_step)


def col_faces(table, by_step):
    return from_behind(table, "gy", by_step)


def row_grads(piece, target, by_step):
    return (
        from_behind(shortened(piece), "gx", by_step).astype(piece.dtype),
        from_behind(shortened(target), "gx", by_step).astype(target.dtype),
    )


def col_grads(piece, target, by_step):
    return (
        from_behind(shortened(piece), "gy", by_step).astype(piece.dtype),
        from_behind(shortened(target), "gy", by_step).astype(target.dtype),
    )


def body(features, occupancy, routes, neighbours, weight, cotangent):
    listed = features.shape[0]
    width = features.shape[2]
    owners = lax.axis_size("gx")
    owner_slots = cotangent.shape[0]
    most_each = owner_slots // owners
    devices_all = owners * lax.axis_size("gy")
    occ_float = occupancy.astype(jnp.float32)
    occ_half = occupancy.astype(jnp.bfloat16)
    values = features.astype(jnp.float32)
    hidden = hidden_of(values, occupancy).astype(jnp.bfloat16)
    cube = hidden.reshape(listed, EDGE, EDGE, EDGE, width)
    layers = [layer_of(cube, layer_id) for layer_id in range(6)]
    remote = [
        row_faces(layers[1], 1),
        row_faces(layers[0], -1),
        col_faces(layers[3], 1),
        col_faces(layers[2], -1),
    ]
    blank = jnp.zeros((1, EDGE, EDGE, width), jnp.bfloat16)
    absent = jnp.zeros_like(layers[0])
    faces = []
    for face_id in range(6):
        far_side = remote[face_id] if face_id < 4 else absent
        table = jnp.concatenate([layers[face_id ^ 1], far_side, blank], axis=0)
        faces.append(table[neighbours[:, face_id]])
    packed = jnp.concatenate(
        [hidden] + [entry.reshape(listed, FACE, width) for entry in faces], axis=1
    )
    route = routes[:, 0]
    same = route[:, None] == route[None, :]
    earlier = jnp.arange(listed)[None, :] < jnp.arange(listed)[:, None]
    rank = jnp.sum(same & earlier, axis=1)
    slot_ids = jnp.arange(owner_slots, dtype=jnp.int32)
    chooser = ((route * most_each + rank)[None, :] == slot_ids[:, None]).astype(jnp.bfloat16)
    buffer = lax.all_to_all(
        cotangent.reshape(owners, most_each, V, width),
        "gx",
        split_axis=0,
        concat_axis=0,
        tiled=True,
    )
    picked = jnp.dot(chooser.T, buffer.reshape(owner_slots, -1), preferred_element_type=jnp.float32)
    grad_here = picked.astype(buffer.dtype).reshape((listed,) + buffer.shape[2:])
    dmixed_here = grad_here * occ_half[..., None]
    mixed, dpacked, kernel_part = block_work(packed, dmixed_here, weight)
    output_here = (values + occ_float[..., None] * mixed).astype(jnp.bfloat16)
    placed = jnp.dot(chooser, output_here.reshape(listed, -1), preferred_element_type=jnp.float32)
    owned_out = lax.all_to_all(
        placed.astype(output_here.dtype).reshape((owners, most_each) + output_here.shape[1:]),
        "gx",
        split_axis=0,
        concat_axis=0,
        tiled=True,
    ).reshape(owner_slots, V, width)
    dpacked_here = dpacked.astype(jnp.bfloat16)
    dpacked_here = lax.optimization_barrier(dpacked_here)
    dcube = dpacked_here[:, :V].astype(jnp.float32).reshape(listed, EDGE, EDGE, EDGE, width)
    slot_rows = jnp.arange(listed, dtype=jnp.int32)
    for face_id in range(6):
        piece = dpacked_here[:, V + face_id * FACE : V + (face_id + 1) * FACE]
        target = neighbours[:, face_id]
        local_map = (target[None, :] == slot_rows[:, None]).astype(jnp.bfloat16)
        landed = jnp.dot(local_map, piece.reshape(listed, -1), preferred_element_type=jnp.float32)
        if face_id < 4:
            if face_id == 0:
                moved, moved_target = row_grads(piece, target, -1)
            elif face_id == 1:
                moved, moved_target = row_grads(piece, target, 1)
            elif face_id == 2:
                moved, moved_target = col_grads(piece, target, -1)
            else:
                moved, moved_target = col_grads(piece, target, 1)
            remote_map = (moved_target[None, :] == (slot_rows + listed)[:, None]).astype(
                jnp.bfloat16
            )
            landed = landed + jnp.dot(
                remote_map, moved.reshape(listed, -1), preferred_element_type=jnp.float32
            )
        dcube = add_layer(dcube, face_id ^ 1, landed.reshape(listed, EDGE, EDGE, width))
    dhidden = dcube.reshape(listed, V, width)
    _, pullback = jax.vjp(lambda inputs: hidden_of(inputs, occupancy), values)
    input_grad = (grad_here.astype(jnp.float32) + pullback(dhidden)[0]).astype(jnp.bfloat16)
    weight_grad = lax.psum(kernel_part, ("gx", "gy")) * float(listed * devices_all * V) ** (-0.5)
    return (owned_out, input_grad, weight_grad)


def solution(mesh):
    return jax.shard_map(
        body,
        mesh=mesh,
        in_specs=(
            P(("gx", "gy"), None, None),
            P(("gx", "gy"), None),
            P(("gx", "gy"), None),
            P(("gx", "gy"), None),
            P(),
            P(("gx", "gy"), None, None),
        ),
        out_specs=(P(("gx", "gy"), None, None), P(("gx", "gy"), None, None), P()),
        check_vma=False,
    )
```

profile of v0, /device:TPU:1, one launch (start us, length us, event | category | flops | bytes accessed | tf_op | source)
XLA Modules:
  0.0 432.5 jit_solution(2433409215501855335)
XLA Ops:
  12.2 4.9 %collective-permute-start = (bf16[4,8,8,256]{3,2,1,0:T(8,128)(2,1)}, bf16[4,8,8,256]{3,2,1,0:T(8,128)(2,1)}, u32[]{:S(2)}, u32[]{:S(2)}) collective-permute-start(bf16[4,8,8,256]{3,2,1,0:T(8,128)(2,1)} %get-tuple-element.547), channel_id=1, source_target_pairs={{0,16},{16,32},{32,48},{48,64},{64,80},{80,96},{96,112},{1,17},{17... | collective-permute-start | bytes 393224 | tf_op jit(solution)/shard_map/ppermute | solution.py:20
  20.1 3.8 collective-permute-start.2
  25.2 5.8 %all-to-all-start = ((bf16[8,1,512,256]{3,2,1,0:T(8,128)(2,1)}), bf16[8,1,512,256]{3,2,1,0:T(8,128)(2,1)}, u32[]{:S(2)}, u32[]{:S(2)}) async-start(bf16[8,1,512,256]{3,2,1,0:T(8,128)(2,1)} %bitcast.740), calls=%async_computation | async-start | bytes 4194304 | tf_op jit(solution)/shard_map/all_to_all | solution.py:239
  31.9 4.8 %collective-permute-start.10 = (s32[4]{0:T(128)}, s32[4]{0:T(128)}, u32[]{:S(2)}, u32[]{:S(2)}) collective-permute-start(s32[4]{0:T(128)} %get-tuple-element.436), channel_id=1, source_target_pairs={{0,1},{1,2},{2,3},{3,4},{4,5},{5,6},{6,7},{7,8},{8,9},{9,10},{10,1... | collective-permute-start | bytes 56 | tf_op jit(solution)/shard_map/ppermute | solution.py:20
  46.8 3.8 gather_fusion.7
  58.3 3.8 gather_fusion.11
  64.4 3.7 gather_fusion.8
  70.6 3.7 gather_fusion.9
  82.7 3.8 collective-permute-start.6
  111.5 121.8 %while.30 = (s32[]{:T(128)}, f32[6912,256]{1,0:T(8,128)}, f32[2,2,512,256]{3,2,1,0:T(8,128)}, bf16[2,2,896,256]{3,2,1,0:T(8,128)(2,1)}, bf16[2,2,896,256]{3,2,1,...) while((s32[]{:T(128)}, f32[6912,256]{1,0:T(8,128)}, ...), condition=%wide.region_3.4_spmd.clone, body=%wide.region_2.3_spmd.clone.sunk | while | flops 11781144576 | bytes 375891072 | solution.py:170
  133.0 3.8 fusion.203
  156.2 5.0 %copy-done.18 = bf16[2,8,8,8,6912]{4,3,2,1,0:T(8,128)(2,1)} copy-done((bf16[2,8,8,8,6912]{4,3,2,1,0:T(8,128)(2,1)}, bf16[2,8,8,8,6912]{4,3,2,1,0:T(8,128)(2,1)S(1)}, u32[]{:S(2)}) %copy-start.18) | copy-done | bytes 14155800 | tf_op jit(solution)/shard_map/while
  161.3 12.0 %convolution_add_fusion.6 = f32[6912,256]{1,0:T(8,128)} fusion(bf16[1024,6912]{1,0:T(8,128)(2,1)} %bitcast.767, bf16[1024,256]{1,0:T(8,128)(2,1)S(1)} %bitcast.683, f32[6912,256]{1,0:T(8,128)} %get-tuple-element.796, pred[]{:T(512)S(6)} %compare.98), kind=kOutput, calls=%fused_computation.86.clone.1 | convolution fusion | flops 3627417600 | bytes 28835840 | tf_op jit(solution)/shard_map/while/body/eval_jaxpr/dot_general | solution.py:130
  173.3 4.8 %fusion.202 = f32[2,2,512,256]{3,2,1,0:T(8,128)} fusion(f32[2,2,512,256]{3,2,1,0:T(8,128)} %get-tuple-element.797, s32[]{:T(128)} %get-tuple-element.795, bf16[2,512,6912]{2,1,0:T(8,128)(2,1)S(1)} %bitcast.768, bf16[6912,256]{1,0:T(8,128)(2,1)S(1)} %copy-done.8), kind=kOutput, calls=%fused_computation.94.clone.1 | convolution fusion | flops 3623878656 | bytes 18743808 | tf_op jit(solution)/shard_map/while/body/eval_jaxpr/dot_general | solution.py:128
  186.2 3.8 fusion.203
  209.3 5.0 %copy-done.18 = bf16[2,8,8,8,6912]{4,3,2,1,0:T(8,128)(2,1)} copy-done((bf16[2,8,8,8,6912]{4,3,2,1,0:T(8,128)(2,1)}, bf16[2,8,8,8,6912]{4,3,2,1,0:T(8,128)(2,1)S(1)}, u32[]{:S(2)}) %copy-start.18) | copy-done | bytes 14155800 | tf_op jit(solution)/shard_map/while
  214.4 14.0 %convolution_add_fusion.6 = f32[6912,256]{1,0:T(8,128)} fusion(bf16[1024,6912]{1,0:T(8,128)(2,1)} %bitcast.767, bf16[1024,256]{1,0:T(8,128)(2,1)S(1)} %bitcast.683, f32[6912,256]{1,0:T(8,128)} %get-tuple-element.796, pred[]{:T(512)S(6)} %compare.98), kind=kOutput, calls=%fused_computation.86.clone.1 | convolution fusion | flops 3627417600 | bytes 28835840 | tf_op jit(solution)/shard_map/while/body/eval_jaxpr/dot_general | solution.py:130
  228.4 4.8 %fusion.202 = f32[2,2,512,256]{3,2,1,0:T(8,128)} fusion(f32[2,2,512,256]{3,2,1,0:T(8,128)} %get-tuple-element.797, s32[]{:T(128)} %get-tuple-element.795, bf16[2,512,6912]{2,1,0:T(8,128)(2,1)S(1)} %bitcast.768, bf16[6912,256]{1,0:T(8,128)(2,1)S(1)} %copy-done.8), kind=kOutput, calls=%fused_computation.94.clone.1 | convolution fusion | flops 3623878656 | bytes 18743808 | tf_op jit(solution)/shard_map/while/body/eval_jaxpr/dot_general | solution.py:128
  239.2 4.9 %collective-permute-start.11 = (bf16[4,64,256]{2,1,0:T(8,128)(2,1)}, bf16[4,64,256]{2,1,0:T(8,128)(2,1)}, u32[]{:S(2)}, u32[]{:S(2)}) collective-permute-start(bf16[4,64,256]{2,1,0:T(8,128)(2,1)} %get-tuple-element.536), channel_id=1, source_target_pairs={{0,1},{1,2},{2,3},{3,4},{4,5},{5,6},{6,7},{7,8},{8,9},{9,10},{10,1... | collective-permute-start | bytes 393224 | tf_op jit(solution)/shard_map/ppermute | solution.py:20
  250.3 3.9 collective-permute-start.7
  268.9 4.4 %fusion.86 = (bf16[4,512,256]{2,1,0:T(8,128)(2,1)}, bf16[4,512,256]{2,1,0:T(8,128)(2,1)S(1)}) fusion(bf16[4,512,256]{2,1,0:T(8,128)(2,1)S(1)} %copy-done.10, f32[1,4,512,256]{3,1,2,0:T(4,128)S(1)} %copy-done.14, f32[4,512]{1,0:T(4,128)S(1)} %multiply_multiply_fusion, f32[4,512]{1,0:T(4,128)S(1)} %copy-done.21, f32[4,8,8,8,256]{4,3,2,1,0:T(8,128)S(1)} %copy.204, ...), kind=kLoop, calls=%fused_computation.290 | loop fusion | flops 11010048 | bytes 9461760 | tf_op jit(solution)/shard_map/convert_element_type | solution.py:286
  275.3 33.8 %all_to_all.10 = bf16[8,1,512,256]{3,2,1,0:T(8,128)(2,1)S(1)} all-to-all(bf16[8,1,512,256]{3,2,1,0:T(8,128)(2,1)S(1)} %copy.197), channel_id=1, replica_groups=mesh['gx'=8,'gy'=16] {'gx'}, dimensions={0} | all-to-all | bytes 4194304 | tf_op jit(solution)/shard_map/all_to_all | solution.py:252
  309.0 108.2 %all-reduce.4.cloned.1.call-done = f32[27,256,256]{2,1,0:T(8,128)} async-done(((f32[27,256,256]{2,1,0:T(8,128)}), f32[27,256,256]{2,1,0:T(8,128)}) %all-reduce.4.cloned.1.call-update) | async-done | bytes 7077904 | tf_op jit(solution)/shard_map/psum | solution.py:287
  417.3 6.7 %broadcast_multiply_fusion = f32[27,256,256]{2,1,0:T(8,128)} fusion(f32[27,256,256]{2,1,0:T(8,128)} %all-reduce.4.cloned.1.call-done), kind=kLoop, calls=%fused_computation.276 | loop fusion | flops 1769472 | bytes 14155776 | tf_op jit(solution)/shard_map/mul | solution.py:287
  (476 shorter events, 148.3 us)
Async XLA Ops:
  8.7 15.1 %copy-start.24 = (f32[4,512]{1,0:T(4,128)}, f32[4,512]{1,0:T(4,128)S(1)}, u32[]{:S(2)}) copy-start(f32[4,512]{1,0:T(4,128)S(1)} %fusion.87) | copy-start | bytes 24580
  12.2 69.2 %collective-permute-start = (bf16[4,8,8,256]{3,2,1,0:T(8,128)(2,1)}, bf16[4,8,8,256]{3,2,1,0:T(8,128)(2,1)}, u32[]{:S(2)}, u32[]{:S(2)}) collective-permute-start(bf16[4,8,8,256]{3,2,1,0:T(8,128)(2,1)} %get-tuple-element.547), channel_id=1, source_target_pairs={{0,16},{16,32},{32,48},{48,64},{64,80},{80,96},{96,112},{1,17},{17... | collective-permute-start | bytes 393224 | tf_op jit(solution)/shard_map/ppermute | solution.py:20
  17.2 13.8 %copy-start.26 = (s32[4,6]{1,0:T(4,128)S(1)}, s32[4,6]{1,0:T(4,128)}, u32[]{:S(2)}) copy-start(s32[4,6]{1,0:T(4,128)} %param.47) | copy-start | bytes 292
  17.2 22.0 %copy-start.7 = (bf16[27,256,256]{2,1,0:T(8,128)(2,1)S(1)}, bf16[27,256,256]{2,1,0:T(8,128)(2,1)}, u32[]{:S(2)}) copy-start(bf16[27,256,256]{2,1,0:T(8,128)(2,1)} %param.48) | copy-start | bytes 10616836
  17.2 65.6 %collective-permute-start.1 = (bf16[4,8,8,256]{3,2,1,0:T(8,128)(2,1)}, bf16[4,8,8,256]{3,2,1,0:T(8,128)(2,1)}, u32[]{:S(2)}, u32[]{:S(2)}) collective-permute-start(bf16[4,8,8,256]{3,2,1,0:T(8,128)(2,1)} %get-tuple-element.546), channel_id=1, source_target_pairs={{16,0},{32,16},{48,32},{64,48},{80,64},{96,80},{112,96},{17,1},{33... | collective-permute-start | bytes 393224 | tf_op jit(solution)/shard_map/ppermute | solution.py:20
  20.1 66.5 %collective-permute-start.2 = (bf16[4,8,8,256]{3,2,1,0:T(8,128)(2,1)}, bf16[4,8,8,256]{3,2,1,0:T(8,128)(2,1)}, u32[]{:S(2)}, u32[]{:S(2)}) collective-permute-start(bf16[4,8,8,256]{3,2,1,0:T(8,128)(2,1)} %get-tuple-element.545), channel_id=1, source_target_pairs={{0,1},{1,2},{2,3},{3,4},{4,5},{5,6},{6,7},{7,8},{8,9},{9,10},{10,1... | collective-permute-start | bytes 393224 | tf_op jit(solution)/shard_map/ppermute | solution.py:20
  23.9 64.6 %collective-permute-start.3 = (bf16[4,8,8,256]{3,2,1,0:T(8,128)(2,1)}, bf16[4,8,8,256]{3,2,1,0:T(8,128)(2,1)}, u32[]{:S(2)}, u32[]{:S(2)}) collective-permute-start(bf16[4,8,8,256]{3,2,1,0:T(8,128)(2,1)} %get-tuple-element.544), channel_id=1, source_target_pairs={{1,0},{2,1},{3,2},{4,3},{5,4},{6,5},{7,6},{8,7},{9,8},{10,9},{11,1... | collective-permute-start | bytes 393224 | tf_op jit(solution)/shard_map/ppermute | solution.py:20
  25.2 80.1 %all-to-all-start = ((bf16[8,1,512,256]{3,2,1,0:T(8,128)(2,1)}), bf16[8,1,512,256]{3,2,1,0:T(8,128)(2,1)}, u32[]{:S(2)}, u32[]{:S(2)}) async-start(bf16[8,1,512,256]{3,2,1,0:T(8,128)(2,1)} %bitcast.740), calls=%async_computation | async-start | bytes 4194304 | tf_op jit(solution)/shard_map/all_to_all | solution.py:239
  31.0 386.3 %all-reduce.4.cloned.1.call-start = ((), (), s32[]{:S(2)}) async-start(), calls=%async_computation.2 | async-start | bytes 14155776 | tf_op jit(solution)/shard_map/psum | solution.py:287
  31.9 218.4 %collective-permute-start.10 = (s32[4]{0:T(128)}, s32[4]{0:T(128)}, u32[]{:S(2)}, u32[]{:S(2)}) collective-permute-start(s32[4]{0:T(128)} %get-tuple-element.436), channel_id=1, source_target_pairs={{0,1},{1,2},{2,3},{3,4},{4,5},{5,6},{6,7},{7,8},{8,9},{9,10},{10,1... | collective-permute-start | bytes 56 | tf_op jit(solution)/shard_map/ppermute | solution.py:20
  77.1 30.9 %copy-start.35 = (s32[4]{0:T(128)}, s32[4]{0:T(128)S(1)}, u32[]{:S(2)}) copy-start(s32[4]{0:T(128)S(1)} %bitcast_add_fusion) | copy-start | bytes 52
  81.4 175.9 %collective-permute-start.8 = (s32[4]{0:T(128)}, s32[4]{0:T(128)}, u32[]{:S(2)}, u32[]{:S(2)}) collective-permute-start(s32[4]{0:T(128)} %get-tuple-element.437), channel_id=1, source_target_pairs={{1,0},{2,1},{3,2},{4,3},{5,4},{6,5},{7,6},{8,7},{9,8},{10,9},{11,1... | collective-permute-start | bytes 56 | tf_op jit(solution)/shard_map/ppermute | solution.py:20
  82.7 175.7 %collective-permute-start.6 = (s32[4]{0:T(128)}, s32[4]{0:T(128)}, u32[]{:S(2)}, u32[]{:S(2)}) collective-permute-start(s32[4]{0:T(128)} %get-tuple-element.438), channel_id=1, source_target_pairs={{0,16},{16,32},{32,48},{48,64},{64,80},{80,96},{96,112},{1,17},{17... | collective-permute-start | bytes 56 | tf_op jit(solution)/shard_map/ppermute | solution.py:20
  86.6 176.0 %collective-permute-start.4 = (s32[4]{0:T(128)}, s32[4]{0:T(128)}, u32[]{:S(2)}, u32[]{:S(2)}) collective-permute-start(s32[4]{0:T(128)} %get-tuple-element.439), channel_id=1, source_target_pairs={{16,0},{32,16},{48,32},{64,48},{80,64},{96,80},{112,96},{17,1},{33... | collective-permute-start | bytes 56 | tf_op jit(solution)/shard_map/ppermute | solution.py:20
  124.9 13.0 %copy-start = (bf16[2304,256]{1,0:T(8,128)(2,1)}, bf16[2304,256]{1,0:T(8,128)(2,1)S(1)}, u32[]{:S(2)}) copy-start(bf16[2304,256]{1,0:T(8,128)(2,1)S(1)} %get-tuple-element.822) | copy-start | bytes 3538948 | tf_op jit(solution)/shard_map/while
  161.3 12.0 %copy-start.8 = (bf16[6912,256]{1,0:T(8,128)(2,1)S(1)}, bf16[6912,256]{1,0:T(8,128)(2,1)}, u32[]{:S(2)}) copy-start(bf16[6912,256]{1,0:T(8,128)(2,1)} %get-tuple-element.819) | copy-start | bytes 10616836 | tf_op jit(solution)/shard_map/while
  161.3 12.0 %copy-start.19 = (bf16[2,8,8,8,6912]{4,3,2,1,0:T(8,128)(2,1)S(1)}, bf16[2,8,8,8,6912]{4,3,2,1,0:T(8,128)(2,1)}, u32[]{:S(2)}) copy-start(bf16[2,8,8,8,6912]{4,3,2,1,0:T(8,128)(2,1)} %copy-done.18) | copy-start | bytes 42467332 | tf_op jit(solution)/shard_map/while
  178.1 13.0 %copy-start = (bf16[2304,256]{1,0:T(8,128)(2,1)}, bf16[2304,256]{1,0:T(8,128)(2,1)S(1)}, u32[]{:S(2)}) copy-start(bf16[2304,256]{1,0:T(8,128)(2,1)S(1)} %get-tuple-element.822) | copy-start | bytes 3538948 | tf_op jit(solution)/shard_map/while
  214.4 14.0 %copy-start.8 = (bf16[6912,256]{1,0:T(8,128)(2,1)S(1)}, bf16[6912,256]{1,0:T(8,128)(2,1)}, u32[]{:S(2)}) copy-start(bf16[6912,256]{1,0:T(8,128)(2,1)} %get-tuple-element.819) | copy-start | bytes 10616836 | tf_op jit(solution)/shard_map/while
  214.4 14.0 %copy-start.19 = (bf16[2,8,8,8,6912]{4,3,2,1,0:T(8,128)(2,1)S(1)}, bf16[2,8,8,8,6912]{4,3,2,1,0:T(8,128)(2,1)}, u32[]{:S(2)}) copy-start(bf16[2,8,8,8,6912]{4,3,2,1,0:T(8,128)(2,1)} %copy-done.18) | copy-start | bytes 42467332 | tf_op jit(solution)/shard_map/while
  239.2 8.8 %collective-permute-start.11 = (bf16[4,64,256]{2,1,0:T(8,128)(2,1)}, bf16[4,64,256]{2,1,0:T(8,128)(2,1)}, u32[]{:S(2)}, u32[]{:S(2)}) collective-permute-start(bf16[4,64,256]{2,1,0:T(8,128)(2,1)} %get-tuple-element.536), channel_id=1, source_target_pairs={{0,1},{1,2},{2,3},{3,4},{4,5},{5,6},{6,7},{7,8},{8,9},{9,10},{10,1... | collective-permute-start | bytes 393224 | tf_op jit(solution)/shard_map/ppermute | solution.py:20
  248.0 7.3 %collective-permute-start.9 = (bf16[4,64,256]{2,1,0:T(8,128)(2,1)}, bf16[4,64,256]{2,1,0:T(8,128)(2,1)S(1)}, u32[]{:S(2)}, u32[]{:S(2)}) collective-permute-start(bf16[4,64,256]{2,1,0:T(8,128)(2,1)} %get-tuple-element.537), channel_id=1, source_target_pairs={{1,0},{2,1},{3,2},{4,3},{5,4},{6,5},{7,6},{8,7},{9,8},{10,9},{11,1... | collective-permute-start | bytes 393224 | tf_op jit(solution)/shard_map/ppermute | solution.py:20
  250.3 8.0 %collective-permute-start.7 = (bf16[4,64,256]{2,1,0:T(8,128)(2,1)S(1)}, bf16[4,64,256]{2,1,0:T(8,128)(2,1)S(1)}, u32[]{:S(2)}, u32[]{:S(2)}) collective-permute-start(bf16[4,64,256]{2,1,0:T(8,128)(2,1)S(1)} %get-tuple-element.538), channel_id=1, source_target_pairs={{0,16},{16,32},{32,48},{48,64},{64,80},{80,96},{96,112},{1,17},{17... | collective-permute-start | bytes 393224 | tf_op jit(solution)/shard_map/ppermute | solution.py:20
  255.3 7.2 %collective-permute-start.5 = (bf16[4,64,256]{2,1,0:T(8,128)(2,1)S(1)}, bf16[4,64,256]{2,1,0:T(8,128)(2,1)S(1)}, u32[]{:S(2)}, u32[]{:S(2)}) collective-permute-start(bf16[4,64,256]{2,1,0:T(8,128)(2,1)S(1)} %get-tuple-element.539), channel_id=1, source_target_pairs={{16,0},{32,16},{48,32},{64,48},{80,64},{96,80},{112,96},{17,1},{33... | collective-permute-start | bytes 393224 | tf_op jit(solution)/shard_map/ppermute | solution.py:20
  (48 other events, 195.4 us)
Sparse Core Ops, SparseCore 0:
  247.3 169.9 all-reduce.3
where the time goes:
time: 441 us; the launch traced here: 432 us
  local copies, waits for them, and re-layouts  131 us (30%)
  waiting for transfers between devices  111 us (25%)
  matrix products  56.6 us (13%)
  starting transfers between devices  41.9 us (10%)
  blocking collectives  33.8 us (8%)
  other arithmetic  26.9 us (6%)
  loops' own time  15.5 us (4%)
  between operations  15.2 us (3%)
    psum x1, waiting for transfers between devices, body(): lax.psum(kernel_part, ('gx', 'gy'))  108 us
    ppermute x12, starting transfers between devices, from_behind(): return lax.ppermute(block, axis, route)  36.1 us
    all_to_all x1, blocking collectives, body(): lax.all_to_all(placed.astype(output_here.dtype).reshape((owners, most_eac...  33.8 us
    gather x12, local copies, waits for them, and re-layouts, block_work(): turned[np.array([entry[0] for entry in face_taps(face_id)])]  33.2 us
    while x244, local copies, waits for them, and re-layouts  30.1 us
    dot_general x2, matrix products, one_group(): lax.dot_general(columns, grad_flat, (((0,), (0,)), ((), ())), preferred_e...  26.1 us
    unnamed x86, local copies, waits for them, and re-layouts  17.9 us
    another operation x1, loops' own time, block_work(): lax.scan(one_group, start_acc, (packs.reshape(turns, group, PACKED, width...  15.5 us
  transfers between devices with their start and end apart: 14, of which 2 were waited for; matrix products, arithmetic and copies ran while one was open for 42% of the time, Pallas kernels for 0%

commit v1 on v0

v1 whole, which is shorter than its diff:
```python
import jax
import jax.numpy as jnp
from jax import lax
from jax.experimental import pallas as pl
from jax.experimental.pallas import tpu as pltpu
from jax.sharding import PartitionSpec as P

EDGE = 8
TAPS = 27
V = 512
FACE = 64
PLANE = 80
MIB = 1 << 20

norm_eps = 1e-06


def from_behind(block, axis, distance):
    count = lax.axis_size(axis)
    return lax.ppermute(block, axis, [(i, (i + distance) % count) for i in range(count)])


def inner_neighbours(neighbours, listed):
    p, q = lax.axis_index("gx"), lax.axis_index("gy")
    inside = jnp.stack(
        [p > 0, p < lax.axis_size("gx") - 1, q > 0, q < lax.axis_size("gy") - 1, True, True]
    )
    return jnp.where(inside[None, :] | (neighbours < listed), neighbours, 2 * listed)


def hop(blocks, sign):
    count = lax.axis_size("gx")
    ways = [
        (p, (p // 2 + (sign if p % 2 == 0 else -sign)) * 2 % count + p % 2)
        for p in range(count)
    ]
    return lax.ppermute(blocks, "gx", ways)


def to_other_core(block):
    return lax.ppermute(block, "gx", [(p, p ^ 1) for p in range(lax.axis_size("gx"))])


def params(limit):
    return pltpu.CompilerParams(vmem_limit_bytes=limit * MIB)


def whole(shape):
    zeros = (0,) * len(shape)
    return pl.BlockSpec(shape, lambda *_: zeros)


def by_brick(shape):
    zeros = (0,) * len(shape)
    return pl.BlockSpec((1,) + shape, lambda s, *_: (s,) + zeros)


def smem():
    return pl.BlockSpec(memory_space=pltpu.SMEM)


def anywhere():
    return pl.BlockSpec(memory_space=pl.ANY)


def mask_of(occ_row, width):
    spread = jnp.broadcast_to(occ_row.astype(jnp.float32), (128, V))
    column = jnp.transpose(spread)
    return jnp.concatenate([column] * (width // 128), axis=1)


def norm_scale(values):
    return lax.rsqrt(jnp.mean(values * values, axis=-1, keepdims=True) + norm_eps)


def sigmoid(u):
    return 1.0 / (1.0 + jnp.exp(-u))


def hidden_kernel(feat_ref, occ_ref, hid_ref, x0_ref, x1_ref, y0_ref, y1_ref):
    width = feat_ref.shape[2]
    values = feat_ref[0].astype(jnp.float32)
    u = values * norm_scale(values)
    hidden = mask_of(occ_ref[0], width) * (u * sigmoid(u))
    hid_ref[0] = hidden.astype(jnp.bfloat16)
    cube = hidden.reshape(EDGE, EDGE, EDGE, width)
    x0_ref[0] = cube[0].reshape(FACE, width).astype(jnp.bfloat16)
    x1_ref[0] = cube[EDGE - 1].reshape(FACE, width).astype(jnp.bfloat16)
    y0_ref[0] = cube[:, 0].reshape(FACE, width).astype(jnp.bfloat16)
    y1_ref[0] = cube[:, EDGE - 1].reshape(FACE, width).astype(jnp.bfloat16)


def hidden_call(features, occ_rows):
    listed, _, width = features.shape
    layer = jax.ShapeDtypeStruct((listed, FACE, width), jnp.bfloat16)
    return pl.pallas_call(
        hidden_kernel,
        grid=(listed,),
        in_specs=[by_brick((V, width)), by_brick((1, V))],
        out_specs=[by_brick((V, width))] + [by_brick((FACE, width))] * 4,
        out_shape=[jax.ShapeDtypeStruct((listed, V, width), jnp.bfloat16)] + [layer] * 4,
        compiler_params=params(16),
        name="hidden",
    )(features, occ_rows)


def hold_kernel(*refs):
    pass


def hold_call(blocks, after):
    return pl.pallas_call(
        hold_kernel,
        in_specs=[anywhere()] * (len(blocks) + len(after)),
        out_specs=[anywhere()] * len(blocks),
        out_shape=[jax.ShapeDtypeStruct(block.shape, block.dtype) for block in blocks],
        input_output_aliases={i: i for i in range(len(blocks))},
        compiler_params=params(16),
        name="hold",
    )(*blocks, *after)


def collect_kernel(place_ref, own_ref, near_ref, far_ref, back_ref, mate_ref, out_ref):
    for step, came_ref in enumerate((own_ref, near_ref, far_ref, back_ref)):
        out_ref[place_ref[2 * step]] = came_ref[0]
        out_ref[place_ref[2 * step + 1]] = mate_ref[step]


def collect_call(place, own, near, far, back, mate):
    shape = (2 * mate.shape[0],) + mate.shape[1:]
    return pl.pallas_call(
        collect_kernel,
        grid=(1,),
        in_specs=[smem()] + [whole(own.shape)] * 4 + [whole(mate.shape)],
        out_specs=whole(shape),
        out_shape=jax.ShapeDtypeStruct(shape, mate.dtype),
        compiler_params=params(20),
        name="collect",
    )(place, own, near, far, back, mate)


def roll_c(block, shift):
    flat = block.reshape((-1,) + block.shape[-2:])
    return pltpu.roll(flat, shift % EDGE, 1).reshape(block.shape)


def c_index(shape):
    return lax.broadcasted_iota(jnp.int32, shape, len(shape) - 2)


def extended_brick(s, near_ref, hid_ref, own, far, store):
    listed, _, width = hid_ref.shape

    def flag(condition):
        return jnp.where(condition, 1.0, 0.0).astype(jnp.float32)

    def face(f):
        n = near_ref[s, f]
        here = own[f ^ 1][jnp.minimum(n, listed - 1)].astype(jnp.float32)
        there = far[f][jnp.clip(n - listed, 0, listed - 1)].astype(jnp.float32)
        value = here * flag(n < listed) + there * flag((n >= listed) & (n < 2 * listed))
        return value.reshape(EDGE, EDGE, width)

    def column(f):
        n = near_ref[s, f]
        brick = hid_ref[jnp.minimum(n, listed - 1)].astype(jnp.float32) * flag(n < listed)
        return brick.reshape(EDGE, EDGE, EDGE, width)

    def extended(core, sides):
        x0, x1, y0, y1 = sides
        blank = jnp.zeros((1, EDGE, width), jnp.float32)
        middle = jnp.concatenate([y0[:, None], core, y1[:, None]], axis=1)
        first = jnp.concatenate([blank, x0, blank], axis=0)[None]
        last = jnp.concatenate([blank, x1, blank], axis=0)[None]
        return jnp.concatenate([first, middle, last], axis=0)

    def put(k, block):
        everything = block.reshape(EDGE + 2, PLANE, width).astype(jnp.bfloat16)
        inner = block[:, 1 : EDGE + 1].reshape(EDGE + 2, FACE, width).astype(jnp.bfloat16)
        store(k, everything, inner)

    core = hid_ref[s].astype(jnp.float32).reshape(EDGE, EDGE, EDGE, width)
    sides = [face(f) for f in range(4)]
    at = c_index(core.shape)
    at_side = c_index(sides[0].shape)
    for k, edge, f in ((0, EDGE - 1, 4), (2, 0, 5)):
        shown = extended(
            jnp.where(at == edge, column(f), core),
            [jnp.where(at_side == edge, 0.0, side) for side in sides],
        )
        put(k, roll_c(shown, 1 - k))
    put(1, extended(core, sides))


def window(even_ref, odd_ref, s, i, j, k):
    if j == 1:
        part = odd_ref[s, k, pl.ds(i, EDGE)]
    else:
        part = even_ref[s, k, pl.ds(i, EDGE), j * EDGE : j * EDGE + FACE]
    return part.reshape(V, part.shape[-1])


def forward_kernel(
    near_ref, place_ref, hid_ref, l0, l1, l2, l3, r0, r1, r2, r3, feat_ref, occ_ref, w_ref,
    *refs,
):
    outs, even_ref, odd_ref = refs[:-2], refs[-2], refs[-1]
    s = pl.program_id(0)
    width = feat_ref.shape[2]

    @pl.when(s == 0)
    def _():
        for out_ref in outs:
            out_ref[...] = jnp.zeros_like(out_ref)

    def store(k, everything, inner):
        even_ref[0, k] = everything
        odd_ref[0, k] = inner

    extended_brick(s, near_ref, hid_ref, (l0, l1, l2, l3), (r0, r1, r2, r3), store)
    total = jnp.zeros((V, width), jnp.float32)
    for i in range(3):
        for j in range(3):
            rows = jnp.concatenate(
                [window(even_ref, odd_ref, 0, i, j, k) for k in range(3)], axis=1
            )
            total = total + jnp.dot(rows, w_ref[3 * i + j], preferred_element_type=jnp.float32)
    result = feat_ref[0].astype(jnp.float32) + mask_of(occ_ref[0], width) * total
    result = result.astype(jnp.bfloat16)
    for step, out_ref in enumerate(outs):

        @pl.when(place_ref[s] // 2 == step)
        def _():
            out_ref[place_ref[s] % 2] = result


def extended_scratch(bricks, width):
    return [
        pltpu.VMEM((bricks, 3, EDGE + 2, PLANE, width), jnp.bfloat16),
        pltpu.VMEM((bricks, 3, EDGE + 2, FACE, width), jnp.bfloat16),
    ]


def forward_call(neighbours, place, hidden, layers, remote, features, occ_rows, weight9, slots):
    listed, _, width = features.shape
    layer = whole((listed, FACE, width))
    return pl.pallas_call(
        forward_kernel,
        grid=(listed,),
        in_specs=[smem(), smem(), whole((listed, V, width))]
        + [layer] * 8
        + [by_brick((V, width)), by_brick((1, V)), whole(weight9.shape)],
        out_specs=[whole((2, V, width))] * (slots // 2),
        out_shape=[jax.ShapeDtypeStruct((2, V, width), jnp.bfloat16)] * (slots // 2),
        scratch_shapes=extended_scratch(1, width),
        compiler_params=params(56),
        cost_estimate=pl.CostEstimate(
            flops=2 * listed * V * TAPS * width * width,
            bytes_accessed=10 * MIB,
            transcendentals=0,
        ),
        name="forward",
    )(neighbours, place, hidden, *layers, *remote, features, occ_rows, weight9)


def weight_kernel(
    near_ref, place_ref, core_ref, hid_ref, l0, l1, l2, l3, r0, r1, r2, r3, occ_ref, after_ref,
    *refs, scale,
):
    came, refs = refs[:-7], refs[-7:]
    mine_ref, theirs_ref, grad_ref, even_ref, odd_ref, turned_ref, sem = refs
    part = V // len(came)
    i = pl.program_id(0)
    listed, _, width = hid_ref.shape
    half = width // 2

    def copy(t, s):
        return pltpu.make_async_copy(
            came[t].at[place_ref[s, 0]],
            grad_ref.at[s, pl.ds(t * part, part)],
            sem.at[t * listed + s],
        )

    @pl.when(i == 0)
    def _():
        for s in range(listed):
            for t in range(len(came)):
                copy(t, s).start()

        @pl.loop(0, listed)
        def _(s):
            def store(k, everything, inner):
                even_ref[s, k] = everything
                odd_ref[s, k] = inner

            extended_brick(s, near_ref, hid_ref, (l0, l1, l2, l3), (r0, r1, r2, r3), store)

        for s in range(listed):
            for t in range(len(came)):
                copy(t, s).wait()
            mixed = grad_ref[s].astype(jnp.float32) * mask_of(occ_ref[s], width)
            turned_ref[:, s * V : (s + 1) * V] = jnp.transpose(mixed).astype(jnp.bfloat16)

    @pl.when(i < 3)
    def _():
        first = core_ref[0] == 0
        for j in range(3):
            for k in range(3):
                rows = jnp.concatenate(
                    [window(even_ref, odd_ref, s, i, j, k) for s in range(listed)], axis=0
                )
                product = jnp.dot(turned_ref[...], rows, preferred_element_type=jnp.float32)
                product = jnp.transpose(product) * scale
                low, high = product[:, :half], product[:, half:]
                mine_ref[3 * j + k] = jnp.where(first, low, high)
                theirs_ref[3 * j + k] = jnp.where(first, high, low).astype(theirs_ref.dtype)

    @pl.when(i == 3)
    def _():
        mine_ref[...] = jnp.zeros_like(mine_ref)
        theirs_ref[...] = jnp.zeros_like(theirs_ref)


def weight_call(
    neighbours, place, core, hidden, layers, remote, came, occ_rows, scale, kind, after
):
    listed, _, width = hidden.shape
    shape = (TAPS + 1, width, width // 2)
    block = pl.BlockSpec((9, width, width // 2), lambda i: (i, 0, 0))
    return pl.pallas_call(
        lambda *refs: weight_kernel(*refs, scale=scale),
        grid=(4,),
        in_specs=[smem(), smem(), smem(), whole(hidden.shape)]
        + [whole((listed, FACE, width))] * 8
        + [whole(occ_rows.shape), anywhere()]
        + [anywhere()] * len(came),
        out_specs=[block, block, whole(hidden.shape)],
        out_shape=[
            jax.ShapeDtypeStruct(shape, jnp.float32),
            jax.ShapeDtypeStruct(shape, kind),
            jax.ShapeDtypeStruct(hidden.shape, jnp.bfloat16),
        ],
        scratch_shapes=extended_scratch(listed, width)
        + [pltpu.VMEM((width, listed * V), jnp.bfloat16), pltpu.SemaphoreType.DMA((len(came) * listed,))],
        compiler_params=params(32),
        cost_estimate=pl.CostEstimate(
            flops=2 * listed * V * TAPS * width * width,
            bytes_accessed=10 * MIB,
            transcendentals=0,
        ),
        name="weight_gradient",
    )(neighbours, place, core, hidden, *layers, *remote, occ_rows, after, *came)


def chip_kernel(mine_ref, theirs_ref, *refs):
    out_ref = refs[-1]
    added = mine_ref[...] + theirs_ref[...].astype(jnp.float32)
    out_ref[...] = added.astype(jnp.bfloat16)


def chip_call(mine, theirs, after):
    taps, width, half = mine.shape
    block = pl.BlockSpec((7, width, half), lambda t: (t, 0, 0))
    return pl.pallas_call(
        chip_kernel,
        grid=(taps // 7,),
        in_specs=[block, block] + [anywhere()] * len(after),
        out_specs=block,
        out_shape=jax.ShapeDtypeStruct(mine.shape, jnp.bfloat16),
        compiler_params=params(12),
        name="chip_sum",
    )(mine, theirs, *after)


def total_kernel(parts_ref, *refs):
    out_ref = refs[-1]
    total = jnp.sum(parts_ref[...].astype(jnp.float32), axis=0)
    for z in range(out_ref.shape[0]):
        out_ref[z] = total.astype(jnp.bfloat16)


def total_call(parts, copies, after):
    _, rows, half = parts.shape
    return pl.pallas_call(
        total_kernel,
        grid=(1,),
        in_specs=[whole(parts.shape)] + [anywhere()] * len(after),
        out_specs=whole((copies, rows, half)),
        out_shape=jax.ShapeDtypeStruct((copies, rows, half), jnp.bfloat16),
        compiler_params=params(20),
        name="total",
    )(parts, *after)


def join_kernel(core_ref, own_ref, other_ref, after_ref, out_ref):
    half = own_ref.shape[2]
    first = core_ref[0] == 0

    def put(low_ref, high_ref):
        out_ref[:, :, :half] = low_ref[...].astype(jnp.float32)
        out_ref[:, :, half:] = high_ref[...].astype(jnp.float32)

    @pl.when(first)
    def _():
        put(own_ref, other_ref)

    @pl.when(jnp.logical_not(first))
    def _():
        put(other_ref, own_ref)


def join_call(core, own, other, after):
    _, width, half = own.shape
    block = pl.BlockSpec((9, width, half), lambda t: (t, 0, 0))
    return pl.pallas_call(
        join_kernel,
        grid=(TAPS // 9,),
        in_specs=[smem(), block, block, anywhere()],
        out_specs=pl.BlockSpec((9, width, 2 * half), lambda t: (t, 0, 0)),
        out_shape=jax.ShapeDtypeStruct((TAPS, width, 2 * half), jnp.float32),
        compiler_params=params(16),
        name="join",
    )(core, own, other, after)


def data_kernel(
    near_ref, buf_ref, occ_ref, w_ref, after_ref,
    grad_ref, s0_ref, s1_ref, s2_ref, s3_ref,
    wide_ref, rows_ref, depth_ref, kept_ref,
):
    s = pl.program_id(0)
    listed = grad_ref.shape[0]
    width = buf_ref.shape[2]
    last = s == listed - 1

    mixed = buf_ref[0].astype(jnp.float32) * mask_of(occ_ref[0], width)
    cube = mixed.reshape(FACE, EDGE, width)
    at = c_index(cube.shape)

    def three(block, index):
        ahead = jnp.where(index == EDGE - 1, 0.0, roll_c(block, -1))
        behind = jnp.where(index == 0, 0.0, roll_c(block, 1))
        flat = (-1, width)
        return [entry.reshape(flat).astype(jnp.bfloat16) for entry in (ahead, block, behind)]

    def back(rows, taps):
        return sum(
            lax.dot_general(
                row, w_ref[tap], (((1,), (1,)), ((), ())), preferred_element_type=jnp.float32
            )
            for row, tap in zip(rows, taps)
        )

    rows = three(cube, at)
    wide_ref[...] = jnp.zeros_like(wide_ref)
    for i in range(3):
        for j in range(3):
            product = back(rows, [9 * i + 3 * j + k for k in range(3)])
            wide_ref[i : i + EDGE, j * EDGE : j * EDGE + FACE] += product.reshape(
                EDGE, FACE, width
            )

    def rounded(block):
        return block.astype(jnp.bfloat16).astype(jnp.float32)

    inside = slice(EDGE, EDGE + FACE)
    grad_ref[s] = rounded(wide_ref[1 : EDGE + 1, inside].reshape(V, width))
    kept_ref[s, 0] = rounded(wide_ref[0, inside])
    kept_ref[s, 1] = rounded(wide_ref[EDGE + 1, inside])
    kept_ref[s, 2] = rounded(wide_ref[1 : EDGE + 1, 0:EDGE].reshape(FACE, width))
    kept_ref[s, 3] = rounded(wide_ref[1 : EDGE + 1, PLANE - EDGE : PLANE].reshape(FACE, width))

    halves = range(width // 128)
    for half in halves:
        rows_ref[half] = mixed[:, half * 128 : (half + 1) * 128]
    for side, c in ((0, 0), (1, EDGE - 1)):
        layer = jnp.concatenate(
            [rows_ref[half, pl.ds(c, FACE, stride=EDGE)] for half in halves], axis=1
        )
        layer = layer.reshape(EDGE, EDGE, width)
        for j, entry in enumerate(three(layer, c_index(layer.shape))):
            depth_ref[side, j, pl.ds(s * FACE, FACE)] = entry

    @pl.when(last)
    def _():
        sends = (s0_ref, s1_ref, s2_ref, s3_ref)
        for side in range(2):
            total = jnp.zeros((listed, EDGE + 2, EDGE, width), jnp.float32)
            for i in range(3):
                product = back(
                    [depth_ref[side, j] for j in range(3)],
                    [9 * i + 3 * j + 2 * side for j in range(3)],
                ).reshape(listed, EDGE, EDGE, width)
                pieces = [product]
                if i > 0:
                    pieces.insert(0, jnp.zeros((listed, i, EDGE, width), jnp.float32))
                if i < 2:
                    pieces.append(jnp.zeros((listed, 2 - i, EDGE, width), jnp.float32))
                total = total + jnp.concatenate(pieces, axis=1)
            rows_ref[...] = jnp.zeros_like(rows_ref)
            for h in range(listed):
                n = near_ref[h, 4 + side]

                @pl.when(n < listed)
                def _():
                    piece = rounded(total[h, 1 : EDGE + 1].reshape(FACE, width))
                    c = (EDGE - 1) * (1 - side)
                    for half in halves:
                        rows_ref[half, pl.ds(c, FACE, stride=EDGE)] = piece[
                            :, half * 128 : (half + 1) * 128
                        ]
                    grad_ref[n] += jnp.concatenate([rows_ref[half] for half in halves], axis=1)

        for f in range(4):
            sums = [jnp.zeros((FACE, width), jnp.float32) for _ in range(listed)]
            for h in range(listed):
                n = near_ref[h, f]
                piece = kept_ref[h, f]
                sums = [
                    total + piece * jnp.where(n == listed + t, 1.0, 0.0).astype(jnp.float32)
                    for t, total in enumerate(sums)
                ]

                @pl.when(n < listed)
                def _():
                    add_face(grad_ref, n, f, piece)

            for t in range(listed):
                sends[f][t] = sums[t].astype(jnp.bfloat16)


def add_face(ref, n, f, piece):
    near_end = f % 2 == 1
    if f < 2:
        start = 0 if near_end else V - FACE
        ref[n, start : start + FACE] += piece
    else:
        for a in range(EDGE):
            start = a * FACE + (0 if near_end else FACE - EDGE)
            ref[n, start : start + EDGE] += piece[a * EDGE : (a + 1) * EDGE]


def data_call(neighbours, grad_in, occ_rows, weight, after):
    listed, _, width = grad_in.shape
    layer = jax.ShapeDtypeStruct((listed, FACE, width), jnp.bfloat16)
    return pl.pallas_call(
        data_kernel,
        grid=(listed,),
        in_specs=[
            smem(), by_brick((V, width)), by_brick((1, V)), whole(weight.shape), anywhere()
        ],
        out_specs=[whole((listed, V, width))] + [whole(layer.shape)] * 4,
        out_shape=[jax.ShapeDtypeStruct((listed, V, width), jnp.float32)] + [layer] * 4,
        scratch_shapes=[
            pltpu.VMEM((EDGE + 2, PLANE, width), jnp.float32),
            pltpu.VMEM((width // 128, V, 128), jnp.float32),
            pltpu.VMEM((2, 3, listed * FACE, width), jnp.bfloat16),
            pltpu.VMEM((listed, 4, FACE, width), jnp.float32),
        ],
        compiler_params=params(32),
        cost_estimate=pl.CostEstimate(
            flops=2 * listed * V * (TAPS + 3) * width * width,
            bytes_accessed=10 * MIB,
            transcendentals=0,
        ),
        name="data_gradient",
    )(neighbours, grad_in, occ_rows, weight, after)


def finish_kernel(
    grad_ref, r0, r1, r2, r3, feat_ref, occ_ref, buf_ref, after_ref, out_ref, work_ref
):
    width = feat_ref.shape[2]
    work_ref[...] = grad_ref[...]
    for f, far in enumerate((r0, r1, r2, r3)):
        add_face(work_ref, 0, f, far[0].astype(jnp.float32))
    values = feat_ref[0].astype(jnp.float32)
    r = norm_scale(values)
    u = values * r
    sig = sigmoid(u)
    d_u = mask_of(occ_ref[0], width) * work_ref[0] * (sig * (1.0 + u * (1.0 - sig)))
    pulled = r * (d_u - u * jnp.mean(u * d_u, axis=-1, keepdims=True))
    out_ref[0] = (buf_ref[0].astype(jnp.float32) + pulled).astype(jnp.bfloat16)


def finish_call(grad, remote, features, occ_rows, grad_in, after):
    listed, _, width = features.shape
    return pl.pallas_call(
        finish_kernel,
        grid=(listed,),
        in_specs=[by_brick((V, width))]
        + [by_brick((FACE, width))] * 4
        + [by_brick((V, width)), by_brick((1, V)), by_brick((V, width)), anywhere()],
        out_specs=by_brick((V, width)),
        out_shape=jax.ShapeDtypeStruct((listed, V, width), jnp.bfloat16),
        scratch_shapes=[pltpu.VMEM((1, V, width), jnp.float32)],
        compiler_params=params(16),
        name="input_gradient",
    )(grad, *remote, features, occ_rows, grad_in, after)


def body(features, occupancy, routes, neighbours, weight, cotangent):
    listed, _, width = features.shape
    slots = cotangent.shape[0]
    rows, columns = lax.axis_size("gx"), lax.axis_size("gy")
    depth = rows // 2
    p = lax.axis_index("gx").astype(jnp.int32)
    z, c = p // 2, p % 2
    core = c.reshape(1)
    occ_rows = occupancy.reshape(listed, 1, V)
    neighbours = inner_neighbours(neighbours, listed)
    steps = jnp.arange(slots, dtype=jnp.int32)
    def way_of(core_id):
        return 1 - 2 * core_id

    source_core = (c + steps) % 2
    from_place = (z - way_of(source_core) * (steps // 2)) % depth * 2 + source_core
    route = routes[:, 0]
    out_place = way_of(c) * (route // 2 - z) % depth * 2 + (route + c) % 2

    hidden, *layers = hidden_call(features, occ_rows)
    remote = [
        from_behind(layers[1], "gx", 1),
        from_behind(layers[0], "gx", -1),
        from_behind(layers[3], "gy", 1),
        from_behind(layers[2], "gy", -1),
    ]
    lower, upper = cotangent[:, : V // 2], cotangent[:, V // 2 :]
    upper = hold_call([upper], remote[:2])[0]
    came = [lax.all_to_all(part, "gx", 0, 0, tiled=True) for part in (lower, upper)]
    placed = forward_call(
        neighbours, out_place, hidden, layers, remote, features, occ_rows,
        weight.reshape(9, 3 * width, width), slots,
    )
    scale = float(listed * rows * columns * V) ** (-0.5)
    mine, theirs, grad_in = weight_call(
        neighbours, routes, core, hidden, layers, remote, came, occ_rows, scale, jnp.bfloat16,
        placed[0],
    )
    near, far, back = hold_call(placed[1:], came)
    near, far, back = hop(near, 1), hop(far, 1), hop(back, -1)
    near, far, back, theirs = hold_call([near, far, back, theirs], [mine])
    far = hop(far, 1)

    chip_sum = chip_call(mine, to_other_core(theirs), [far])
    mate = to_other_core(jnp.stack([block[1] for block in (placed[0], near, far, back)]))
    owned_out = collect_call(from_place, placed[0], near, far, back, mate)
    same_core = [
        [(2 * layer + core_id) * columns + q for q in range(columns) for layer in range(depth)]
        for core_id in range(2)
    ]

    def all_to_all(pieces):
        return lax.all_to_all(
            pieces, ("gx", "gy"), 0, 0, axis_index_groups=same_core, tiled=True
        )

    parts = all_to_all(chip_sum.reshape(columns * depth, -1, width // 2))
    grad, *sends = data_call(neighbours, grad_in, occ_rows, weight, chip_sum)
    landed = [
        from_behind(sends[1], "gx", 1),
        from_behind(sends[0], "gx", -1),
        from_behind(sends[3], "gy", 1),
        from_behind(sends[2], "gy", -1),
    ]
    arrived = [landed[1], landed[0], landed[3], landed[2]]

    pieces = total_call(parts, columns * depth, [*arrived, mate])
    own = all_to_all(pieces)
    input_grad = finish_call(grad, arrived, features, occ_rows, grad_in, pieces)
    own = hold_call([own], [input_grad, owned_out])[0].reshape(chip_sum.shape)
    weight_grad = join_call(core, own, to_other_core(own), input_grad)
    return (owned_out, input_grad, weight_grad)


def solution(mesh):
    return jax.shard_map(
        body,
        mesh=mesh,
        in_specs=(
            P(("gx", "gy"), None, None),
            P(("gx", "gy"), None),
            P(("gx", "gy"), None),
            P(("gx", "gy"), None),
            P(),
            P(("gx", "gy"), None, None),
        ),
        out_specs=(P(("gx", "gy"), None, None), P(("gx", "gy"), None, None), P()),
        check_vma=False,
    )
```

time: 441 us -> 170 us (0.39); the launches traced: 432 us -> 170 us
  local copies, waits for them, and re-layouts: 131 us -> 22.3 us
  waiting for transfers between devices: 111 us -> 42 us
  matrix products: 56.6 us -> 0 us
  Pallas kernels: 0 us -> 51.1 us
  blocking collectives: 33.8 us -> 0 us
  other arithmetic: 26.9 us -> 1.26 us
  loops' own time: 15.5 us -> 0 us
  between operations: 15.2 us -> 1.05 us
  starting transfers between devices: 41.9 us -> 51.9 us
    psum x1 -> x0, waiting for transfers between devices: 108 us -> none  [body(): lax.psum(kernel_part, ('gx', 'gy'))]
    dot_general x30 -> x0, matrix products: 56.6 us -> none  [the longest x2 26.1 us: one_group(): lax.dot_general(columns, grad_flat, (((0,), (0,)), ((), ())), preferred_e...]
    pallas_call x0 -> x13, Pallas kernels: none -> 51.1 us  [the longest x1 15.2 us: weight_call(): pl.pallas_call(lambda *refs: weight_kernel(*refs, scale=scale), grid=(4,)...]
    gather x18 -> x0, local copies, waits for them, and re-layouts: 41.7 us -> none  [the longest x12 33.2 us: block_work(): turned[np.array([entry[0] for entry in face_taps(face_id)])]]
    all_to_all x1 -> x0, blocking collectives: 33.8 us -> none  [body(): lax.all_to_all(placed.astype(output_here.dtype).reshape((owners, most_eac...]
    while x244 -> x0, local copies, waits for them, and re-layouts: 30.1 us -> none
    ppermute x12 -> x15, waiting for transfers between devices: 3.07 us -> 25.2 us  [the longest x8 13.1 us: from_behind(): lax.ppermute(block, axis, [(i, (i + distance) % count) for i in range(cou...]
    all_to_all x1 -> x4, starting transfers between devices: 5.81 us -> 26.8 us  [the longest x2 14.8 us: all_to_all(): lax.all_to_all(pieces, ('gx', 'gy'), 0, 0, axis_index_groups=same_core, t...]
  transfers between devices with their start and end apart: 14 -> 19, of which waited for: 2 -> 9; matrix products, arithmetic and copies ran while one was open for 42% -> 1% of each run, Pallas kernels for 0% -> 27%
where the time goes in v1:
time: 170 us
  starting transfers between devices  51.9 us (31%)
  Pallas kernels  51.1 us (30%)
  waiting for transfers between devices  42 us (25%)
  local copies, waits for them, and re-layouts  22.3 us (13%)
    unnamed x97, local copies, waits for them, and re-layouts  18.1 us
    all_to_all x2, waiting for transfers between devices, all_to_all(): lax.all_to_all(pieces, ('gx', 'gy'), 0, 0, axis_index_groups=same_core, t...  16.4 us
    pallas_call x1, Pallas kernels, weight_call(): pl.pallas_call(lambda *refs: weight_kernel(*refs, scale=scale), grid=(4,)...  15.2 us
    all_to_all x2, starting transfers between devices, all_to_all(): lax.all_to_all(pieces, ('gx', 'gy'), 0, 0, axis_index_groups=same_core, t...  14.8 us
    ppermute x8, starting transfers between devices, from_behind(): lax.ppermute(block, axis, [(i, (i + distance) % count) for i in range(cou...  14 us
    ppermute x8, waiting for transfers between devices, from_behind(): lax.ppermute(block, axis, [(i, (i + distance) % count) for i in range(cou...  13.1 us
    pallas_call x1, Pallas kernels, forward_call(): pl.pallas_call(forward_kernel, grid=(listed,), in_specs=[smem(), smem(),...  12.9 us
    all_to_all x2, starting transfers between devices, body(): lax.all_to_all(part, 'gx', 0, 0, tiled=True)  11.9 us
  transfers between devices with their start and end apart: 19, of which 9 were waited for; matrix products, arithmetic and copies ran while one was open for 1% of the time, Pallas kernels for 27%

profile of v1, /device:TPU:1, one launch (start us, length us, event | category | flops | bytes accessed | tf_op | source)
XLA Modules:
  0.0 169.5 jit_solution(13555209965143797242)
XLA Ops:
  0.6 3.0 %fusion.10 = (bf16[8,256,256]{2,1,0:T(8,128)(2,1)}, bf16[8,256,256]{2,1,0:T(8,128)(2,1)}) fusion(bf16[8,512,256]{2,1,0:T(8,128)(2,1)} %param.11), kind=kLoop, calls=%fused_computation.34 | loop fusion | bytes 4194304 | tf_op jit(solution)/shard_map/slice | solution.py:628
  3.7 6.9 %all-to-all-start = ((bf16[8,256,256]{2,1,0:T(8,128)(2,1)}), bf16[8,256,256]{2,1,0:T(8,128)(2,1)S(1)}, u32[]{:S(2)}, u32[]{:S(2)}) async-start(bf16[8,256,256]{2,1,0:T(8,128)(2,1)} %get-tuple-element.52), calls=%async_computation | async-start | bytes 2097152 | tf_op jit(solution)/shard_map/all_to_all | solution.py:630
  10.7 2.1 %hidden.1 = (bf16[4,512,256]{2,1,0:T(8,128)(2,1)S(1)}, bf16[4,64,256]{2,1,0:T(8,128)(2,1)S(1)}, bf16[4,64,256]{2,1,0:T(8,128)(2,1)S(1)}, bf16[4,64,256]{2,1,0:T(8,128)(2,1)}, bf16[4,64,256]{2,1,0:T(8,128)(2,1)}) custom-call(bf16[4,512,256]{2,1,0:T(8,128)(2,1)S(1)} %copy-done.5, s32[4,1,512]{2,1,0:T(1,128)S(1)} %reshape.22.occ_ref.refs_12_), custom_call_target="tpu_custom_call" | custom-call | tf_op jit(solution)/shard_map/hidden/pallas_call | solution.py:96
  12.8 1.7 %collective-permute-start = (bf16[4,64,256]{2,1,0:T(8,128)(2,1)S(1)}, bf16[4,64,256]{2,1,0:T(8,128)(2,1)S(1)}, u32[]{:S(2)}, u32[]{:S(2)}) collective-permute-start(bf16[4,64,256]{2,1,0:T(8,128)(2,1)S(1)} %get-tuple-element.29.l1.refs_5_), channel_id=1, source_target_pairs={{0,16},{16,32},{32,48},{48,64},{64,80},{80,96},{96,112},{112,0},{1... | collective-permute-start | bytes 393224 | tf_op jit(solution)/shard_map/ppermute | solution.py:20
  14.5 4.9 %collective-permute-start.3 = (bf16[4,64,256]{2,1,0:T(8,128)(2,1)}, bf16[4,64,256]{2,1,0:T(8,128)(2,1)S(1)}, u32[]{:S(2)}, u32[]{:S(2)}) collective-permute-start(bf16[4,64,256]{2,1,0:T(8,128)(2,1)} %get-tuple-element.30.l2.refs_6_), channel_id=1, source_target_pairs={{0,15},{1,0},{2,1},{3,2},{4,3},{5,4},{6,5},{7,6},{8,7},{9,8},{10,9... | collective-permute-start | bytes 393224 | tf_op jit(solution)/shard_map/ppermute | solution.py:20
  19.6 6.6 %collective-permute-done.1.r1.refs_2_.refs_9_ = bf16[4,64,256]{2,1,0:T(8,128)(2,1)S(1)} collective-permute-done((bf16[4,64,256]{2,1,0:T(8,128)(2,1)S(1)}, bf16[4,64,256]{2,1,0:T(8,128)(2,1)S(1)}, u32[]{:S(2)}, u32[]{:S(2)}) %collective-permute-start.1) | collective-permute-done | bytes 131104 | tf_op jit(solution)/shard_map/ppermute | solution.py:20
  26.8 5.0 %all-to-all-start.1 = ((bf16[8,256,256]{2,1,0:T(8,128)(2,1)}), bf16[8,256,256]{2,1,0:T(8,128)(2,1)S(1)}, u32[]{:S(2)}, u32[]{:S(2)}) async-start(bf16[8,256,256]{2,1,0:T(8,128)(2,1)} %hold.4), calls=%async_computation.1 | async-start | bytes 2097152 | tf_op jit(solution)/shard_map/all_to_all | solution.py:630
  33.7 12.9 %forward.1 = (bf16[2,512,256]{2,1,0:T(8,128)(2,1)}, bf16[2,512,256]{2,1,0:T(8,128)(2,1)}, bf16[2,512,256]{2,1,0:T(8,128)(2,1)}, bf16[2,512,256]{2,1,0:T(8,128)(2,1)}) custom-call(s32[4,6]{1,0:T(4,128)} %or_select_fusion.near_ref.refs_0_, s32[4]{0:T(128)} %fusion.place_ref, bf16[4,512,256]{2,1,0:T(8,128)(2,1)} %copy-done.35, bf16[4,64,256]{2,1,0:T(8,128)(2,1)} %copy-done.37, ...), custom_call_target="tpu_custom_call" | custom-call | flops 7247757312 | bytes 10485760 | tf_op jit(solution)/shard_map/forward/pallas_call | solution.py:247
  47.0 2.4 %collective-permute-start.4 = (bf16[2,512,256]{2,1,0:T(8,128)(2,1)}, bf16[2,512,256]{2,1,0:T(8,128)(2,1)S(1)}, u32[]{:S(2)}, u32[]{:S(2)}) collective-permute-start(bf16[2,512,256]{2,1,0:T(8,128)(2,1)} %get-tuple-element.36), channel_id=1, source_target_pairs={{0,32},{16,112},{32,64},{48,16},{64,96},{80,48},{96,0},{112,80},{1... | collective-permute-start | bytes 1572872 | tf_op jit(solution)/shard_map/ppermute | solution.py:37
  50.9 15.2 %weight_gradient.1 = (f32[28,256,128]{2,1,0:T(8,128)S(1)}, bf16[28,256,128]{2,1,0:T(8,128)(2,1)S(1)}, bf16[4,512,256]{2,1,0:T(8,128)(2,1)S(1)}) custom-call(s32[4,6]{1,0:T(4,128)S(1)} %copy-done.33, s32[4,1]{1,0:T(4,128)S(1)} %copy.18.refs_1_, s32[1]{0:T(128)} %bitcast.6.refs_2_.core_ref, bf16[4,512,256]{2,1,0:T(8,128)(2,1)S(1)} %copy-done.36, ...), custom_call_target="tpu_custom_call" | custom-call | flops 7247757312 | bytes 10485760 | tf_op jit(solution)/shard_map/weight_gradient/pallas_call | solution.py:330
  67.1 2.8 %collective-permute-start.9 = (bf16[28,256,128]{2,1,0:T(8,128)(2,1)S(1)}, bf16[28,256,128]{2,1,0:T(8,128)(2,1)S(1)}, u32[]{:S(2)}, u32[]{:S(2)}) collective-permute-start(bf16[28,256,128]{2,1,0:T(8,128)(2,1)S(1)} %get-tuple-element.45), channel_id=1, source_target_pairs={{0,16},{16,0},{32,48},{48,32},{64,80},{80,64},{96,112},{112,96},{1... | collective-permute-start | bytes 5505032 | tf_op jit(solution)/shard_map/ppermute | solution.py:41
  70.5 7.7 %collective-permute-done.7.far_ref.refs_0_ = bf16[2,512,256]{2,1,0:T(8,128)(2,1)S(1)} collective-permute-done((bf16[2,512,256]{2,1,0:T(8,128)(2,1)S(1)}, bf16[2,512,256]{2,1,0:T(8,128)(2,1)S(1)}, u32[]{:S(2)}, u32[]{:S(2)}) %collective-permute-start.7) | collective-permute-done | bytes 524320 | tf_op jit(solution)/shard_map/ppermute | solution.py:37
  80.3 8.9 %all-to-all-start.2 = ((bf16[64,112,128]{2,1,0:T(8,128)(2,1)}), bf16[64,112,128]{2,1,0:T(8,128)(2,1)S(1)}, u32[]{:S(2)}, u32[]{:S(2)}) async-start(bf16[64,112,128]{2,1,0:T(8,128)(2,1)} %bitcast.23), calls=%async_computation.2 | async-start | bytes 3670016 | tf_op jit(solution)/shard_map/all_to_all | solution.py:654
  92.0 2.0 %copy-done.34 = bf16[27,256,256]{2,1,0:T(8,128)(2,1)S(1)} copy-done((bf16[27,256,256]{2,1,0:T(8,128)(2,1)S(1)}, bf16[27,256,256]{2,1,0:T(8,128)(2,1)}, u32[]{:S(2)}) %copy-start.34) | copy-done | bytes 3538968
  94.0 11.0 %data_gradient.1 = (f32[4,512,256]{2,1,0:T(8,128)S(1)}, bf16[4,64,256]{2,1,0:T(8,128)(2,1)S(1)}, bf16[4,64,256]{2,1,0:T(8,128)(2,1)S(1)}, bf16[4,64,256]{2,1,0:T(8,128)(2,1)S(1)}, bf16[4,64,256]{2,1,0:T(8,128)(2,1)S(1)}) custom-call(s32[4,6]{1,0:T(4,128)S(1)} %copy-done.33, bf16[4,512,256]{2,1,0:T(8,128)(2,1)S(1)} %copy-done.16, ...), custom_call_target="tpu_custom_call" | custom-call | flops 8053063680 | bytes 10485760 | tf_op jit(solution)/shard_map/data_gradient/pallas_call | solution.py:546
  108.6 5.0 %collective-permute-start.12 = (bf16[4,64,256]{2,1,0:T(8,128)(2,1)S(1)}, bf16[4,64,256]{2,1,0:T(8,128)(2,1)S(1)}, u32[]{:S(2)}, u32[]{:S(2)}) collective-permute-start(bf16[4,64,256]{2,1,0:T(8,128)(2,1)S(1)} %get-tuple-element.49), channel_id=1, source_target_pairs={{0,15},{1,0},{2,1},{3,2},{4,3},{5,4},{6,5},{7,6},{8,7},{9,8},{10,9... | collective-permute-start | bytes 393224 | tf_op jit(solution)/shard_map/ppermute | solution.py:20
  116.9 4.6 %collective-permute-done.13.refs_3_.r3 = bf16[4,64,256]{2,1,0:T(8,128)(2,1)S(1)} collective-permute-done((bf16[4,64,256]{2,1,0:T(8,128)(2,1)S(1)}, bf16[4,64,256]{2,1,0:T(8,128)(2,1)S(1)}, u32[]{:S(2)}, u32[]{:S(2)}) %collective-permute-start.13) | collective-permute-done | bytes 131104 | tf_op jit(solution)/shard_map/ppermute | solution.py:20
  126.4 6.0 %all-to-all-start.3 = ((bf16[64,112,128]{2,1,0:T(8,128)(2,1)}), bf16[64,112,128]{2,1,0:T(8,128)(2,1)S(1)}, u32[]{:S(2)}, u32[]{:S(2)}) async-start(bf16[64,112,128]{2,1,0:T(8,128)(2,1)} %total.1.after_ref), calls=%async_computation.3 | async-start | bytes 3670016 | tf_op jit(solution)/shard_map/all_to_all | solution.py:654
  135.5 2.0 %collect.1.refs_2_ = bf16[8,512,256]{2,1,0:T(8,128)(2,1)} custom-call(s32[8]{0:T(128)S(1)} %fusion.4.place_ref, bf16[2,512,256]{2,1,0:T(8,128)(2,1)S(1)} %copy-done.14, bf16[2,512,256]{2,1,0:T(8,128)(2,1)S(1)} %get-tuple-element.41.near_ref, bf16[2,512,256]{2,1,0:T(8,128)(2,1)S(1)} %copy-done.10, bf16[2,512,256]{2,1,0:T(8,128)(2,1)S(1)} %copy-done.8, ...), custom_call_target="tpu_custom_call" | custom-call | tf_op jit(solution)/shard_map/collect/pallas_call | solution.py:131
  138.5 2.9 %input_gradient.1.refs_1_.after_ref = bf16[4,512,256]{2,1,0:T(8,128)(2,1)} custom-call(f32[4,512,256]{2,1,0:T(8,128)S(1)} %copy-done.12, bf16[4,64,256]{2,1,0:T(8,128)(2,1)S(1)} %collective-permute-done.10.refs_0_.r0, bf16[4,64,256]{2,1,0:T(8,128)(2,1)S(1)} %copy-done.20, bf16[4,64,256]{2,1,0:T(8,128)(2,1)S(1)} %copy-done.23, ...), custom_call_target="tpu_custom_call" | custom-call | tf_op jit(solution)/shard_map/input_gradient/pallas_call | solution.py:588
  141.3 16.4 %all-to-all-done.3.refs_0_ = bf16[64,112,128]{2,1,0:T(8,128)(2,1)S(1)} async-done(((bf16[64,112,128]{2,1,0:T(8,128)(2,1)}), bf16[64,112,128]{2,1,0:T(8,128)(2,1)S(1)}, u32[]{:S(2)}, u32[]{:S(2)}) %all-to-all-start.3) | async-done | bytes 1835040 | tf_op jit(solution)/shard_map/all_to_all | solution.py:654
  160.6 2.4 %collective-permute-start.14 = (bf16[28,256,128]{2,1,0:T(8,128)(2,1)S(1)}, bf16[28,256,128]{2,1,0:T(8,128)(2,1)S(1)}, u32[]{:S(2)}, u32[]{:S(2)}) collective-permute-start(bf16[28,256,128]{2,1,0:T(8,128)(2,1)S(1)} %bitcast.21), channel_id=1, source_target_pairs={{0,16},{16,0},{32,48},{48,32},{64,80},{80,64},{96,112},{112,96},{1... | collective-permute-start | bytes 5505032 | tf_op jit(solution)/shard_map/ppermute | solution.py:41
  163.0 3.4 %collective-permute-done.14.other_ref = bf16[28,256,128]{2,1,0:T(8,128)(2,1)S(1)} collective-permute-done((bf16[28,256,128]{2,1,0:T(8,128)(2,1)S(1)}, bf16[28,256,128]{2,1,0:T(8,128)(2,1)S(1)}, u32[]{:S(2)}, u32[]{:S(2)}) %collective-permute-start.14) | collective-permute-done | bytes 1835040 | tf_op jit(solution)/shard_map/ppermute | solution.py:41
  166.4 3.1 %join.1 = f32[27,256,256]{2,1,0:T(8,128)} custom-call(s32[1]{0:T(128)} %bitcast.6.refs_2_.core_ref, bf16[28,256,128]{2,1,0:T(8,128)(2,1)S(1)} %bitcast.22, bf16[28,256,128]{2,1,0:T(8,128)(2,1)S(1)} %collective-permute-done.14.other_ref, bf16[4,512,256]{2,1,0:T(8,128)(2,1)S(1)} %copy-done.1), custom_call_target="tpu_custom_call" | custom-call | tf_op jit(solution)/shard_map/join/pallas_call | solution.py:415
  (137 shorter events, 29.6 us)
Async XLA Ops:
  3.7 22.5 %all-to-all-start = ((bf16[8,256,256]{2,1,0:T(8,128)(2,1)}), bf16[8,256,256]{2,1,0:T(8,128)(2,1)S(1)}, u32[]{:S(2)}, u32[]{:S(2)}) async-start(bf16[8,256,256]{2,1,0:T(8,128)(2,1)} %get-tuple-element.52), calls=%async_computation | async-start | bytes 2097152 | tf_op jit(solution)/shard_map/all_to_all | solution.py:630
  10.7 15.6 %copy-start.31 = (s32[4,1,512]{2,1,0:T(1,128)}, s32[4,1,512]{2,1,0:T(1,128)S(1)}, u32[]{:S(2)}) copy-start(s32[4,1,512]{2,1,0:T(1,128)S(1)} %reshape.22.occ_ref.refs_12_) | copy-start | bytes 24580
  12.7 13.5 %copy-start.35 = (bf16[4,512,256]{2,1,0:T(8,128)(2,1)}, bf16[4,512,256]{2,1,0:T(8,128)(2,1)S(1)}, u32[]{:S(2)}) copy-start(bf16[4,512,256]{2,1,0:T(8,128)(2,1)S(1)} %get-tuple-element.27.hid_ref.refs_3_) | copy-start | bytes 3145732
  12.7 13.5 %copy-start.37 = (bf16[4,64,256]{2,1,0:T(8,128)(2,1)}, bf16[4,64,256]{2,1,0:T(8,128)(2,1)S(1)}, u32[]{:S(2)}) copy-start(bf16[4,64,256]{2,1,0:T(8,128)(2,1)S(1)} %get-tuple-element.28.l0.refs_4_) | copy-start | bytes 393220
  12.7 13.5 %copy-start.39 = (bf16[4,64,256]{2,1,0:T(8,128)(2,1)}, bf16[4,64,256]{2,1,0:T(8,128)(2,1)S(1)}, u32[]{:S(2)}) copy-start(bf16[4,64,256]{2,1,0:T(8,128)(2,1)S(1)} %get-tuple-element.29.l1.refs_5_) | copy-start | bytes 393220
  12.8 13.4 %collective-permute-start.1 = (bf16[4,64,256]{2,1,0:T(8,128)(2,1)S(1)}, bf16[4,64,256]{2,1,0:T(8,128)(2,1)S(1)}, u32[]{:S(2)}, u32[]{:S(2)}) collective-permute-start(bf16[4,64,256]{2,1,0:T(8,128)(2,1)S(1)} %get-tuple-element.28.l0.refs_4_), channel_id=1, source_target_pairs={{0,112},{16,0},{32,16},{48,32},{64,48},{80,64},{96,80},{112,96},{1... | collective-permute-start | bytes 393224 | tf_op jit(solution)/shard_map/ppermute | solution.py:20
  12.8 13.4 %collective-permute-start = (bf16[4,64,256]{2,1,0:T(8,128)(2,1)S(1)}, bf16[4,64,256]{2,1,0:T(8,128)(2,1)S(1)}, u32[]{:S(2)}, u32[]{:S(2)}) collective-permute-start(bf16[4,64,256]{2,1,0:T(8,128)(2,1)S(1)} %get-tuple-element.29.l1.refs_5_), channel_id=1, source_target_pairs={{0,16},{16,32},{32,48},{48,64},{64,80},{80,96},{96,112},{112,0},{1... | collective-permute-start | bytes 393224 | tf_op jit(solution)/shard_map/ppermute | solution.py:20
  14.5 18.5 %collective-permute-start.3 = (bf16[4,64,256]{2,1,0:T(8,128)(2,1)}, bf16[4,64,256]{2,1,0:T(8,128)(2,1)S(1)}, u32[]{:S(2)}, u32[]{:S(2)}) collective-permute-start(bf16[4,64,256]{2,1,0:T(8,128)(2,1)} %get-tuple-element.30.l2.refs_6_), channel_id=1, source_target_pairs={{0,15},{1,0},{2,1},{3,2},{4,3},{5,4},{6,5},{7,6},{8,7},{9,8},{10,9... | collective-permute-start | bytes 393224 | tf_op jit(solution)/shard_map/ppermute | solution.py:20
  19.4 13.6 %collective-permute-start.2 = (bf16[4,64,256]{2,1,0:T(8,128)(2,1)}, bf16[4,64,256]{2,1,0:T(8,128)(2,1)S(1)}, u32[]{:S(2)}, u32[]{:S(2)}) collective-permute-start(bf16[4,64,256]{2,1,0:T(8,128)(2,1)} %get-tuple-element.31.l3.refs_7_), channel_id=1, source_target_pairs={{0,1},{1,2},{2,3},{3,4},{4,5},{5,6},{6,7},{7,8},{8,9},{9,10},{10,1... | collective-permute-start | bytes 393224 | tf_op jit(solution)/shard_map/ppermute | solution.py:20
  26.8 20.1 %all-to-all-start.1 = ((bf16[8,256,256]{2,1,0:T(8,128)(2,1)}), bf16[8,256,256]{2,1,0:T(8,128)(2,1)S(1)}, u32[]{:S(2)}, u32[]{:S(2)}) async-start(bf16[8,256,256]{2,1,0:T(8,128)(2,1)} %hold.4), calls=%async_computation.1 | async-start | bytes 2097152 | tf_op jit(solution)/shard_map/all_to_all | solution.py:630
  47.0 19.1 %collective-permute-start.4 = (bf16[2,512,256]{2,1,0:T(8,128)(2,1)}, bf16[2,512,256]{2,1,0:T(8,128)(2,1)S(1)}, u32[]{:S(2)}, u32[]{:S(2)}) collective-permute-start(bf16[2,512,256]{2,1,0:T(8,128)(2,1)} %get-tuple-element.36), channel_id=1, source_target_pairs={{0,32},{16,112},{32,64},{48,16},{64,96},{80,48},{96,0},{112,80},{1... | collective-permute-start | bytes 1572872 | tf_op jit(solution)/shard_map/ppermute | solution.py:37
  49.4 17.7 %collective-permute-start.5 = (bf16[2,512,256]{2,1,0:T(8,128)(2,1)}, bf16[2,512,256]{2,1,0:T(8,128)(2,1)S(1)}, u32[]{:S(2)}, u32[]{:S(2)}) collective-permute-start(bf16[2,512,256]{2,1,0:T(8,128)(2,1)} %get-tuple-element.37), channel_id=1, source_target_pairs={{0,32},{16,112},{32,64},{48,16},{64,96},{80,48},{96,0},{112,80},{1... | collective-permute-start | bytes 1572872 | tf_op jit(solution)/shard_map/ppermute | solution.py:37
  50.0 17.1 %collective-permute-start.6 = (bf16[2,512,256]{2,1,0:T(8,128)(2,1)}, bf16[2,512,256]{2,1,0:T(8,128)(2,1)S(1)}, u32[]{:S(2)}, u32[]{:S(2)}) collective-permute-start(bf16[2,512,256]{2,1,0:T(8,128)(2,1)} %get-tuple-element.38), channel_id=1, source_target_pairs={{0,96},{16,48},{32,0},{48,80},{64,32},{80,112},{96,64},{112,16},{1... | collective-permute-start | bytes 1572872 | tf_op jit(solution)/shard_map/ppermute | solution.py:37
  67.1 23.1 %copy-start.7 = (bf16[2,512,256]{2,1,0:T(8,128)(2,1)}, bf16[2,512,256]{2,1,0:T(8,128)(2,1)S(1)}, u32[]{:S(2)}) copy-start(bf16[2,512,256]{2,1,0:T(8,128)(2,1)S(1)} %get-tuple-element.43.back_ref) | copy-start | bytes 1572868
  67.1 11.1 %collective-permute-start.9 = (bf16[28,256,128]{2,1,0:T(8,128)(2,1)S(1)}, bf16[28,256,128]{2,1,0:T(8,128)(2,1)S(1)}, u32[]{:S(2)}, u32[]{:S(2)}) collective-permute-start(bf16[28,256,128]{2,1,0:T(8,128)(2,1)S(1)} %get-tuple-element.45), channel_id=1, source_target_pairs={{0,16},{16,0},{32,48},{48,32},{64,80},{80,64},{96,112},{112,96},{1... | collective-permute-start | bytes 5505032 | tf_op jit(solution)/shard_map/ppermute | solution.py:41
  69.9 8.3 %collective-permute-start.7 = (bf16[2,512,256]{2,1,0:T(8,128)(2,1)S(1)}, bf16[2,512,256]{2,1,0:T(8,128)(2,1)S(1)}, u32[]{:S(2)}, u32[]{:S(2)}) collective-permute-start(bf16[2,512,256]{2,1,0:T(8,128)(2,1)S(1)} %get-tuple-element.42), channel_id=1, source_target_pairs={{0,32},{16,112},{32,64},{48,16},{64,96},{80,48},{96,0},{112,80},{1... | collective-permute-start | bytes 1572872 | tf_op jit(solution)/shard_map/ppermute | solution.py:37
  80.3 41.8 %all-to-all-start.2 = ((bf16[64,112,128]{2,1,0:T(8,128)(2,1)}), bf16[64,112,128]{2,1,0:T(8,128)(2,1)S(1)}, u32[]{:S(2)}, u32[]{:S(2)}) async-start(bf16[64,112,128]{2,1,0:T(8,128)(2,1)} %bitcast.23), calls=%async_computation.2 | async-start | bytes 3670016 | tf_op jit(solution)/shard_map/all_to_all | solution.py:654
  90.4 23.2 %collective-permute-start.8 = (bf16[4,512,256]{2,1,0:T(8,128)(2,1)S(1)}, bf16[4,512,256]{2,1,0:T(8,128)(2,1)S(1)}, u32[]{:S(2)}, u32[]{:S(2)}) collective-permute-start(bf16[4,512,256]{2,1,0:T(8,128)(2,1)S(1)} %pad_maximum_fusion), channel_id=1, source_target_pairs={{0,16},{16,0},{32,48},{48,32},{64,80},{80,64},{96,112},{112,96},{1... | collective-permute-start | bytes 3145736 | tf_op jit(solution)/shard_map/ppermute | solution.py:41
  106.3 7.8 %collective-permute-start.10 = (bf16[4,64,256]{2,1,0:T(8,128)(2,1)S(1)}, bf16[4,64,256]{2,1,0:T(8,128)(2,1)S(1)}, u32[]{:S(2)}, u32[]{:S(2)}) collective-permute-start(bf16[4,64,256]{2,1,0:T(8,128)(2,1)S(1)} %get-tuple-element.47), channel_id=1, source_target_pairs={{0,112},{16,0},{32,16},{48,32},{64,48},{80,64},{96,80},{112,96},{1... | collective-permute-start | bytes 393224 | tf_op jit(solution)/shard_map/ppermute | solution.py:20
  107.5 6.6 %collective-permute-start.11 = (bf16[4,64,256]{2,1,0:T(8,128)(2,1)S(1)}, bf16[4,64,256]{2,1,0:T(8,128)(2,1)S(1)}, u32[]{:S(2)}, u32[]{:S(2)}) collective-permute-start(bf16[4,64,256]{2,1,0:T(8,128)(2,1)S(1)} %get-tuple-element.48), channel_id=1, source_target_pairs={{0,16},{16,32},{32,48},{48,64},{64,80},{80,96},{96,112},{112,0},{1... | collective-permute-start | bytes 393224 | tf_op jit(solution)/shard_map/ppermute | solution.py:20
  108.6 7.6 %collective-permute-start.12 = (bf16[4,64,256]{2,1,0:T(8,128)(2,1)S(1)}, bf16[4,64,256]{2,1,0:T(8,128)(2,1)S(1)}, u32[]{:S(2)}, u32[]{:S(2)}) collective-permute-start(bf16[4,64,256]{2,1,0:T(8,128)(2,1)S(1)} %get-tuple-element.49), channel_id=1, source_target_pairs={{0,15},{1,0},{2,1},{3,2},{4,3},{5,4},{6,5},{7,6},{8,7},{9,8},{10,9... | collective-permute-start | bytes 393224 | tf_op jit(solution)/shard_map/ppermute | solution.py:20
  113.6 7.8 %collective-permute-start.13 = (bf16[4,64,256]{2,1,0:T(8,128)(2,1)S(1)}, bf16[4,64,256]{2,1,0:T(8,128)(2,1)S(1)}, u32[]{:S(2)}, u32[]{:S(2)}) collective-permute-start(bf16[4,64,256]{2,1,0:T(8,128)(2,1)S(1)} %get-tuple-element.50), channel_id=1, source_target_pairs={{0,1},{1,2},{2,3},{3,4},{4,5},{5,6},{6,7},{7,8},{8,9},{9,10},{10,1... | collective-permute-start | bytes 393224 | tf_op jit(solution)/shard_map/ppermute | solution.py:20
  126.4 31.4 %all-to-all-start.3 = ((bf16[64,112,128]{2,1,0:T(8,128)(2,1)}), bf16[64,112,128]{2,1,0:T(8,128)(2,1)S(1)}, u32[]{:S(2)}, u32[]{:S(2)}) async-start(bf16[64,112,128]{2,1,0:T(8,128)(2,1)} %total.1.after_ref), calls=%async_computation.3 | async-start | bytes 3670016 | tf_op jit(solution)/shard_map/all_to_all | solution.py:654
  160.6 5.8 %collective-permute-start.14 = (bf16[28,256,128]{2,1,0:T(8,128)(2,1)S(1)}, bf16[28,256,128]{2,1,0:T(8,128)(2,1)S(1)}, u32[]{:S(2)}, u32[]{:S(2)}) collective-permute-start(bf16[28,256,128]{2,1,0:T(8,128)(2,1)S(1)} %bitcast.21), channel_id=1, source_target_pairs={{0,16},{16,0},{32,48},{48,32},{64,80},{80,64},{96,112},{112,96},{1... | collective-permute-start | bytes 5505032 | tf_op jit(solution)/shard_map/ppermute | solution.py:41
  (44 other events, 111.5 us)

commit v2 on v1

--- a/solution.py
+++ b/solution.py
@@ -61,6 +61,15 @@
 
 def anywhere():
     return pl.BlockSpec(memory_space=pl.ANY)
+
+
+def glance(arrays):
+    specs = []
+    for array in arrays:
+        zeros = (0,) * array.ndim
+        block = (1,) * (array.ndim - 2) + (16, 128)
+        specs.append(pl.BlockSpec(block, lambda *_, zeros=zeros: zeros))
+    return specs
 
 
 def mask_of(occ_row, width):
@@ -99,7 +108,7 @@
         in_specs=[by_brick((V, width)), by_brick((1, V))],
         out_specs=[by_brick((V, width))] + [by_brick((FACE, width))] * 4,
         out_shape=[jax.ShapeDtypeStruct((listed, V, width), jnp.bfloat16)] + [layer] * 4,
-        compiler_params=params(16),
+        compiler_params=params(56),
         name="hidden",
     )(features, occ_rows)
 
@@ -111,7 +120,8 @@
 def hold_call(blocks, after):
     return pl.pallas_call(
         hold_kernel,
-        in_specs=[anywhere()] * (len(blocks) + len(after)),
+        grid=(1,),
+        in_specs=[anywhere()] * len(blocks) + glance(after),
         out_specs=[anywhere()] * len(blocks),
         out_shape=[jax.ShapeDtypeStruct(block.shape, block.dtype) for block in blocks],
         input_output_aliases={i: i for i in range(len(blocks))},
@@ -120,23 +130,46 @@
     )(*blocks, *after)
 
 
-def collect_kernel(place_ref, own_ref, near_ref, far_ref, back_ref, mate_ref, out_ref):
+def cut_kernel(blocks_ref, *refs):
+    refs[-1][...] = blocks_ref[...]
+
+
+def cut_call(blocks, part, parts, after):
+    count, rows, width = blocks.shape
+    shape = (count, rows // parts, width)
+    return pl.pallas_call(
+        cut_kernel,
+        grid=(count // 2,),
+        in_specs=[pl.BlockSpec((2,) + shape[1:], lambda i: (i, part, 0))] + glance(after),
+        out_specs=pl.BlockSpec((2,) + shape[1:], lambda i: (i, 0, 0)),
+        out_shape=jax.ShapeDtypeStruct(shape, blocks.dtype),
+        compiler_params=params(56),
+        name="cut",
+    )(blocks, *after)
+
+
+def collect_kernel(
+    place_ref, own_ref, near_ref, far_ref, back_ref, mate_ref, after_ref, out_ref
+):
     for step, came_ref in enumerate((own_ref, near_ref, far_ref, back_ref)):
         out_ref[place_ref[2 * step]] = came_ref[0]
         out_ref[place_ref[2 * step + 1]] = mate_ref[step]
 
 
-def collect_call(place, own, near, far, back, mate):
+def collect_call(place, own, near, far, back, mate, after):
     shape = (2 * mate.shape[0],) + mate.shape[1:]
     return pl.pallas_call(
         collect_kernel,
         grid=(1,),
-        in_specs=[smem()] + [whole(own.shape)] * 4 + [whole(mate.shape)],
+        in_specs=[smem()] + [whole(own.shape)] * 4 + [whole(mate.shape)] + glance([after]),
         out_specs=whole(shape),
         out_shape=jax.ShapeDtypeStruct(shape, mate.dtype),
-        compiler_params=params(20),
+        compiler_params=params(56),
+        cost_estimate=pl.CostEstimate(
+            flops=0, bytes_accessed=4 * shape[0] * shape[1] * shape[2], transcendentals=0
+        ),
         name="collect",
-    )(place, own, near, far, back, mate)
+    )(place, own, near, far, back, mate, after)
 
 
 def roll_c(block, shift):
@@ -332,7 +365,8 @@
         grid=(4,),
         in_specs=[smem(), smem(), smem(), whole(hidden.shape)]
         + [whole((listed, FACE, width))] * 8
-        + [whole(occ_rows.shape), anywhere()]
+        + [whole(occ_rows.shape)]
+        + glance([after])
         + [anywhere()] * len(came),
         out_specs=[block, block, whole(hidden.shape)],
         out_shape=[
@@ -364,7 +398,7 @@
     return pl.pallas_call(
         chip_kernel,
         grid=(taps // 7,),
-        in_specs=[block, block] + [anywhere()] * len(after),
+        in_specs=[block, block] + glance(after),
         out_specs=block,
         out_shape=jax.ShapeDtypeStruct(mine.shape, jnp.bfloat16),
         compiler_params=params(12),
@@ -384,7 +418,7 @@
     return pl.pallas_call(
         total_kernel,
         grid=(1,),
-        in_specs=[whole(parts.shape)] + [anywhere()] * len(after),
+        in_specs=[whole(parts.shape)] + glance(after),
         out_specs=whole((copies, rows, half)),
         out_shape=jax.ShapeDtypeStruct((copies, rows, half), jnp.bfloat16),
         compiler_params=params(20),
@@ -392,7 +426,7 @@
     )(parts, *after)
 
 
-def join_kernel(core_ref, own_ref, other_ref, after_ref, out_ref):
+def join_kernel(core_ref, own_ref, other_ref, after0_ref, after1_ref, out_ref):
     half = own_ref.shape[2]
     first = core_ref[0] == 0
 
@@ -415,16 +449,16 @@
     return pl.pallas_call(
         join_kernel,
         grid=(TAPS // 9,),
-        in_specs=[smem(), block, block, anywhere()],
+        in_specs=[smem(), block, block] + glance(after),
         out_specs=pl.BlockSpec((9, width, 2 * half), lambda t: (t, 0, 0)),
         out_shape=jax.ShapeDtypeStruct((TAPS, width, 2 * half), jnp.float32),
         compiler_params=params(16),
         name="join",
-    )(core, own, other, after)
+    )(core, own, other, *after)
 
 
 def data_kernel(
-    near_ref, buf_ref, occ_ref, w_ref, after_ref,
+    near_ref, buf_ref, occ_ref, w_ref,
     grad_ref, s0_ref, s1_ref, s2_ref, s3_ref,
     wide_ref, rows_ref, depth_ref, kept_ref,
 ):
@@ -540,15 +574,13 @@
             ref[n, start : start + EDGE] += piece[a * EDGE : (a + 1) * EDGE]
 
 
-def data_call(neighbours, grad_in, occ_rows, weight, after):
+def data_call(neighbours, grad_in, occ_rows, weight):
     listed, _, width = grad_in.shape
     layer = jax.ShapeDtypeStruct((listed, FACE, width), jnp.bfloat16)
     return pl.pallas_call(
         data_kernel,
         grid=(listed,),
-        in_specs=[
-            smem(), by_brick((V, width)), by_brick((1, V)), whole(weight.shape), anywhere()
-        ],
+        in_specs=[smem(), by_brick((V, width)), by_brick((1, V)), whole(weight.shape)],
         out_specs=[whole((listed, V, width))] + [whole(layer.shape)] * 4,
         out_shape=[jax.ShapeDtypeStruct((listed, V, width), jnp.float32)] + [layer] * 4,
         scratch_shapes=[
@@ -564,7 +596,7 @@
             transcendentals=0,
         ),
         name="data_gradient",
-    )(neighbours, grad_in, occ_rows, weight, after)
+    )(neighbours, grad_in, occ_rows, weight)
 
 
 def finish_kernel(
@@ -590,11 +622,15 @@
         grid=(listed,),
         in_specs=[by_brick((V, width))]
         + [by_brick((FACE, width))] * 4
-        + [by_brick((V, width)), by_brick((1, V)), by_brick((V, width)), anywhere()],
+        + [by_brick((V, width)), by_brick((1, V)), by_brick((V, width))]
+        + glance([after]),
         out_specs=by_brick((V, width)),
         out_shape=jax.ShapeDtypeStruct((listed, V, width), jnp.bfloat16),
         scratch_shapes=[pltpu.VMEM((1, V, width), jnp.float32)],
-        compiler_params=params(16),
+        compiler_params=params(56),
+        cost_estimate=pl.CostEstimate(
+            flops=0, bytes_accessed=10 * listed * V * width, transcendentals=listed * V * width
+        ),
         name="input_gradient",
     )(grad, *remote, features, occ_rows, grad_in, after)
 
@@ -625,9 +661,10 @@
         from_behind(layers[3], "gy", 1),
         from_behind(layers[2], "gy", -1),
     ]
-    lower, upper = cotangent[:, : V // 2], cotangent[:, V // 2 :]
-    upper = hold_call([upper], remote[:2])[0]
-    came = [lax.all_to_all(part, "gx", 0, 0, tiled=True) for part in (lower, upper)]
+    came = [
+        lax.all_to_all(cut_call(cotangent, part, 2, after), "gx", 0, 0, tiled=True)
+        for part, after in ((0, []), (1, remote[:2]))
+    ]
     placed = forward_call(
         neighbours, out_place, hidden, layers, remote, features, occ_rows,
         weight.reshape(9, 3 * width, width), slots,
@@ -642,9 +679,10 @@
     near, far, back, theirs = hold_call([near, far, back, theirs], [mine])
     far = hop(far, 1)
 
-    chip_sum = chip_call(mine, to_other_core(theirs), [far])
+    grad, *sends = data_call(neighbours, grad_in, occ_rows, weight)
+
+    chip_sum = chip_call(mine, to_other_core(theirs), [far, grad])
     mate = to_other_core(jnp.stack([block[1] for block in (placed[0], near, far, back)]))
-    owned_out = collect_call(from_place, placed[0], near, far, back, mate)
     same_core = [
         [(2 * layer + core_id) * columns + q for q in range(columns) for layer in range(depth)]
         for core_id in range(2)
@@ -656,7 +694,6 @@
         )
 
     parts = all_to_all(chip_sum.reshape(columns * depth, -1, width // 2))
-    grad, *sends = data_call(neighbours, grad_in, occ_rows, weight, chip_sum)
     landed = [
         from_behind(sends[1], "gx", 1),
         from_behind(sends[0], "gx", -1),
@@ -666,10 +703,10 @@
     arrived = [landed[1], landed[0], landed[3], landed[2]]
 
     pieces = total_call(parts, columns * depth, [*arrived, mate])
-    own = all_to_all(pieces)
+    own = all_to_all(pieces).reshape(chip_sum.shape)
+    owned_out = collect_call(from_place, placed[0], near, far, back, mate, pieces)
     input_grad = finish_call(grad, arrived, features, occ_rows, grad_in, pieces)
-    own = hold_call([own], [input_grad, owned_out])[0].reshape(chip_sum.shape)
-    weight_grad = join_call(core, own, to_other_core(own), input_grad)
+    weight_grad = join_call(core, own, to_other_core(own), [owned_out, input_grad])
     return (owned_out, input_grad, weight_grad)
 
 

time: 170 us -> 174 us (1.024)
  blocking collectives: 0 us -> 30 us
  waiting for transfers between devices: 42 us -> 22.9 us
  local copies, waits for them, and re-layouts: 22.3 us -> 8.71 us
  Pallas kernels: 51.1 us -> 61.8 us
  starting transfers between devices: 51.9 us -> 47.1 us
    all_to_all x0 -> x1, blocking collectives: none -> 30 us  [all_to_all(): lax.all_to_all(pieces, ('gx', 'gy'), 0, 0, axis_index_groups=same_core, t...]
    all_to_all x2 -> x1, waiting for transfers between devices: 16.4 us -> 0.01 us  [all_to_all(): lax.all_to_all(pieces, ('gx', 'gy'), 0, 0, axis_index_groups=same_core, t...]
    unnamed x97 -> x81, local copies, waits for them, and re-layouts: 18.1 us -> 5.94 us
    ppermute x8, waiting for transfers between devices: 13.1 us -> 21.3 us  [from_behind(): lax.ppermute(block, axis, [(i, (i + distance) % count) for i in range(cou...]
    ppermute x4, waiting for transfers between devices: 8.68 us -> 1.29 us  [hop(): return lax.ppermute(blocks, 'gx', ways)]
    all_to_all x2 -> x1, starting transfers between devices: 14.8 us -> 9.14 us  [all_to_all(): lax.all_to_all(pieces, ('gx', 'gy'), 0, 0, axis_index_groups=same_core, t...]
    pallas_call x5, Pallas kernels: 1.58 us -> 7.06 us  [the longest x2 6.73 us: cut_call(): pl.pallas_call(cut_kernel, grid=(count // 2,), in_specs=[pl.BlockSpec((2,...]
    ppermute x3, waiting for transfers between devices: 3.42 us -> 0.01 us  [to_other_core(): lax.ppermute(block, 'gx', [(p, p ^ 1) for p in range(lax.axis_size('gx'))])]
  transfers between devices with their start and end apart: 19 -> 18, of which waited for: 9 -> 8; matrix products, arithmetic and copies ran while one was open for 1% -> 3% of each run, Pallas kernels for 27% -> 31%
where the time goes in v2:
time: 174 us; the launch traced here: 173 us
  Pallas kernels  61.8 us (36%)
  starting transfers between devices  47.1 us (27%)
  blocking collectives  30 us (17%)
  waiting for transfers between devices  22.9 us (13%)
  local copies, waits for them, and re-layouts  8.71 us (5%)
  other arithmetic  1.85 us (1%)
    all_to_all x1, blocking collectives, all_to_all(): lax.all_to_all(pieces, ('gx', 'gy'), 0, 0, axis_index_groups=same_core, t...  30 us
    ppermute x8, waiting for transfers between devices, from_behind(): lax.ppermute(block, axis, [(i, (i + distance) % count) for i in range(cou...  21.3 us
    pallas_call x1, Pallas kernels, weight_call(): pl.pallas_call(lambda *refs: weight_kernel(*refs, scale=scale), grid=(4,)...  14.8 us
    ppermute x8, starting transfers between devices, from_behind(): lax.ppermute(block, axis, [(i, (i + distance) % count) for i in range(cou...  13.2 us
    pallas_call x1, Pallas kernels, forward_call(): pl.pallas_call(forward_kernel, grid=(listed,), in_specs=[smem(), smem(),...  12.9 us
    all_to_all x2, starting transfers between devices, body(): lax.all_to_all(cut_call(cotangent, part, 2, after), 'gx', 0, 0, tiled=True)  12.6 us
    pallas_call x1, Pallas kernels, data_call(): pl.pallas_call(data_kernel, grid=(listed,), in_specs=[smem(), by_brick((V...  11.2 us
    all_to_all x1, starting transfers between devices, all_to_all(): lax.all_to_all(pieces, ('gx', 'gy'), 0, 0, axis_index_groups=same_core, t...  9.14 us
  transfers between devices with their start and end apart: 18, of which 8 were waited for; matrix products, arithmetic and copies ran while one was open for 3% of the time, Pallas kernels for 31%

profile of v2, /device:TPU:1, one launch (start us, length us, event | category | flops | bytes accessed | tf_op | source)
XLA Modules:
  0.0 173.4 jit_solution(7243149013485289074)
XLA Ops:
  0.6 3.4 %cut.2 = bf16[8,256,256]{2,1,0:T(8,128)(2,1)} custom-call(bf16[8,512,256]{2,1,0:T(8,128)(2,1)} %blocks_ref.3), custom_call_target="tpu_custom_call" | custom-call | tf_op jit(solution)/shard_map/cut/pallas_call | solution.py:140
  4.0 6.8 %all-to-all-start = ((bf16[8,256,256]{2,1,0:T(8,128)(2,1)}), bf16[8,256,256]{2,1,0:T(8,128)(2,1)S(1)}, u32[]{:S(2)}, u32[]{:S(2)}) async-start(bf16[8,256,256]{2,1,0:T(8,128)(2,1)} %cut.2), calls=%async_computation | async-start | bytes 2097152 | tf_op jit(solution)/shard_map/all_to_all | solution.py:665
  11.4 3.9 %hidden.1 = (bf16[4,512,256]{2,1,0:T(8,128)(2,1)}, bf16[4,64,256]{2,1,0:T(8,128)(2,1)}, bf16[4,64,256]{2,1,0:T(8,128)(2,1)}, bf16[4,64,256]{2,1,0:T(8,128)(2,1)}, bf16[4,64,256]{2,1,0:T(8,128)(2,1)}) custom-call(bf16[4,512,256]{2,1,0:T(8,128)(2,1)} %feat_ref.5, s32[4,1,512]{2,1,0:T(1,128)} %reshape.22.occ_ref.refs_12_), custom_call_target="tpu_custom_call" | custom-call | tf_op jit(solution)/shard_map/hidden/pallas_call | solution.py:105
  18.2 3.7 %collective-permute-start.3 = (bf16[4,64,256]{2,1,0:T(8,128)(2,1)}, bf16[4,64,256]{2,1,0:T(8,128)(2,1)S(1)}, u32[]{:S(2)}, u32[]{:S(2)}) collective-permute-start(bf16[4,64,256]{2,1,0:T(8,128)(2,1)} %get-tuple-element.30.l2.refs_6_), channel_id=1, source_target_pairs={{0,15},{1,0},{2,1},{3,2},{4,3},{5,4},{6,5},{7,6},{8,7},{9,8},{10,9... | collective-permute-start | bytes 393224 | tf_op jit(solution)/shard_map/ppermute | solution.py:20
  22.0 2.3 %collective-permute-done.r0.refs_0_.refs_8_ = bf16[4,64,256]{2,1,0:T(8,128)(2,1)S(1)} collective-permute-done((bf16[4,64,256]{2,1,0:T(8,128)(2,1)}, bf16[4,64,256]{2,1,0:T(8,128)(2,1)S(1)}, u32[]{:S(2)}, u32[]{:S(2)}) %collective-permute-start) | collective-permute-done | bytes 131104 | tf_op jit(solution)/shard_map/ppermute | solution.py:20
  24.3 2.0 %collective-permute-done.1.r1.refs_1_.refs_9_ = bf16[4,64,256]{2,1,0:T(8,128)(2,1)S(1)} collective-permute-done((bf16[4,64,256]{2,1,0:T(8,128)(2,1)}, bf16[4,64,256]{2,1,0:T(8,128)(2,1)S(1)}, u32[]{:S(2)}, u32[]{:S(2)}) %collective-permute-start.1) | collective-permute-done | bytes 131104 | tf_op jit(solution)/shard_map/ppermute | solution.py:20
  27.0 3.4 %cut.3 = bf16[8,256,256]{2,1,0:T(8,128)(2,1)} custom-call(bf16[8,512,256]{2,1,0:T(8,128)(2,1)} %blocks_ref.3, bf16[4,64,256]{2,1,0:T(8,128)(2,1)} %copy-done.15, bf16[4,64,256]{2,1,0:T(8,128)(2,1)} %copy-done.17), custom_call_target="tpu_custom_call" | custom-call | tf_op jit(solution)/shard_map/cut/pallas_call | solution.py:140
  30.4 5.8 %all-to-all-start.1 = ((bf16[8,256,256]{2,1,0:T(8,128)(2,1)}), bf16[8,256,256]{2,1,0:T(8,128)(2,1)S(1)}, u32[]{:S(2)}, u32[]{:S(2)}) async-start(bf16[8,256,256]{2,1,0:T(8,128)(2,1)} %cut.3), calls=%async_computation.1 | async-start | bytes 2097152 | tf_op jit(solution)/shard_map/all_to_all | solution.py:665
  38.1 12.9 %forward.1 = (bf16[2,512,256]{2,1,0:T(8,128)(2,1)}, bf16[2,512,256]{2,1,0:T(8,128)(2,1)}, bf16[2,512,256]{2,1,0:T(8,128)(2,1)}, bf16[2,512,256]{2,1,0:T(8,128)(2,1)}) custom-call(s32[4,6]{1,0:T(4,128)} %or_select_fusion.near_ref.refs_0_, s32[4]{0:T(128)} %fusion.place_ref, bf16[4,512,256]{2,1,0:T(8,128)(2,1)} %get-tuple-element.27.hid_ref.refs_3_, ...), custom_call_target="tpu_custom_call" | custom-call | flops 7247757312 | bytes 10485760 | tf_op jit(solution)/shard_map/forward/pallas_call | solution.py:280
  51.4 2.4 %collective-permute-start.4 = (bf16[2,512,256]{2,1,0:T(8,128)(2,1)}, bf16[2,512,256]{2,1,0:T(8,128)(2,1)S(1)}, u32[]{:S(2)}, u32[]{:S(2)}) collective-permute-start(bf16[2,512,256]{2,1,0:T(8,128)(2,1)} %get-tuple-element.36), channel_id=1, source_target_pairs={{0,32},{16,112},{32,64},{48,16},{64,96},{80,48},{96,0},{112,80},{1... | collective-permute-start | bytes 1572872 | tf_op jit(solution)/shard_map/ppermute | solution.py:37
  55.4 14.8 %weight_gradient.1 = (f32[28,256,128]{2,1,0:T(8,128)S(1)}, bf16[28,256,128]{2,1,0:T(8,128)(2,1)S(1)}, bf16[4,512,256]{2,1,0:T(8,128)(2,1)S(1)}) custom-call(s32[4,6]{1,0:T(4,128)S(1)} %copy-done.20, s32[4,1]{1,0:T(4,128)S(1)} %copy.16.refs_1_, s32[1]{0:T(128)} %bitcast.6.refs_2_.core_ref, bf16[4,512,256]{2,1,0:T(8,128)(2,1)S(1)} %copy-done.22, ...), custom_call_target="tpu_custom_call" | custom-call | flops 7247757312 | bytes 10485760 | tf_op jit(solution)/shard_map/weight_gradient/pallas_call | solution.py:363
  71.5 2.7 %collective-permute-start.9 = (bf16[28,256,128]{2,1,0:T(8,128)(2,1)S(1)}, bf16[28,256,128]{2,1,0:T(8,128)(2,1)S(1)}, u32[]{:S(2)}, u32[]{:S(2)}) collective-permute-start(bf16[28,256,128]{2,1,0:T(8,128)(2,1)S(1)} %get-tuple-element.44), channel_id=1, source_target_pairs={{0,16},{16,0},{32,48},{48,32},{64,80},{80,64},{96,112},{112,96},{1... | collective-permute-start | bytes 5505032 | tf_op jit(solution)/shard_map/ppermute | solution.py:41
  74.9 11.2 %data_gradient.1 = (f32[4,512,256]{2,1,0:T(8,128)S(1)}, bf16[4,64,256]{2,1,0:T(8,128)(2,1)S(1)}, bf16[4,64,256]{2,1,0:T(8,128)(2,1)S(1)}, bf16[4,64,256]{2,1,0:T(8,128)(2,1)S(1)}, bf16[4,64,256]{2,1,0:T(8,128)(2,1)S(1)}) custom-call(s32[4,6]{1,0:T(4,128)S(1)} %copy-done.20, bf16[4,512,256]{2,1,0:T(8,128)(2,1)S(1)} %get-tuple-element.45.buf_ref, ...), custom_call_target="tpu_custom_call" | custom-call | flops 8053063680 | bytes 10485760 | tf_op jit(solution)/shard_map/data_gradient/pallas_call | solution.py:580
  88.8 9.1 %all-to-all-start.2 = ((bf16[64,112,128]{2,1,0:T(8,128)(2,1)}), bf16[64,112,128]{2,1,0:T(8,128)(2,1)S(1)}, u32[]{:S(2)}, u32[]{:S(2)}) async-start(bf16[64,112,128]{2,1,0:T(8,128)(2,1)} %bitcast.21), calls=%async_computation.2 | async-start | bytes 3670016 | tf_op jit(solution)/shard_map/all_to_all | solution.py:692
  101.4 1.7 collective-permute-start.11
  103.1 4.9 %collective-permute-start.12 = (bf16[4,64,256]{2,1,0:T(8,128)(2,1)S(1)}, bf16[4,64,256]{2,1,0:T(8,128)(2,1)S(1)}, u32[]{:S(2)}, u32[]{:S(2)}) collective-permute-start(bf16[4,64,256]{2,1,0:T(8,128)(2,1)S(1)} %copy-done.32), channel_id=1, source_target_pairs={{0,15},{1,0},{2,1},{3,2},{4,3},{5,4},{6,5},{7,6},{8,7},{9,8},{10,9... | collective-permute-start | bytes 393224 | tf_op jit(solution)/shard_map/ppermute | solution.py:20
  108.1 7.8 %collective-permute-done.10.refs_0_.r0 = bf16[4,64,256]{2,1,0:T(8,128)(2,1)S(1)} collective-permute-done((bf16[4,64,256]{2,1,0:T(8,128)(2,1)S(1)}, bf16[4,64,256]{2,1,0:T(8,128)(2,1)S(1)}, u32[]{:S(2)}, u32[]{:S(2)}) %collective-permute-start.10) | collective-permute-done | bytes 131104 | tf_op jit(solution)/shard_map/ppermute | solution.py:20
  117.5 3.3 %collective-permute-done.12.refs_2_.r2 = bf16[4,64,256]{2,1,0:T(8,128)(2,1)S(1)} collective-permute-done((bf16[4,64,256]{2,1,0:T(8,128)(2,1)S(1)}, bf16[4,64,256]{2,1,0:T(8,128)(2,1)S(1)}, u32[]{:S(2)}, u32[]{:S(2)}) %collective-permute-start.12) | collective-permute-done | bytes 131104 | tf_op jit(solution)/shard_map/ppermute | solution.py:20
  120.8 4.2 %collective-permute-done.13.refs_3_.r3 = bf16[4,64,256]{2,1,0:T(8,128)(2,1)S(1)} collective-permute-done((bf16[4,64,256]{2,1,0:T(8,128)(2,1)S(1)}, bf16[4,64,256]{2,1,0:T(8,128)(2,1)S(1)}, u32[]{:S(2)}, u32[]{:S(2)}) %collective-permute-start.13) | collective-permute-done | bytes 131104 | tf_op jit(solution)/shard_map/ppermute | solution.py:20
  126.1 30.0 %all_to_all.20 = bf16[64,112,128]{2,1,0:T(8,128)(2,1)S(1)} all-to-all(bf16[64,112,128]{2,1,0:T(8,128)(2,1)S(1)} %total.1.after_ref), channel_id=1, replica_groups={{0,32,64,96,1,33,65,97,2,34,66,98,3,35,67,99,4,36,68,100,5,37,69,101,6,..., dimensions={0} | all-to-all | bytes 3670016 | tf_op jit(solution)/shard_map/all_to_all | solution.py:692
  156.1 3.6 %collective-permute-start.14 = (bf16[28,256,128]{2,1,0:T(8,128)(2,1)S(1)}, bf16[28,256,128]{2,1,0:T(8,128)(2,1)S(1)}, u32[]{:S(2)}, u32[]{:S(2)}) collective-permute-start(bf16[28,256,128]{2,1,0:T(8,128)(2,1)S(1)} %bitcast.22), channel_id=1, source_target_pairs={{0,16},{16,0},{32,48},{48,32},{64,80},{80,64},{96,112},{112,96},{1... | collective-permute-start | bytes 5505032 | tf_op jit(solution)/shard_map/ppermute | solution.py:41
  160.2 5.0 %input_gradient.1.after1_ref = bf16[4,512,256]{2,1,0:T(8,128)(2,1)} custom-call(f32[4,512,256]{2,1,0:T(8,128)} %copy-done.1, bf16[4,64,256]{2,1,0:T(8,128)(2,1)} %copy-done.11, bf16[4,64,256]{2,1,0:T(8,128)(2,1)} %copy-done.12, bf16[4,64,256]{2,1,0:T(8,128)(2,1)} %copy-done.13, bf16[4,64,256]{2,1,0:T(8,128)(2,1)} %copy-done.14, ...), custom_call_target="tpu_custom_call" | custom-call | bytes 5242880 | tf_op jit(solution)/shard_map/input_gradient/pallas_call | solution.py:620
  165.2 3.4 %collect.1.after0_ref = bf16[8,512,256]{2,1,0:T(8,128)(2,1)} custom-call(s32[8]{0:T(128)} %fusion.4.place_ref, bf16[2,512,256]{2,1,0:T(8,128)(2,1)} %get-tuple-element.32.refs_13_.own_ref, bf16[2,512,256]{2,1,0:T(8,128)(2,1)} %copy-done.7, bf16[2,512,256]{2,1,0:T(8,128)(2,1)} %copy-done.6, bf16[2,512,256]{2,1,0:T(8,128)(2,1)} %copy-done.8, ...), custom_call_target="tpu_custom_call" | custom-call | bytes 4194304 | tf_op jit(solution)/shard_map/collect/pallas_call | solution.py:161
  170.3 3.1 %join.1 = f32[27,256,256]{2,1,0:T(8,128)} custom-call(s32[1]{0:T(128)} %bitcast.6.refs_2_.core_ref, bf16[28,256,128]{2,1,0:T(8,128)(2,1)S(1)} %bitcast.23, bf16[28,256,128]{2,1,0:T(8,128)(2,1)S(1)} %collective-permute-done.14.other_ref, bf16[8,512,256]{2,1,0:T(8,128)(2,1)S(1)} %copy-done.2, bf16[4,512,256]{2,1,0:T(8,128)(2,1)S(1)} %copy-done.5), custom_call_target="tpu_custom_call" | custom-call | tf_op jit(solution)/shard_map/join/pallas_call | solution.py:449
  (118 shorter events, 20.8 us)
Async XLA Ops:
  0.6 10.2 %copy-start.37 = (s32[4,512]{1,0:T(4,128)S(1)}, s32[4,512]{1,0:T(4,128)}, u32[]{:S(2)}) copy-start(s32[4,512]{1,0:T(4,128)} %param.7) | copy-start | bytes 24580
  4.0 26.4 %all-to-all-start = ((bf16[8,256,256]{2,1,0:T(8,128)(2,1)}), bf16[8,256,256]{2,1,0:T(8,128)(2,1)S(1)}, u32[]{:S(2)}, u32[]{:S(2)}) async-start(bf16[8,256,256]{2,1,0:T(8,128)(2,1)} %cut.2), calls=%async_computation | async-start | bytes 2097152 | tf_op jit(solution)/shard_map/all_to_all | solution.py:665
  15.3 9.0 %collective-permute-start = (bf16[4,64,256]{2,1,0:T(8,128)(2,1)}, bf16[4,64,256]{2,1,0:T(8,128)(2,1)S(1)}, u32[]{:S(2)}, u32[]{:S(2)}) collective-permute-start(bf16[4,64,256]{2,1,0:T(8,128)(2,1)} %get-tuple-element.29.l1.refs_5_), channel_id=1, source_target_pairs={{0,16},{16,32},{32,48},{48,64},{64,80},{80,96},{96,112},{112,0},{1... | collective-permute-start | bytes 393224 | tf_op jit(solution)/shard_map/ppermute | solution.py:20
  17.0 9.4 %collective-permute-start.1 = (bf16[4,64,256]{2,1,0:T(8,128)(2,1)}, bf16[4,64,256]{2,1,0:T(8,128)(2,1)S(1)}, u32[]{:S(2)}, u32[]{:S(2)}) collective-permute-start(bf16[4,64,256]{2,1,0:T(8,128)(2,1)} %get-tuple-element.28.l0.refs_4_), channel_id=1, source_target_pairs={{0,112},{16,0},{32,16},{48,32},{64,48},{80,64},{96,80},{112,96},{1... | collective-permute-start | bytes 393224 | tf_op jit(solution)/shard_map/ppermute | solution.py:20
  17.0 20.5 %collective-permute-start.2 = (bf16[4,64,256]{2,1,0:T(8,128)(2,1)}, bf16[4,64,256]{2,1,0:T(8,128)(2,1)S(1)}, u32[]{:S(2)}, u32[]{:S(2)}) collective-permute-start(bf16[4,64,256]{2,1,0:T(8,128)(2,1)} %get-tuple-element.31.l3.refs_7_), channel_id=1, source_target_pairs={{0,1},{1,2},{2,3},{3,4},{4,5},{5,6},{6,7},{7,8},{8,9},{9,10},{10,1... | collective-permute-start | bytes 393224 | tf_op jit(solution)/shard_map/ppermute | solution.py:20
  18.2 19.3 %collective-permute-start.3 = (bf16[4,64,256]{2,1,0:T(8,128)(2,1)}, bf16[4,64,256]{2,1,0:T(8,128)(2,1)S(1)}, u32[]{:S(2)}, u32[]{:S(2)}) collective-permute-start(bf16[4,64,256]{2,1,0:T(8,128)(2,1)} %get-tuple-element.30.l2.refs_6_), channel_id=1, source_target_pairs={{0,15},{1,0},{2,1},{3,2},{4,3},{5,4},{6,5},{7,6},{8,7},{9,8},{10,9... | collective-permute-start | bytes 393224 | tf_op jit(solution)/shard_map/ppermute | solution.py:20
  30.4 20.9 %all-to-all-start.1 = ((bf16[8,256,256]{2,1,0:T(8,128)(2,1)}), bf16[8,256,256]{2,1,0:T(8,128)(2,1)S(1)}, u32[]{:S(2)}, u32[]{:S(2)}) async-start(bf16[8,256,256]{2,1,0:T(8,128)(2,1)} %cut.3), calls=%async_computation.1 | async-start | bytes 2097152 | tf_op jit(solution)/shard_map/all_to_all | solution.py:665
  51.4 18.8 %collective-permute-start.4 = (bf16[2,512,256]{2,1,0:T(8,128)(2,1)}, bf16[2,512,256]{2,1,0:T(8,128)(2,1)S(1)}, u32[]{:S(2)}, u32[]{:S(2)}) collective-permute-start(bf16[2,512,256]{2,1,0:T(8,128)(2,1)} %get-tuple-element.36), channel_id=1, source_target_pairs={{0,32},{16,112},{32,64},{48,16},{64,96},{80,48},{96,0},{112,80},{1... | collective-permute-start | bytes 1572872 | tf_op jit(solution)/shard_map/ppermute | solution.py:37
  53.8 17.7 %collective-permute-start.5 = (bf16[2,512,256]{2,1,0:T(8,128)(2,1)}, bf16[2,512,256]{2,1,0:T(8,128)(2,1)S(1)}, u32[]{:S(2)}, u32[]{:S(2)}) collective-permute-start(bf16[2,512,256]{2,1,0:T(8,128)(2,1)} %get-tuple-element.37), channel_id=1, source_target_pairs={{0,32},{16,112},{32,64},{48,16},{64,96},{80,48},{96,0},{112,80},{1... | collective-permute-start | bytes 1572872 | tf_op jit(solution)/shard_map/ppermute | solution.py:37
  54.4 17.1 %collective-permute-start.6 = (bf16[2,512,256]{2,1,0:T(8,128)(2,1)}, bf16[2,512,256]{2,1,0:T(8,128)(2,1)S(1)}, u32[]{:S(2)}, u32[]{:S(2)}) collective-permute-start(bf16[2,512,256]{2,1,0:T(8,128)(2,1)} %get-tuple-element.38), channel_id=1, source_target_pairs={{0,96},{16,48},{32,0},{48,80},{64,32},{80,112},{96,64},{112,16},{1... | collective-permute-start | bytes 1572872 | tf_op jit(solution)/shard_map/ppermute | solution.py:37
  71.5 27.4 %copy-start.7 = (bf16[2,512,256]{2,1,0:T(8,128)(2,1)}, bf16[2,512,256]{2,1,0:T(8,128)(2,1)S(1)}, u32[]{:S(2)}) copy-start(bf16[2,512,256]{2,1,0:T(8,128)(2,1)S(1)} %get-tuple-element.41.near_ref) | copy-start | bytes 1572868
  71.5 14.6 %collective-permute-start.9 = (bf16[28,256,128]{2,1,0:T(8,128)(2,1)S(1)}, bf16[28,256,128]{2,1,0:T(8,128)(2,1)S(1)}, u32[]{:S(2)}, u32[]{:S(2)}) collective-permute-start(bf16[28,256,128]{2,1,0:T(8,128)(2,1)S(1)} %get-tuple-element.44), channel_id=1, source_target_pairs={{0,16},{16,0},{32,48},{48,32},{64,80},{80,64},{96,112},{112,96},{1... | collective-permute-start | bytes 5505032 | tf_op jit(solution)/shard_map/ppermute | solution.py:41
  74.3 11.9 %collective-permute-start.7 = (bf16[2,512,256]{2,1,0:T(8,128)(2,1)S(1)}, bf16[2,512,256]{2,1,0:T(8,128)(2,1)S(1)}, u32[]{:S(2)}, u32[]{:S(2)}) collective-permute-start(bf16[2,512,256]{2,1,0:T(8,128)(2,1)S(1)} %get-tuple-element.42), channel_id=1, source_target_pairs={{0,32},{16,112},{32,64},{48,16},{64,96},{80,48},{96,0},{112,80},{1... | collective-permute-start | bytes 1572872 | tf_op jit(solution)/shard_map/ppermute | solution.py:37
  86.2 13.8 %copy-start.6 = (bf16[2,512,256]{2,1,0:T(8,128)(2,1)}, bf16[2,512,256]{2,1,0:T(8,128)(2,1)S(1)}, u32[]{:S(2)}) copy-start(bf16[2,512,256]{2,1,0:T(8,128)(2,1)S(1)} %collective-permute-done.7.refs_0_.far_ref) | copy-start | bytes 1572868
  88.8 36.3 %all-to-all-start.2 = ((bf16[64,112,128]{2,1,0:T(8,128)(2,1)}), bf16[64,112,128]{2,1,0:T(8,128)(2,1)S(1)}, u32[]{:S(2)}, u32[]{:S(2)}) async-start(bf16[64,112,128]{2,1,0:T(8,128)(2,1)} %bitcast.21), calls=%async_computation.2 | async-start | bytes 3670016 | tf_op jit(solution)/shard_map/all_to_all | solution.py:692
  100.2 24.9 %collective-permute-start.8 = (bf16[4,512,256]{2,1,0:T(8,128)(2,1)S(1)}, bf16[4,512,256]{2,1,0:T(8,128)(2,1)S(1)}, u32[]{:S(2)}, u32[]{:S(2)}) collective-permute-start(bf16[4,512,256]{2,1,0:T(8,128)(2,1)S(1)} %pad_maximum_fusion), channel_id=1, source_target_pairs={{0,16},{16,0},{32,48},{48,32},{64,80},{80,64},{96,112},{112,96},{1... | collective-permute-start | bytes 3145736 | tf_op jit(solution)/shard_map/ppermute | solution.py:41
  101.4 14.5 %collective-permute-start.10 = (bf16[4,64,256]{2,1,0:T(8,128)(2,1)S(1)}, bf16[4,64,256]{2,1,0:T(8,128)(2,1)S(1)}, u32[]{:S(2)}, u32[]{:S(2)}) collective-permute-start(bf16[4,64,256]{2,1,0:T(8,128)(2,1)S(1)} %copy-done.36), channel_id=1, source_target_pairs={{0,112},{16,0},{32,16},{48,32},{64,48},{80,64},{96,80},{112,96},{1... | collective-permute-start | bytes 393224 | tf_op jit(solution)/shard_map/ppermute | solution.py:20
  101.4 16.1 %collective-permute-start.11 = (bf16[4,64,256]{2,1,0:T(8,128)(2,1)S(1)}, bf16[4,64,256]{2,1,0:T(8,128)(2,1)S(1)}, u32[]{:S(2)}, u32[]{:S(2)}) collective-permute-start(bf16[4,64,256]{2,1,0:T(8,128)(2,1)S(1)} %copy-done.34), channel_id=1, source_target_pairs={{0,16},{16,32},{32,48},{48,64},{64,80},{80,96},{96,112},{112,0},{1... | collective-permute-start | bytes 393224 | tf_op jit(solution)/shard_map/ppermute | solution.py:20
  103.1 17.7 %collective-permute-start.12 = (bf16[4,64,256]{2,1,0:T(8,128)(2,1)S(1)}, bf16[4,64,256]{2,1,0:T(8,128)(2,1)S(1)}, u32[]{:S(2)}, u32[]{:S(2)}) collective-permute-start(bf16[4,64,256]{2,1,0:T(8,128)(2,1)S(1)} %copy-done.32), channel_id=1, source_target_pairs={{0,15},{1,0},{2,1},{3,2},{4,3},{5,4},{6,5},{7,6},{8,7},{9,8},{10,9... | collective-permute-start | bytes 393224 | tf_op jit(solution)/shard_map/ppermute | solution.py:20
  108.1 17.0 %collective-permute-start.13 = (bf16[4,64,256]{2,1,0:T(8,128)(2,1)S(1)}, bf16[4,64,256]{2,1,0:T(8,128)(2,1)S(1)}, u32[]{:S(2)}, u32[]{:S(2)}) collective-permute-start(bf16[4,64,256]{2,1,0:T(8,128)(2,1)S(1)} %get-tuple-element.50), channel_id=1, source_target_pairs={{0,1},{1,2},{2,3},{3,4},{4,5},{5,6},{6,7},{7,8},{8,9},{9,10},{10,1... | collective-permute-start | bytes 393224 | tf_op jit(solution)/shard_map/ppermute | solution.py:20
  115.9 9.5 %copy-start.11 = (bf16[4,64,256]{2,1,0:T(8,128)(2,1)}, bf16[4,64,256]{2,1,0:T(8,128)(2,1)S(1)}, u32[]{:S(2)}) copy-start(bf16[4,64,256]{2,1,0:T(8,128)(2,1)S(1)} %collective-permute-done.10.refs_0_.r0) | copy-start | bytes 393220
  117.5 7.9 %copy-start.12 = (bf16[4,64,256]{2,1,0:T(8,128)(2,1)}, bf16[4,64,256]{2,1,0:T(8,128)(2,1)S(1)}, u32[]{:S(2)}) copy-start(bf16[4,64,256]{2,1,0:T(8,128)(2,1)S(1)} %collective-permute-done.11.refs_1_.r1) | copy-start | bytes 393220
  126.1 30.0 %copy-start = (bf16[64,112,128]{2,1,0:T(8,128)(2,1)}, bf16[64,112,128]{2,1,0:T(8,128)(2,1)S(1)}, u32[]{:S(2)}) copy-start(bf16[64,112,128]{2,1,0:T(8,128)(2,1)S(1)} %total.1.after_ref) | copy-start | bytes 5505028
  156.1 12.6 %collective-permute-start.14 = (bf16[28,256,128]{2,1,0:T(8,128)(2,1)S(1)}, bf16[28,256,128]{2,1,0:T(8,128)(2,1)S(1)}, u32[]{:S(2)}, u32[]{:S(2)}) collective-permute-start(bf16[28,256,128]{2,1,0:T(8,128)(2,1)S(1)} %bitcast.22), channel_id=1, source_target_pairs={{0,16},{16,0},{32,48},{48,32},{64,80},{80,64},{96,112},{112,96},{1... | collective-permute-start | bytes 5505032 | tf_op jit(solution)/shard_map/ppermute | solution.py:41
  (34 other events, 103.2 us)

commit v3 on v2

--- a/solution.py
+++ b/solution.py
@@ -15,9 +15,22 @@
 norm_eps = 1e-06
 
 
-def from_behind(block, axis, distance):
-    count = lax.axis_size(axis)
-    return lax.ppermute(block, axis, [(i, (i + distance) % count) for i in range(count)])
+def from_behind(block, distance):
+    count = lax.axis_size("gx")
+    return lax.ppermute(block, "gx", [(i, (i + distance) % count) for i in range(count)])
+
+
+def column_pair(first, second):
+    rows, columns = lax.axis_size("gx"), lax.axis_size("gy")
+
+    def shifted(block, sign):
+        ways = []
+        for p in range(rows):
+            step = sign if p % 2 == 0 else -sign
+            ways += [(p * columns + q, p * columns + (q + step) % columns) for q in range(columns)]
+        return lax.ppermute(block, ("gx", "gy"), ways)
+
+    return shifted(first, 1), shifted(second, -1)
 
 
 def inner_neighbours(neighbours, listed):
@@ -86,7 +99,7 @@
     return 1.0 / (1.0 + jnp.exp(-u))
 
 
-def hidden_kernel(feat_ref, occ_ref, hid_ref, x0_ref, x1_ref, y0_ref, y1_ref):
+def hidden_kernel(core_ref, feat_ref, occ_ref, hid_ref, x0_ref, x1_ref, ya_ref, yb_ref):
     width = feat_ref.shape[2]
     values = feat_ref[0].astype(jnp.float32)
     u = values * norm_scale(values)
@@ -95,22 +108,24 @@
     cube = hidden.reshape(EDGE, EDGE, EDGE, width)
     x0_ref[0] = cube[0].reshape(FACE, width).astype(jnp.bfloat16)
     x1_ref[0] = cube[EDGE - 1].reshape(FACE, width).astype(jnp.bfloat16)
-    y0_ref[0] = cube[:, 0].reshape(FACE, width).astype(jnp.bfloat16)
-    y1_ref[0] = cube[:, EDGE - 1].reshape(FACE, width).astype(jnp.bfloat16)
-
-
-def hidden_call(features, occ_rows):
+    first = core_ref[0] == 0
+    low, high = cube[:, 0].reshape(FACE, width), cube[:, EDGE - 1].reshape(FACE, width)
+    ya_ref[0] = jnp.where(first, high, low).astype(jnp.bfloat16)
+    yb_ref[0] = jnp.where(first, low, high).astype(jnp.bfloat16)
+
+
+def hidden_call(core, features, occ_rows):
     listed, _, width = features.shape
     layer = jax.ShapeDtypeStruct((listed, FACE, width), jnp.bfloat16)
     return pl.pallas_call(
         hidden_kernel,
         grid=(listed,),
-        in_specs=[by_brick((V, width)), by_brick((1, V))],
+        in_specs=[smem(), by_brick((V, width)), by_brick((1, V))],
         out_specs=[by_brick((V, width))] + [by_brick((FACE, width))] * 4,
         out_shape=[jax.ShapeDtypeStruct((listed, V, width), jnp.bfloat16)] + [layer] * 4,
-        compiler_params=params(56),
+        compiler_params=params(16),
         name="hidden",
-    )(features, occ_rows)
+    )(core, features, occ_rows)
 
 
 def hold_kernel(*refs):
@@ -130,24 +145,6 @@
     )(*blocks, *after)
 
 
-def cut_kernel(blocks_ref, *refs):
-    refs[-1][...] = blocks_ref[...]
-
-
-def cut_call(blocks, part, parts, after):
-    count, rows, width = blocks.shape
-    shape = (count, rows // parts, width)
-    return pl.pallas_call(
-        cut_kernel,
-        grid=(count // 2,),
-        in_specs=[pl.BlockSpec((2,) + shape[1:], lambda i: (i, part, 0))] + glance(after),
-        out_specs=pl.BlockSpec((2,) + shape[1:], lambda i: (i, 0, 0)),
-        out_shape=jax.ShapeDtypeStruct(shape, blocks.dtype),
-        compiler_params=params(56),
-        name="cut",
-    )(blocks, *after)
-
-
 def collect_kernel(
     place_ref, own_ref, near_ref, far_ref, back_ref, mate_ref, after_ref, out_ref
 ):
@@ -164,7 +161,7 @@
         in_specs=[smem()] + [whole(own.shape)] * 4 + [whole(mate.shape)] + glance([after]),
         out_specs=whole(shape),
         out_shape=jax.ShapeDtypeStruct(shape, mate.dtype),
-        compiler_params=params(56),
+        compiler_params=params(20),
         cost_estimate=pl.CostEstimate(
             flops=0, bytes_accessed=4 * shape[0] * shape[1] * shape[2], transcendentals=0
         ),
@@ -181,16 +178,24 @@
     return lax.broadcasted_iota(jnp.int32, shape, len(shape) - 2)
 
 
-def extended_brick(s, near_ref, hid_ref, own, far, store):
+def extended_brick(s, near_ref, core_ref, hid_ref, own, far, store):
     listed, _, width = hid_ref.shape
 
     def flag(condition):
         return jnp.where(condition, 1.0, 0.0).astype(jnp.float32)
 
+    first = core_ref[0] == 0
+
     def face(f):
         n = near_ref[s, f]
-        here = own[f ^ 1][jnp.minimum(n, listed - 1)].astype(jnp.float32)
-        there = far[f][jnp.clip(n - listed, 0, listed - 1)].astype(jnp.float32)
+        at_here, at_there = jnp.minimum(n, listed - 1), jnp.clip(n - listed, 0, listed - 1)
+        if f < 2:
+            here, there = own[f ^ 1][at_here], far[f][at_there]
+        else:
+            a, b = (2, 3) if f == 2 else (3, 2)
+            here = jnp.where(first, own[a][at_here], own[b][at_here])
+            there = jnp.where(first, far[a][at_there], far[b][at_there])
+        here, there = here.astype(jnp.float32), there.astype(jnp.float32)
         value = here * flag(n < listed) + there * flag((n >= listed) & (n < 2 * listed))
         return value.reshape(EDGE, EDGE, width)
 
@@ -234,7 +239,7 @@
 
 
 def forward_kernel(
-    near_ref, place_ref, hid_ref, l0, l1, l2, l3, r0, r1, r2, r3, feat_ref, occ_ref, w_ref,
+    near_ref, place_ref, core_ref, hid_ref, l0, l1, l2, l3, r0, r1, r2, r3, feat_ref, occ_ref, w_ref,
     *refs,
 ):
     outs, even_ref, odd_ref = refs[:-2], refs[-2], refs[-1]
@@ -250,7 +255,7 @@
         even_ref[0, k] = everything
         odd_ref[0, k] = inner
 
-    extended_brick(s, near_ref, hid_ref, (l0, l1, l2, l3), (r0, r1, r2, r3), store)
+    extended_brick(s, near_ref, core_ref, hid_ref, (l0, l1, l2, l3), (r0, r1, r2, r3), store)
     total = jnp.zeros((V, width), jnp.float32)
     for i in range(3):
         for j in range(3):
@@ -274,13 +279,15 @@
     ]
 
 
-def forward_call(neighbours, place, hidden, layers, remote, features, occ_rows, weight9, slots):
+def forward_call(
+    neighbours, place, core, hidden, layers, remote, features, occ_rows, weight9, slots
+):
     listed, _, width = features.shape
     layer = whole((listed, FACE, width))
     return pl.pallas_call(
         forward_kernel,
         grid=(listed,),
-        in_specs=[smem(), smem(), whole((listed, V, width))]
+        in_specs=[smem(), smem(), smem(), whole((listed, V, width))]
         + [layer] * 8
         + [by_brick((V, width)), by_brick((1, V)), whole(weight9.shape)],
         out_specs=[whole((2, V, width))] * (slots // 2),
@@ -293,7 +300,7 @@
             transcendentals=0,
         ),
         name="forward",
-    )(neighbours, place, hidden, *layers, *remote, features, occ_rows, weight9)
+    )(neighbours, place, core, hidden, *layers, *remote, features, occ_rows, weight9)
 
 
 def weight_kernel(
@@ -326,7 +333,7 @@
                 even_ref[s, k] = everything
                 odd_ref[s, k] = inner
 
-            extended_brick(s, near_ref, hid_ref, (l0, l1, l2, l3), (r0, r1, r2, r3), store)
+            extended_brick(s, near_ref, core_ref, hid_ref, (l0, l1, l2, l3), (r0, r1, r2, r3), store)
 
         for s in range(listed):
             for t in range(len(came)):
@@ -458,8 +465,8 @@
 
 
 def data_kernel(
-    near_ref, buf_ref, occ_ref, w_ref,
-    grad_ref, s0_ref, s1_ref, s2_ref, s3_ref,
+    near_ref, core_ref, buf_ref, occ_ref, w_ref,
+    grad_ref, s0_ref, s1_ref, sa_ref, sb_ref,
     wide_ref, rows_ref, depth_ref, kept_ref,
 ):
     s = pl.program_id(0)
@@ -517,7 +524,6 @@
 
     @pl.when(last)
     def _():
-        sends = (s0_ref, s1_ref, s2_ref, s3_ref)
         for side in range(2):
             total = jnp.zeros((listed, EDGE + 2, EDGE, width), jnp.float32)
             for i in range(3):
@@ -545,6 +551,7 @@
                         ]
                     grad_ref[n] += jnp.concatenate([rows_ref[half] for half in halves], axis=1)
 
+        leaving = []
         for f in range(4):
             sums = [jnp.zeros((FACE, width), jnp.float32) for _ in range(listed)]
             for h in range(listed):
@@ -559,8 +566,13 @@
                 def _():
                     add_face(grad_ref, n, f, piece)
 
-            for t in range(listed):
-                sends[f][t] = sums[t].astype(jnp.bfloat16)
+            leaving.append(sums)
+        first = core_ref[0] == 0
+        for t in range(listed):
+            s0_ref[t] = leaving[0][t].astype(jnp.bfloat16)
+            s1_ref[t] = leaving[1][t].astype(jnp.bfloat16)
+            sa_ref[t] = jnp.where(first, leaving[3][t], leaving[2][t]).astype(jnp.bfloat16)
+            sb_ref[t] = jnp.where(first, leaving[2][t], leaving[3][t]).astype(jnp.bfloat16)
 
 
 def add_face(ref, n, f, piece):
@@ -574,13 +586,13 @@
             ref[n, start : start + EDGE] += piece[a * EDGE : (a + 1) * EDGE]
 
 
-def data_call(neighbours, grad_in, occ_rows, weight):
+def data_call(neighbours, core, grad_in, occ_rows, weight):
     listed, _, width = grad_in.shape
     layer = jax.ShapeDtypeStruct((listed, FACE, width), jnp.bfloat16)
     return pl.pallas_call(
         data_kernel,
         grid=(listed,),
-        in_specs=[smem(), by_brick((V, width)), by_brick((1, V)), whole(weight.shape)],
+        in_specs=[smem(), smem(), by_brick((V, width)), by_brick((1, V)), whole(weight.shape)],
         out_specs=[whole((listed, V, width))] + [whole(layer.shape)] * 4,
         out_shape=[jax.ShapeDtypeStruct((listed, V, width), jnp.float32)] + [layer] * 4,
         scratch_shapes=[
@@ -596,16 +608,18 @@
             transcendentals=0,
         ),
         name="data_gradient",
-    )(neighbours, grad_in, occ_rows, weight)
+    )(neighbours, core, grad_in, occ_rows, weight)
 
 
 def finish_kernel(
-    grad_ref, r0, r1, r2, r3, feat_ref, occ_ref, buf_ref, after_ref, out_ref, work_ref
+    core_ref, grad_ref, r0, r1, ra, rb, feat_ref, occ_ref, buf_ref, after_ref, out_ref, work_ref
 ):
     width = feat_ref.shape[2]
     work_ref[...] = grad_ref[...]
-    for f, far in enumerate((r0, r1, r2, r3)):
-        add_face(work_ref, 0, f, far[0].astype(jnp.float32))
+    first = core_ref[0] == 0
+    came = (r0[0], r1[0], jnp.where(first, rb[0], ra[0]), jnp.where(first, ra[0], rb[0]))
+    for f, far in enumerate(came):
+        add_face(work_ref, 0, f, far.astype(jnp.float32))
     values = feat_ref[0].astype(jnp.float32)
     r = norm_scale(values)
     u = values * r
@@ -615,12 +629,12 @@
     out_ref[0] = (buf_ref[0].astype(jnp.float32) + pulled).astype(jnp.bfloat16)
 
 
-def finish_call(grad, remote, features, occ_rows, grad_in, after):
+def finish_call(core, grad, remote, features, occ_rows, grad_in, after):
     listed, _, width = features.shape
     return pl.pallas_call(
         finish_kernel,
         grid=(listed,),
-        in_specs=[by_brick((V, width))]
+        in_specs=[smem(), by_brick((V, width))]
         + [by_brick((FACE, width))] * 4
         + [by_brick((V, width)), by_brick((1, V)), by_brick((V, width))]
         + glance([after]),
@@ -632,7 +646,7 @@
             flops=0, bytes_accessed=10 * listed * V * width, transcendentals=listed * V * width
         ),
         name="input_gradient",
-    )(grad, *remote, features, occ_rows, grad_in, after)
+    )(core, grad, *remote, features, occ_rows, grad_in, after)
 
 
 def body(features, occupancy, routes, neighbours, weight, cotangent):
@@ -654,19 +668,18 @@
     route = routes[:, 0]
     out_place = way_of(c) * (route // 2 - z) % depth * 2 + (route + c) % 2
 
-    hidden, *layers = hidden_call(features, occ_rows)
+    hidden, *layers = hidden_call(core, features, occ_rows)
     remote = [
-        from_behind(layers[1], "gx", 1),
-        from_behind(layers[0], "gx", -1),
-        from_behind(layers[3], "gy", 1),
-        from_behind(layers[2], "gy", -1),
+        from_behind(layers[1], 1),
+        from_behind(layers[0], -1),
+        *column_pair(layers[2], layers[3]),
     ]
     came = [
-        lax.all_to_all(cut_call(cotangent, part, 2, after), "gx", 0, 0, tiled=True)
-        for part, after in ((0, []), (1, remote[:2]))
+        lax.all_to_all(part, "gx", 0, 0, tiled=True)
+        for part in (cotangent[:, : V // 2], cotangent[:, V // 2 :])
     ]
     placed = forward_call(
-        neighbours, out_place, hidden, layers, remote, features, occ_rows,
+        neighbours, out_place, core, hidden, layers, remote, features, occ_rows,
         weight.reshape(9, 3 * width, width), slots,
     )
     scale = float(listed * rows * columns * V) ** (-0.5)
@@ -679,7 +692,7 @@
     near, far, back, theirs = hold_call([near, far, back, theirs], [mine])
     far = hop(far, 1)
 
-    grad, *sends = data_call(neighbours, grad_in, occ_rows, weight)
+    grad, *sends = data_call(neighbours, core, grad_in, occ_rows, weight)
 
     chip_sum = chip_call(mine, to_other_core(theirs), [far, grad])
     mate = to_other_core(jnp.stack([block[1] for block in (placed[0], near, far, back)]))
@@ -694,18 +707,16 @@
         )
 
     parts = all_to_all(chip_sum.reshape(columns * depth, -1, width // 2))
-    landed = [
-        from_behind(sends[1], "gx", 1),
-        from_behind(sends[0], "gx", -1),
-        from_behind(sends[3], "gy", 1),
-        from_behind(sends[2], "gy", -1),
+    arrived = [
+        from_behind(sends[0], -1), from_behind(sends[1], 1), *column_pair(sends[2], sends[3])
     ]
-    arrived = [landed[1], landed[0], landed[3], landed[2]]
-
-    pieces = total_call(parts, columns * depth, [*arrived, mate])
-    own = all_to_all(pieces).reshape(chip_sum.shape)
+
+    token = sum(block[0, :16, :128].astype(jnp.float32) for block in [*arrived, mate])
+    pieces = total_call(parts, columns * depth, [token])
+    own = all_to_all(pieces)
     owned_out = collect_call(from_place, placed[0], near, far, back, mate, pieces)
-    input_grad = finish_call(grad, arrived, features, occ_rows, grad_in, pieces)
+    input_grad = finish_call(core, grad, arrived, features, occ_rows, grad_in, pieces)
+    own = hold_call([own], [owned_out, input_grad])[0].reshape(chip_sum.shape)
     weight_grad = join_call(core, own, to_other_core(own), [owned_out, input_grad])
     return (owned_out, input_grad, weight_grad)
 

time: 174 us -> 164 us (0.943)
  blocking collectives: 30 us -> 0 us
  waiting for transfers between devices: 22.9 us -> 45.1 us
  Pallas kernels: 61.8 us -> 54.2 us
  starting transfers between devices: 47.1 us -> 52.2 us
    all_to_all x1 -> x0, blocking collectives: 30 us -> none  [all_to_all(): lax.all_to_all(pieces, ('gx', 'gy'), 0, 0, axis_index_groups=same_core, t...]
    all_to_all x1 -> x2, waiting for transfers between devices: 0.01 us -> 16.8 us  [all_to_all(): lax.all_to_all(pieces, ('gx', 'gy'), 0, 0, axis_index_groups=same_core, t...]
    pallas_call x5 -> x3, Pallas kernels: 26.8 us -> 17.5 us  [the longest x1 11.2 us: data_call(): pl.pallas_call(data_kernel, grid=(listed,), in_specs=[smem(), smem(), by_...]
    all_to_all x1 -> x2, starting transfers between devices: 9.14 us -> 15.2 us  [all_to_all(): lax.all_to_all(pieces, ('gx', 'gy'), 0, 0, axis_index_groups=same_core, t...]
    all_to_all x2, waiting for transfers between devices: 0.3 us -> 6.34 us  [body(): lax.all_to_all(part, 'gx', 0, 0, tiled=True)]
    ppermute x8, waiting for transfers between devices: 21.3 us -> 17.3 us  [the longest x4 12 us: from_behind(): lax.ppermute(block, 'gx', [(i, (i + distance) % count) for i in range(cou...]
    ppermute x3, waiting for transfers between devices: 0.01 us -> 3.42 us  [to_other_core(): lax.ppermute(block, 'gx', [(p, p ^ 1) for p in range(lax.axis_size('gx'))])]
    slice x0 -> x1, local copies, waits for them, and re-layouts: none -> 3.05 us  [body(): cotangent[:, V // 2:]]
  transfers between devices with their start and end apart: 18 -> 19, of which waited for: 8 -> 8; matrix products, arithmetic and copies ran while one was open for 3% -> 2% of each run, Pallas kernels for 31% -> 29%
where the time goes in v3:
time: 164 us; the launch traced here: 163 us
  Pallas kernels  54.2 us (33%)
  starting transfers between devices  52.2 us (32%)
  waiting for transfers between devices  45.1 us (28%)
  local copies, waits for them, and re-layouts  9.38 us (6%)
    all_to_all x2, waiting for transfers between devices, all_to_all(): lax.all_to_all(pieces, ('gx', 'gy'), 0, 0, axis_index_groups=same_core, t...  16.8 us
    all_to_all x2, starting transfers between devices, all_to_all(): lax.all_to_all(pieces, ('gx', 'gy'), 0, 0, axis_index_groups=same_core, t...  15.2 us
    pallas_call x1, Pallas kernels, weight_call(): pl.pallas_call(lambda *refs: weight_kernel(*refs, scale=scale), grid=(4,)...  14.8 us
    pallas_call x1, Pallas kernels, forward_call(): pl.pallas_call(forward_kernel, grid=(listed,), in_specs=[smem(), smem(),...  12.8 us
    ppermute x4, waiting for transfers between devices, from_behind(): lax.ppermute(block, 'gx', [(i, (i + distance) % count) for i in range(cou...  12 us
    all_to_all x2, starting transfers between devices, body(): lax.all_to_all(part, 'gx', 0, 0, tiled=True)  11.8 us
    pallas_call x1, Pallas kernels, data_call(): pl.pallas_call(data_kernel, grid=(listed,), in_specs=[smem(), smem(), by_...  11.2 us
    ppermute x4, starting transfers between devices, shifted(): return lax.ppermute(block, ('gx', 'gy'), ways)  9.84 us
  transfers between devices with their start and end apart: 19, of which 8 were waited for; matrix products, arithmetic and copies ran while one was open for 2% of the time, Pallas kernels for 29%

profile of v3, /device:TPU:1, one launch (start us, length us, event | category | flops | bytes accessed | tf_op | source)
XLA Modules:
  0.0 163.4 jit_solution(16245701393218859714)
XLA Ops:
  0.6 3.0 %fusion.10 = (bf16[8,256,256]{2,1,0:T(8,128)(2,1)}, bf16[8,256,256]{2,1,0:T(8,128)(2,1)}) fusion(bf16[8,512,256]{2,1,0:T(8,128)(2,1)} %param.11), kind=kLoop, calls=%fused_computation.35 | loop fusion | bytes 4194304 | tf_op jit(solution)/shard_map/slice | solution.py:679
  3.7 6.9 %all-to-all-start.1 = ((bf16[8,256,256]{2,1,0:T(8,128)(2,1)}), bf16[8,256,256]{2,1,0:T(8,128)(2,1)S(1)}, u32[]{:S(2)}, u32[]{:S(2)}) async-start(bf16[8,256,256]{2,1,0:T(8,128)(2,1)} %get-tuple-element.51), calls=%async_computation.1 | async-start | bytes 2097152 | tf_op jit(solution)/shard_map/all_to_all | solution.py:678
  12.9 1.7 %collective-permute-start = (bf16[4,64,256]{2,1,0:T(8,128)(2,1)S(1)}, bf16[4,64,256]{2,1,0:T(8,128)(2,1)S(1)}, u32[]{:S(2)}, u32[]{:S(2)}) collective-permute-start(bf16[4,64,256]{2,1,0:T(8,128)(2,1)S(1)} %get-tuple-element.29.l1.refs_5_), channel_id=1, source_target_pairs={{0,16},{16,32},{32,48},{48,64},{64,80},{80,96},{96,112},{112,0},{1... | collective-permute-start | bytes 393224 | tf_op jit(solution)/shard_map/ppermute | solution.py:20
  14.6 4.9 %collective-permute-start.2 = (bf16[4,64,256]{2,1,0:T(8,128)(2,1)S(1)}, bf16[4,64,256]{2,1,0:T(8,128)(2,1)S(1)}, u32[]{:S(2)}, u32[]{:S(2)}) collective-permute-start(bf16[4,64,256]{2,1,0:T(8,128)(2,1)S(1)} %get-tuple-element.30.l2.refs_6_), channel_id=1, source_target_pairs={{0,1},{1,2},{2,3},{3,4},{4,5},{5,6},{6,7},{7,8},{8,9},{9,10},{10,1... | collective-permute-start | bytes 393224 | tf_op jit(solution)/shard_map/ppermute | solution.py:31
  19.7 6.1 %all-to-all-done.1.refs_4_.refs_15_ = bf16[8,256,256]{2,1,0:T(8,128)(2,1)S(1)} async-done(((bf16[8,256,256]{2,1,0:T(8,128)(2,1)}), bf16[8,256,256]{2,1,0:T(8,128)(2,1)S(1)}, u32[]{:S(2)}, u32[]{:S(2)}) %all-to-all-start.1) | async-done | bytes 1048608 | tf_op jit(solution)/shard_map/all_to_all | solution.py:678
  25.8 4.8 %all-to-all-start = ((bf16[8,256,256]{2,1,0:T(8,128)(2,1)}), bf16[8,256,256]{2,1,0:T(8,128)(2,1)S(1)}, u32[]{:S(2)}, u32[]{:S(2)}) async-start(bf16[8,256,256]{2,1,0:T(8,128)(2,1)} %get-tuple-element.52), calls=%async_computation | async-start | bytes 2097152 | tf_op jit(solution)/shard_map/all_to_all | solution.py:678
  32.6 12.8 %forward.1 = (bf16[2,512,256]{2,1,0:T(8,128)(2,1)}, bf16[2,512,256]{2,1,0:T(8,128)(2,1)}, bf16[2,512,256]{2,1,0:T(8,128)(2,1)}, bf16[2,512,256]{2,1,0:T(8,128)(2,1)}) custom-call(s32[4,6]{1,0:T(4,128)} %or_select_fusion.near_ref.refs_0_, s32[4]{0:T(128)} %fusion.place_ref, s32[1]{0:T(128)} %bitcast.5.core_ref.refs_2_, bf16[4,512,256]{2,1,0:T(8,128)(2,1)} %copy-done.18, ...), custom_call_target="tpu_custom_call" | custom-call | flops 7247757312 | bytes 10485760 | tf_op jit(solution)/shard_map/forward/pallas_call | solution.py:287
  45.8 2.5 %collective-permute-start.4 = (bf16[2,512,256]{2,1,0:T(8,128)(2,1)}, bf16[2,512,256]{2,1,0:T(8,128)(2,1)S(1)}, u32[]{:S(2)}, u32[]{:S(2)}) collective-permute-start(bf16[2,512,256]{2,1,0:T(8,128)(2,1)} %get-tuple-element.36), channel_id=1, source_target_pairs={{0,32},{16,112},{32,64},{48,16},{64,96},{80,48},{96,0},{112,80},{1... | collective-permute-start | bytes 1572872 | tf_op jit(solution)/shard_map/ppermute | solution.py:50
  49.9 14.8 %weight_gradient.1 = (f32[28,256,128]{2,1,0:T(8,128)S(1)}, bf16[28,256,128]{2,1,0:T(8,128)(2,1)S(1)}, bf16[4,512,256]{2,1,0:T(8,128)(2,1)S(1)}) custom-call(s32[4,6]{1,0:T(4,128)S(1)} %copy-done.16, s32[4,1]{1,0:T(4,128)S(1)} %copy.17.refs_1_, s32[1]{0:T(128)} %bitcast.5.core_ref.refs_2_, bf16[4,512,256]{2,1,0:T(8,128)(2,1)S(1)} %copy-done.19, ...), custom_call_target="tpu_custom_call" | custom-call | flops 7247757312 | bytes 10485760 | tf_op jit(solution)/shard_map/weight_gradient/pallas_call | solution.py:370
  66.0 2.7 %collective-permute-start.9 = (bf16[28,256,128]{2,1,0:T(8,128)(2,1)S(1)}, bf16[28,256,128]{2,1,0:T(8,128)(2,1)S(1)}, u32[]{:S(2)}, u32[]{:S(2)}) collective-permute-start(bf16[28,256,128]{2,1,0:T(8,128)(2,1)S(1)} %get-tuple-element.44), channel_id=1, source_target_pairs={{0,16},{16,0},{32,48},{48,32},{64,80},{80,64},{96,112},{112,96},{1... | collective-permute-start | bytes 5505032 | tf_op jit(solution)/shard_map/ppermute | solution.py:54
  69.4 11.2 %data_gradient.1 = (f32[4,512,256]{2,1,0:T(8,128)S(1)}, bf16[4,64,256]{2,1,0:T(8,128)(2,1)S(1)}, bf16[4,64,256]{2,1,0:T(8,128)(2,1)S(1)}, bf16[4,64,256]{2,1,0:T(8,128)(2,1)S(1)}, bf16[4,64,256]{2,1,0:T(8,128)(2,1)S(1)}) custom-call(s32[4,6]{1,0:T(4,128)S(1)} %copy-done.16, s32[1]{0:T(128)} %bitcast.5.core_ref.refs_2_, ...), custom_call_target="tpu_custom_call" | custom-call | flops 8053063680 | bytes 10485760 | tf_op jit(solution)/shard_map/data_gradient/pallas_call | solution.py:592
  80.7 2.1 %chip_sum.1 = bf16[28,256,128]{2,1,0:T(8,128)(2,1)} custom-call(f32[28,256,128]{2,1,0:T(8,128)S(1)} %get-tuple-element.40.refs_4_.mine_ref, bf16[28,256,128]{2,1,0:T(8,128)(2,1)S(1)} %collective-permute-done.9.theirs_ref, bf16[2,512,256]{2,1,0:T(8,128)(2,1)S(1)} %collective-permute-done.7.refs_0_.far_ref, f32[4,512,256]{2,1,0:T(8,128)S(1)} %get-tuple-element.46.refs_1_.grad_ref), custom_call_target="tpu_custom_call" | custom-call | tf_op jit(solution)/shard_map/chip_sum/pallas_call | solution.py:405
  82.8 9.4 %all-to-all-start.2 = ((bf16[64,112,128]{2,1,0:T(8,128)(2,1)}), bf16[64,112,128]{2,1,0:T(8,128)(2,1)S(1)}, u32[]{:S(2)}, u32[]{:S(2)}) async-start(bf16[64,112,128]{2,1,0:T(8,128)(2,1)} %bitcast.7), calls=%async_computation.2 | async-start | bytes 3670016 | tf_op jit(solution)/shard_map/all_to_all | solution.py:705
  95.4 1.7 %collective-permute-start.11 = (bf16[4,64,256]{2,1,0:T(8,128)(2,1)S(1)}, bf16[4,64,256]{2,1,0:T(8,128)(2,1)S(1)}, u32[]{:S(2)}, u32[]{:S(2)}) collective-permute-start(bf16[4,64,256]{2,1,0:T(8,128)(2,1)S(1)} %copy-done.39), channel_id=1, source_target_pairs={{0,16},{16,32},{32,48},{48,64},{64,80},{80,96},{96,112},{112,0},{1... | collective-permute-start | bytes 393224 | tf_op jit(solution)/shard_map/ppermute | solution.py:20
  97.1 4.9 %collective-permute-start.12 = (bf16[4,64,256]{2,1,0:T(8,128)(2,1)S(1)}, bf16[4,64,256]{2,1,0:T(8,128)(2,1)S(1)}, u32[]{:S(2)}, u32[]{:S(2)}) collective-permute-start(bf16[4,64,256]{2,1,0:T(8,128)(2,1)S(1)} %copy-done.37), channel_id=1, source_target_pairs={{0,1},{1,2},{2,3},{3,4},{4,5},{5,6},{6,7},{7,8},{8,9},{9,10},{10,1... | collective-permute-start | bytes 393224 | tf_op jit(solution)/shard_map/ppermute | solution.py:31
  102.0 12.0 %collective-permute-done.10.r0 = bf16[4,64,256]{2,1,0:T(8,128)(2,1)S(1)} collective-permute-done((bf16[4,64,256]{2,1,0:T(8,128)(2,1)S(1)}, bf16[4,64,256]{2,1,0:T(8,128)(2,1)S(1)}, u32[]{:S(2)}, u32[]{:S(2)}) %collective-permute-start.10) | collective-permute-done | bytes 131104 | tf_op jit(solution)/shard_map/ppermute | solution.py:20
  115.4 3.9 %collective-permute-done.13.rb = bf16[4,64,256]{2,1,0:T(8,128)(2,1)S(1)} collective-permute-done((bf16[4,64,256]{2,1,0:T(8,128)(2,1)S(1)}, bf16[4,64,256]{2,1,0:T(8,128)(2,1)S(1)}, u32[]{:S(2)}, u32[]{:S(2)}) %collective-permute-start.13) | collective-permute-done | bytes 131104 | tf_op jit(solution)/shard_map/ppermute | solution.py:31
  121.6 5.8 %all-to-all-start.3 = ((bf16[64,112,128]{2,1,0:T(8,128)(2,1)}), bf16[64,112,128]{2,1,0:T(8,128)(2,1)S(1)}, u32[]{:S(2)}, u32[]{:S(2)}) async-start(bf16[64,112,128]{2,1,0:T(8,128)(2,1)} %total.1.after_ref), calls=%async_computation.3 | async-start | bytes 3670016 | tf_op jit(solution)/shard_map/all_to_all | solution.py:705
  127.4 5.2 %input_gradient.1.refs_2_.after1_ref = bf16[4,512,256]{2,1,0:T(8,128)(2,1)} custom-call(s32[1]{0:T(128)} %bitcast.5.core_ref.refs_2_, f32[4,512,256]{2,1,0:T(8,128)} %copy-done.3, bf16[4,64,256]{2,1,0:T(8,128)(2,1)} %copy-done.42, bf16[4,64,256]{2,1,0:T(8,128)(2,1)} %copy-done.43, bf16[4,64,256]{2,1,0:T(8,128)(2,1)} %copy-done.44, ...), custom_call_target="tpu_custom_call" | custom-call | bytes 5242880 | tf_op jit(solution)/shard_map/input_gradient/pallas_call | solution.py:634
  132.6 2.2 %collect.1.refs_1_.after0_ref = bf16[8,512,256]{2,1,0:T(8,128)(2,1)} custom-call(s32[8]{0:T(128)S(1)} %fusion.4.place_ref, bf16[2,512,256]{2,1,0:T(8,128)(2,1)S(1)} %copy-done.10, bf16[2,512,256]{2,1,0:T(8,128)(2,1)S(1)} %copy-done.6, bf16[2,512,256]{2,1,0:T(8,128)(2,1)S(1)} %collective-permute-done.7.refs_0_.far_ref, bf16[2,512,256]{2,1,0:T(8,128)(2,1)S(1)} %copy-done.8, ...), custom_call_target="tpu_custom_call" | custom-call | bytes 4194304 | tf_op jit(solution)/shard_map/collect/pallas_call | solution.py:158
  134.9 16.8 %all-to-all-done.3.refs_0_ = bf16[64,112,128]{2,1,0:T(8,128)(2,1)S(1)} async-done(((bf16[64,112,128]{2,1,0:T(8,128)(2,1)}), bf16[64,112,128]{2,1,0:T(8,128)(2,1)S(1)}, u32[]{:S(2)}, u32[]{:S(2)}) %all-to-all-start.3) | async-done | bytes 1835040 | tf_op jit(solution)/shard_map/all_to_all | solution.py:705
  153.3 3.5 %collective-permute-start.14 = (bf16[28,256,128]{2,1,0:T(8,128)(2,1)S(1)}, bf16[28,256,128]{2,1,0:T(8,128)(2,1)S(1)}, u32[]{:S(2)}, u32[]{:S(2)}) collective-permute-start(bf16[28,256,128]{2,1,0:T(8,128)(2,1)S(1)} %bitcast.23), channel_id=1, source_target_pairs={{0,16},{16,0},{32,48},{48,32},{64,80},{80,64},{96,112},{112,96},{1... | collective-permute-start | bytes 5505032 | tf_op jit(solution)/shard_map/ppermute | solution.py:54
  156.8 3.4 %collective-permute-done.14.other_ref = bf16[28,256,128]{2,1,0:T(8,128)(2,1)S(1)} collective-permute-done((bf16[28,256,128]{2,1,0:T(8,128)(2,1)S(1)}, bf16[28,256,128]{2,1,0:T(8,128)(2,1)S(1)}, u32[]{:S(2)}, u32[]{:S(2)}) %collective-permute-start.14) | collective-permute-done | bytes 1835040 | tf_op jit(solution)/shard_map/ppermute | solution.py:54
  160.3 3.1 %join.1 = f32[27,256,256]{2,1,0:T(8,128)} custom-call(s32[1]{0:T(128)} %bitcast.5.core_ref.refs_2_, bf16[28,256,128]{2,1,0:T(8,128)(2,1)S(1)} %bitcast.24, bf16[28,256,128]{2,1,0:T(8,128)(2,1)S(1)} %collective-permute-done.14.other_ref, bf16[8,512,256]{2,1,0:T(8,128)(2,1)S(1)} %copy-done.1, bf16[4,512,256]{2,1,0:T(8,128)(2,1)S(1)} %copy-done.2), custom_call_target="tpu_custom_call" | custom-call | tf_op jit(solution)/shard_map/join/pallas_call | solution.py:456
  (138 shorter events, 16.5 us)
Async XLA Ops:
  3.7 22.1 %all-to-all-start.1 = ((bf16[8,256,256]{2,1,0:T(8,128)(2,1)}), bf16[8,256,256]{2,1,0:T(8,128)(2,1)S(1)}, u32[]{:S(2)}, u32[]{:S(2)}) async-start(bf16[8,256,256]{2,1,0:T(8,128)(2,1)} %get-tuple-element.51), calls=%async_computation.1 | async-start | bytes 2097152 | tf_op jit(solution)/shard_map/all_to_all | solution.py:678
  10.6 20.0 %copy-start.48 = (s32[4,6]{1,0:T(4,128)S(1)}, s32[4,6]{1,0:T(4,128)}, u32[]{:S(2)}) copy-start(s32[4,6]{1,0:T(4,128)} %param.9) | copy-start | bytes 292
  10.6 20.5 %copy-start.47 = (s32[4,1]{0,1:T(1,128)S(1)}, s32[4,1]{0,1:T(1,128)}, u32[]{:S(2)}) copy-start(s32[4,1]{0,1:T(1,128)} %param.8) | copy-start | bytes 52
  10.7 21.2 %copy-start.14 = (s32[4,1,512]{2,1,0:T(1,128)}, s32[4,1,512]{2,1,0:T(1,128)S(1)}, u32[]{:S(2)}) copy-start(s32[4,1,512]{2,1,0:T(1,128)S(1)} %reshape.32.occ_ref.refs_12_) | copy-start | bytes 24580
  12.8 19.1 %copy-start.26 = (bf16[4,64,256]{2,1,0:T(8,128)(2,1)}, bf16[4,64,256]{2,1,0:T(8,128)(2,1)S(1)}, u32[]{:S(2)}) copy-start(bf16[4,64,256]{2,1,0:T(8,128)(2,1)S(1)} %get-tuple-element.31.l3.refs_7_) | copy-start | bytes 393220
  12.8 19.0 %collective-permute-start.1 = (bf16[4,64,256]{2,1,0:T(8,128)(2,1)S(1)}, bf16[4,64,256]{2,1,0:T(8,128)(2,1)S(1)}, u32[]{:S(2)}, u32[]{:S(2)}) collective-permute-start(bf16[4,64,256]{2,1,0:T(8,128)(2,1)S(1)} %get-tuple-element.28.l0.refs_4_), channel_id=1, source_target_pairs={{0,112},{16,0},{32,16},{48,32},{64,48},{80,64},{96,80},{112,96},{1... | collective-permute-start | bytes 393224 | tf_op jit(solution)/shard_map/ppermute | solution.py:20
  12.9 18.9 %collective-permute-start = (bf16[4,64,256]{2,1,0:T(8,128)(2,1)S(1)}, bf16[4,64,256]{2,1,0:T(8,128)(2,1)S(1)}, u32[]{:S(2)}, u32[]{:S(2)}) collective-permute-start(bf16[4,64,256]{2,1,0:T(8,128)(2,1)S(1)} %get-tuple-element.29.l1.refs_5_), channel_id=1, source_target_pairs={{0,16},{16,32},{32,48},{48,64},{64,80},{80,96},{96,112},{112,0},{1... | collective-permute-start | bytes 393224 | tf_op jit(solution)/shard_map/ppermute | solution.py:20
  14.6 17.2 %collective-permute-start.2 = (bf16[4,64,256]{2,1,0:T(8,128)(2,1)S(1)}, bf16[4,64,256]{2,1,0:T(8,128)(2,1)S(1)}, u32[]{:S(2)}, u32[]{:S(2)}) collective-permute-start(bf16[4,64,256]{2,1,0:T(8,128)(2,1)S(1)} %get-tuple-element.30.l2.refs_6_), channel_id=1, source_target_pairs={{0,1},{1,2},{2,3},{3,4},{4,5},{5,6},{6,7},{7,8},{8,9},{9,10},{10,1... | collective-permute-start | bytes 393224 | tf_op jit(solution)/shard_map/ppermute | solution.py:31
  19.5 12.3 %collective-permute-start.3 = (bf16[4,64,256]{2,1,0:T(8,128)(2,1)S(1)}, bf16[4,64,256]{2,1,0:T(8,128)(2,1)S(1)}, u32[]{:S(2)}, u32[]{:S(2)}) collective-permute-start(bf16[4,64,256]{2,1,0:T(8,128)(2,1)S(1)} %get-tuple-element.31.l3.refs_7_), channel_id=1, source_target_pairs={{0,15},{1,0},{2,1},{3,2},{4,3},{5,4},{6,5},{7,6},{8,7},{9,8},{10,9... | collective-permute-start | bytes 393224 | tf_op jit(solution)/shard_map/ppermute | solution.py:31
  25.8 19.9 %all-to-all-start = ((bf16[8,256,256]{2,1,0:T(8,128)(2,1)}), bf16[8,256,256]{2,1,0:T(8,128)(2,1)S(1)}, u32[]{:S(2)}, u32[]{:S(2)}) async-start(bf16[8,256,256]{2,1,0:T(8,128)(2,1)} %get-tuple-element.52), calls=%async_computation | async-start | bytes 2097152 | tf_op jit(solution)/shard_map/all_to_all | solution.py:678
  45.8 18.9 %collective-permute-start.4 = (bf16[2,512,256]{2,1,0:T(8,128)(2,1)}, bf16[2,512,256]{2,1,0:T(8,128)(2,1)S(1)}, u32[]{:S(2)}, u32[]{:S(2)}) collective-permute-start(bf16[2,512,256]{2,1,0:T(8,128)(2,1)} %get-tuple-element.36), channel_id=1, source_target_pairs={{0,32},{16,112},{32,64},{48,16},{64,96},{80,48},{96,0},{112,80},{1... | collective-permute-start | bytes 1572872 | tf_op jit(solution)/shard_map/ppermute | solution.py:50
  48.3 17.7 %collective-permute-start.5 = (bf16[2,512,256]{2,1,0:T(8,128)(2,1)}, bf16[2,512,256]{2,1,0:T(8,128)(2,1)S(1)}, u32[]{:S(2)}, u32[]{:S(2)}) collective-permute-start(bf16[2,512,256]{2,1,0:T(8,128)(2,1)} %get-tuple-element.37), channel_id=1, source_target_pairs={{0,32},{16,112},{32,64},{48,16},{64,96},{80,48},{96,0},{112,80},{1... | collective-permute-start | bytes 1572872 | tf_op jit(solution)/shard_map/ppermute | solution.py:50
  48.9 17.1 %collective-permute-start.6 = (bf16[2,512,256]{2,1,0:T(8,128)(2,1)}, bf16[2,512,256]{2,1,0:T(8,128)(2,1)S(1)}, u32[]{:S(2)}, u32[]{:S(2)}) collective-permute-start(bf16[2,512,256]{2,1,0:T(8,128)(2,1)} %get-tuple-element.38), channel_id=1, source_target_pairs={{0,96},{16,48},{32,0},{48,80},{64,32},{80,112},{96,64},{112,16},{1... | collective-permute-start | bytes 1572872 | tf_op jit(solution)/shard_map/ppermute | solution.py:50
  66.0 27.1 %copy-start.5 = (bf16[2,512,256]{2,1,0:T(8,128)(2,1)}, bf16[2,512,256]{2,1,0:T(8,128)(2,1)S(1)}, u32[]{:S(2)}) copy-start(bf16[2,512,256]{2,1,0:T(8,128)(2,1)S(1)} %get-tuple-element.41.near_ref) | copy-start | bytes 1572868
  66.0 14.6 %collective-permute-start.9 = (bf16[28,256,128]{2,1,0:T(8,128)(2,1)S(1)}, bf16[28,256,128]{2,1,0:T(8,128)(2,1)S(1)}, u32[]{:S(2)}, u32[]{:S(2)}) collective-permute-start(bf16[28,256,128]{2,1,0:T(8,128)(2,1)S(1)} %get-tuple-element.44), channel_id=1, source_target_pairs={{0,16},{16,0},{32,48},{48,32},{64,80},{80,64},{96,112},{112,96},{1... | collective-permute-start | bytes 5505032 | tf_op jit(solution)/shard_map/ppermute | solution.py:54
  68.7 12.0 %collective-permute-start.7 = (bf16[2,512,256]{2,1,0:T(8,128)(2,1)S(1)}, bf16[2,512,256]{2,1,0:T(8,128)(2,1)S(1)}, u32[]{:S(2)}, u32[]{:S(2)}) collective-permute-start(bf16[2,512,256]{2,1,0:T(8,128)(2,1)S(1)} %get-tuple-element.42), channel_id=1, source_target_pairs={{0,32},{16,112},{32,64},{48,16},{64,96},{80,48},{96,0},{112,80},{1... | collective-permute-start | bytes 1572872 | tf_op jit(solution)/shard_map/ppermute | solution.py:50
  82.8 37.2 %all-to-all-start.2 = ((bf16[64,112,128]{2,1,0:T(8,128)(2,1)}), bf16[64,112,128]{2,1,0:T(8,128)(2,1)S(1)}, u32[]{:S(2)}, u32[]{:S(2)}) async-start(bf16[64,112,128]{2,1,0:T(8,128)(2,1)} %bitcast.7), calls=%async_computation.2 | async-start | bytes 3670016 | tf_op jit(solution)/shard_map/all_to_all | solution.py:705
  94.4 24.9 %collective-permute-start.8 = (bf16[4,512,256]{2,1,0:T(8,128)(2,1)S(1)}, bf16[4,512,256]{2,1,0:T(8,128)(2,1)S(1)}, u32[]{:S(2)}, u32[]{:S(2)}) collective-permute-start(bf16[4,512,256]{2,1,0:T(8,128)(2,1)S(1)} %pad_maximum_fusion), channel_id=1, source_target_pairs={{0,16},{16,0},{32,48},{48,32},{64,80},{80,64},{96,112},{112,96},{1... | collective-permute-start | bytes 3145736 | tf_op jit(solution)/shard_map/ppermute | solution.py:54
  95.4 18.6 %collective-permute-start.10 = (bf16[4,64,256]{2,1,0:T(8,128)(2,1)S(1)}, bf16[4,64,256]{2,1,0:T(8,128)(2,1)S(1)}, u32[]{:S(2)}, u32[]{:S(2)}) collective-permute-start(bf16[4,64,256]{2,1,0:T(8,128)(2,1)S(1)} %copy-done.41), channel_id=1, source_target_pairs={{0,112},{16,0},{32,16},{48,32},{64,48},{80,64},{96,80},{112,96},{1... | collective-permute-start | bytes 393224 | tf_op jit(solution)/shard_map/ppermute | solution.py:20
  95.4 18.6 %collective-permute-start.11 = (bf16[4,64,256]{2,1,0:T(8,128)(2,1)S(1)}, bf16[4,64,256]{2,1,0:T(8,128)(2,1)S(1)}, u32[]{:S(2)}, u32[]{:S(2)}) collective-permute-start(bf16[4,64,256]{2,1,0:T(8,128)(2,1)S(1)} %copy-done.39), channel_id=1, source_target_pairs={{0,16},{16,32},{32,48},{48,64},{64,80},{80,96},{96,112},{112,0},{1... | collective-permute-start | bytes 393224 | tf_op jit(solution)/shard_map/ppermute | solution.py:20
  97.1 18.3 %collective-permute-start.12 = (bf16[4,64,256]{2,1,0:T(8,128)(2,1)S(1)}, bf16[4,64,256]{2,1,0:T(8,128)(2,1)S(1)}, u32[]{:S(2)}, u32[]{:S(2)}) collective-permute-start(bf16[4,64,256]{2,1,0:T(8,128)(2,1)S(1)} %copy-done.37), channel_id=1, source_target_pairs={{0,1},{1,2},{2,3},{3,4},{4,5},{5,6},{6,7},{7,8},{8,9},{9,10},{10,1... | collective-permute-start | bytes 393224 | tf_op jit(solution)/shard_map/ppermute | solution.py:31
  102.0 17.3 %collective-permute-start.13 = (bf16[4,64,256]{2,1,0:T(8,128)(2,1)S(1)}, bf16[4,64,256]{2,1,0:T(8,128)(2,1)S(1)}, u32[]{:S(2)}, u32[]{:S(2)}) collective-permute-start(bf16[4,64,256]{2,1,0:T(8,128)(2,1)S(1)} %get-tuple-element.50), channel_id=1, source_target_pairs={{0,15},{1,0},{2,1},{3,2},{4,3},{5,4},{6,5},{7,6},{8,7},{9,8},{10,9... | collective-permute-start | bytes 393224 | tf_op jit(solution)/shard_map/ppermute | solution.py:31
  121.6 30.1 %all-to-all-start.3 = ((bf16[64,112,128]{2,1,0:T(8,128)(2,1)}), bf16[64,112,128]{2,1,0:T(8,128)(2,1)S(1)}, u32[]{:S(2)}, u32[]{:S(2)}) async-start(bf16[64,112,128]{2,1,0:T(8,128)(2,1)} %total.1.after_ref), calls=%async_computation.3 | async-start | bytes 3670016 | tf_op jit(solution)/shard_map/all_to_all | solution.py:705
  153.3 7.0 %collective-permute-start.14 = (bf16[28,256,128]{2,1,0:T(8,128)(2,1)S(1)}, bf16[28,256,128]{2,1,0:T(8,128)(2,1)S(1)}, u32[]{:S(2)}, u32[]{:S(2)}) collective-permute-start(bf16[28,256,128]{2,1,0:T(8,128)(2,1)S(1)} %bitcast.23), channel_id=1, source_target_pairs={{0,16},{16,0},{32,48},{48,32},{64,80},{80,64},{96,112},{112,96},{1... | collective-permute-start | bytes 5505032 | tf_op jit(solution)/shard_map/ppermute | solution.py:54
  (44 other events, 217.9 us)

commit v4 on v3

--- a/solution.py
+++ b/solution.py
@@ -433,35 +433,33 @@
     )(parts, *after)
 
 
-def join_kernel(core_ref, own_ref, other_ref, after0_ref, after1_ref, out_ref):
-    half = own_ref.shape[2]
-    first = core_ref[0] == 0
-
-    def put(low_ref, high_ref):
-        out_ref[:, :, :half] = low_ref[...].astype(jnp.float32)
-        out_ref[:, :, half:] = high_ref[...].astype(jnp.float32)
-
-    @pl.when(first)
-    def _():
-        put(own_ref, other_ref)
-
-    @pl.when(jnp.logical_not(first))
-    def _():
-        put(other_ref, own_ref)
-
-
-def join_call(core, own, other, after):
-    _, width, half = own.shape
-    block = pl.BlockSpec((9, width, half), lambda t: (t, 0, 0))
-    return pl.pallas_call(
-        join_kernel,
-        grid=(TAPS // 9,),
-        in_specs=[smem(), block, block] + glance(after),
-        out_specs=pl.BlockSpec((9, width, 2 * half), lambda t: (t, 0, 0)),
+def half_kernel(core_ref, block_ref, *refs):
+    refs[-1][...] = block_ref[...].astype(jnp.float32)
+
+
+def half_call(core, block, is_other, base):
+    _, width, half = block.shape
+
+    def place(t, core_ref):
+        return t, 0, (1 - core_ref[0] if is_other else core_ref[0])
+
+    return pl.pallas_call(
+        half_kernel,
+        grid_spec=pltpu.PrefetchScalarGridSpec(
+            num_scalar_prefetch=1,
+            grid=(TAPS // 9,),
+            in_specs=[pl.BlockSpec((9, width, half), lambda t, core_ref: (t, 0, 0))]
+            + [anywhere()] * len(base),
+            out_specs=pl.BlockSpec((9, width, half), place),
+        ),
         out_shape=jax.ShapeDtypeStruct((TAPS, width, 2 * half), jnp.float32),
+        input_output_aliases={2: 0} if base else {},
         compiler_params=params(16),
-        name="join",
-    )(core, own, other, *after)
+        cost_estimate=pl.CostEstimate(
+            flops=0, bytes_accessed=6 * TAPS * width * half, transcendentals=0
+        ),
+        name="half",
+    )(core, block, *base)
 
 
 def data_kernel(
@@ -716,8 +714,10 @@
     own = all_to_all(pieces)
     owned_out = collect_call(from_place, placed[0], near, far, back, mate, pieces)
     input_grad = finish_call(core, grad, arrived, features, occ_rows, grad_in, pieces)
-    own = hold_call([own], [owned_out, input_grad])[0].reshape(chip_sum.shape)
-    weight_grad = join_call(core, own, to_other_core(own), [owned_out, input_grad])
+    token = sum(block[0, :16, :128].astype(jnp.float32) for block in (owned_out, input_grad))
+    own = hold_call([own], [token])[0].reshape(chip_sum.shape)
+    weight_grad = half_call(core, own, False, [])
+    weight_grad = half_call(core, to_other_core(own), True, [weight_grad])
     return (owned_out, input_grad, weight_grad)
 
 

time: 164 us -> 162 us (0.988)
  waiting for transfers between devices: 45.1 us -> 43.2 us
    ppermute x3, waiting for transfers between devices: 3.42 us -> 1.24 us  [to_other_core(): lax.ppermute(block, 'gx', [(p, p ^ 1) for p in range(lax.axis_size('gx'))])]
    pallas_call x1 -> x2, Pallas kernels: 3.15 us -> 4.36 us  [half_call(): pl.pallas_call(half_kernel, grid_spec=pltpu.PrefetchScalarGridSpec(num_sc...]
    unnamed x99 -> x85, local copies, waits for them, and re-layouts: 4.15 us -> 3.51 us
  transfers between devices with their start and end apart: 19 -> 19, of which waited for: 8 -> 8; matrix products, arithmetic and copies ran while one was open for 2% -> 2% of each run, Pallas kernels for 29% -> 31%
where the time goes in v4:
time: 162 us; the launch traced here: 161 us
  Pallas kernels  55.5 us (34%)
  starting transfers between devices  51.9 us (32%)
  waiting for transfers between devices  43.2 us (27%)
  local copies, waits for them, and re-layouts  7.75 us (5%)
  other arithmetic  2.01 us (1%)
    all_to_all x2, waiting for transfers between devices, all_to_all(): lax.all_to_all(pieces, ('gx', 'gy'), 0, 0, axis_index_groups=same_core, t...  16.3 us
    pallas_call x1, Pallas kernels, weight_call(): pl.pallas_call(lambda *refs: weight_kernel(*refs, scale=scale), grid=(4,)...  14.8 us
    all_to_all x2, starting transfers between devices, all_to_all(): lax.all_to_all(pieces, ('gx', 'gy'), 0, 0, axis_index_groups=same_core, t...  14.8 us
    pallas_call x1, Pallas kernels, forward_call(): pl.pallas_call(forward_kernel, grid=(listed,), in_specs=[smem(), smem(),...  12.8 us
    ppermute x4, waiting for transfers between devices, from_behind(): lax.ppermute(block, 'gx', [(i, (i + distance) % count) for i in range(cou...  12.8 us
    all_to_all x2, starting transfers between devices, body(): lax.all_to_all(part, 'gx', 0, 0, tiled=True)  11.8 us
    pallas_call x1, Pallas kernels, data_call(): pl.pallas_call(data_kernel, grid=(listed,), in_specs=[smem(), smem(), by_...  11.3 us
    ppermute x4, starting transfers between devices, shifted(): return lax.ppermute(block, ('gx', 'gy'), ways)  9.84 us
  transfers between devices with their start and end apart: 19, of which 8 were waited for; matrix products, arithmetic and copies ran while one was open for 2% of the time, Pallas kernels for 31%

profile of v4, /device:TPU:1, one launch (start us, length us, event | category | flops | bytes accessed | tf_op | source)
XLA Modules:
  0.0 161.5 jit_solution(2272737261353288384)
XLA Ops:
  0.6 3.0 %fusion.10 = (bf16[8,256,256]{2,1,0:T(8,128)(2,1)}, bf16[8,256,256]{2,1,0:T(8,128)(2,1)}) fusion(bf16[8,512,256]{2,1,0:T(8,128)(2,1)} %param.11), kind=kLoop, calls=%fused_computation.36 | loop fusion | bytes 4194304 | tf_op jit(solution)/shard_map/slice | solution.py:677
  3.7 6.9 %all-to-all-start.1 = ((bf16[8,256,256]{2,1,0:T(8,128)(2,1)}), bf16[8,256,256]{2,1,0:T(8,128)(2,1)S(1)}, u32[]{:S(2)}, u32[]{:S(2)}) async-start(bf16[8,256,256]{2,1,0:T(8,128)(2,1)} %get-tuple-element.51), calls=%async_computation.1 | async-start | bytes 2097152 | tf_op jit(solution)/shard_map/all_to_all | solution.py:676
  12.9 1.7 %collective-permute-start = (bf16[4,64,256]{2,1,0:T(8,128)(2,1)S(1)}, bf16[4,64,256]{2,1,0:T(8,128)(2,1)S(1)}, u32[]{:S(2)}, u32[]{:S(2)}) collective-permute-start(bf16[4,64,256]{2,1,0:T(8,128)(2,1)S(1)} %get-tuple-element.29.l1.refs_5_), channel_id=1, source_target_pairs={{0,16},{16,32},{32,48},{48,64},{64,80},{80,96},{96,112},{112,0},{1... | collective-permute-start | bytes 393224 | tf_op jit(solution)/shard_map/ppermute | solution.py:20
  14.6 4.9 %collective-permute-start.2 = (bf16[4,64,256]{2,1,0:T(8,128)(2,1)S(1)}, bf16[4,64,256]{2,1,0:T(8,128)(2,1)S(1)}, u32[]{:S(2)}, u32[]{:S(2)}) collective-permute-start(bf16[4,64,256]{2,1,0:T(8,128)(2,1)S(1)} %get-tuple-element.30.l2.refs_6_), channel_id=1, source_target_pairs={{0,1},{1,2},{2,3},{3,4},{4,5},{5,6},{6,7},{7,8},{8,9},{9,10},{10,1... | collective-permute-start | bytes 393224 | tf_op jit(solution)/shard_map/ppermute | solution.py:31
  19.7 6.1 %all-to-all-done.1.refs_4_.refs_15_ = bf16[8,256,256]{2,1,0:T(8,128)(2,1)S(1)} async-done(((bf16[8,256,256]{2,1,0:T(8,128)(2,1)}), bf16[8,256,256]{2,1,0:T(8,128)(2,1)S(1)}, u32[]{:S(2)}, u32[]{:S(2)}) %all-to-all-start.1) | async-done | bytes 1048608 | tf_op jit(solution)/shard_map/all_to_all | solution.py:676
  25.8 4.8 %all-to-all-start = ((bf16[8,256,256]{2,1,0:T(8,128)(2,1)}), bf16[8,256,256]{2,1,0:T(8,128)(2,1)S(1)}, u32[]{:S(2)}, u32[]{:S(2)}) async-start(bf16[8,256,256]{2,1,0:T(8,128)(2,1)} %get-tuple-element.52), calls=%async_computation | async-start | bytes 2097152 | tf_op jit(solution)/shard_map/all_to_all | solution.py:676
  32.6 12.8 %forward.1 = (bf16[2,512,256]{2,1,0:T(8,128)(2,1)}, bf16[2,512,256]{2,1,0:T(8,128)(2,1)}, bf16[2,512,256]{2,1,0:T(8,128)(2,1)}, bf16[2,512,256]{2,1,0:T(8,128)(2,1)}) custom-call(s32[4,6]{1,0:T(4,128)} %or_select_fusion.near_ref.refs_0_, s32[4]{0:T(128)} %fusion.place_ref, s32[1]{0:T(128)} %bitcast.5.core_ref.refs_2_, bf16[4,512,256]{2,1,0:T(8,128)(2,1)} %copy-done.11, ...), custom_call_target="tpu_custom_call" | custom-call | flops 7247757312 | bytes 10485760 | tf_op jit(solution)/shard_map/forward/pallas_call | solution.py:287
  45.8 2.6 %collective-permute-start.4 = (bf16[2,512,256]{2,1,0:T(8,128)(2,1)}, bf16[2,512,256]{2,1,0:T(8,128)(2,1)S(1)}, u32[]{:S(2)}, u32[]{:S(2)}) collective-permute-start(bf16[2,512,256]{2,1,0:T(8,128)(2,1)} %get-tuple-element.36), channel_id=1, source_target_pairs={{0,32},{16,112},{32,64},{48,16},{64,96},{80,48},{96,0},{112,80},{1... | collective-permute-start | bytes 1572872 | tf_op jit(solution)/shard_map/ppermute | solution.py:50
  49.9 14.8 %weight_gradient.1 = (f32[28,256,128]{2,1,0:T(8,128)S(1)}, bf16[28,256,128]{2,1,0:T(8,128)(2,1)S(1)}, bf16[4,512,256]{2,1,0:T(8,128)(2,1)S(1)}) custom-call(s32[4,6]{1,0:T(4,128)S(1)} %copy-done.9, s32[4,1]{1,0:T(4,128)S(1)} %copy.18.refs_1_, s32[1]{0:T(128)} %bitcast.5.core_ref.refs_2_, bf16[4,512,256]{2,1,0:T(8,128)(2,1)S(1)} %copy-done.12, ...), custom_call_target="tpu_custom_call" | custom-call | flops 7247757312 | bytes 10485760 | tf_op jit(solution)/shard_map/weight_gradient/pallas_call | solution.py:370
  66.0 2.5 %collective-permute-start.9 = (bf16[28,256,128]{2,1,0:T(8,128)(2,1)S(1)}, bf16[28,256,128]{2,1,0:T(8,128)(2,1)S(1)}, u32[]{:S(2)}, u32[]{:S(2)}) collective-permute-start(bf16[28,256,128]{2,1,0:T(8,128)(2,1)S(1)} %get-tuple-element.44), channel_id=1, source_target_pairs={{0,16},{16,0},{32,48},{48,32},{64,80},{80,64},{96,112},{112,96},{1... | collective-permute-start | bytes 5505032 | tf_op jit(solution)/shard_map/ppermute | solution.py:54
  69.3 11.3 %data_gradient.1 = (f32[4,512,256]{2,1,0:T(8,128)S(1)}, bf16[4,64,256]{2,1,0:T(8,128)(2,1)S(1)}, bf16[4,64,256]{2,1,0:T(8,128)(2,1)S(1)}, bf16[4,64,256]{2,1,0:T(8,128)(2,1)S(1)}, bf16[4,64,256]{2,1,0:T(8,128)(2,1)S(1)}) custom-call(s32[4,6]{1,0:T(4,128)S(1)} %copy-done.9, s32[1]{0:T(128)} %bitcast.5.core_ref.refs_2_, ...), custom_call_target="tpu_custom_call" | custom-call | flops 8053063680 | bytes 10485760 | tf_op jit(solution)/shard_map/data_gradient/pallas_call | solution.py:590
  80.7 2.1 %chip_sum.1 = bf16[28,256,128]{2,1,0:T(8,128)(2,1)} custom-call(f32[28,256,128]{2,1,0:T(8,128)S(1)} %get-tuple-element.40.refs_4_.mine_ref, bf16[28,256,128]{2,1,0:T(8,128)(2,1)S(1)} %collective-permute-done.9.theirs_ref, bf16[2,512,256]{2,1,0:T(8,128)(2,1)S(1)} %collective-permute-done.7.refs_0_.far_ref, f32[4,512,256]{2,1,0:T(8,128)S(1)} %get-tuple-element.46.refs_1_.grad_ref), custom_call_target="tpu_custom_call" | custom-call | tf_op jit(solution)/shard_map/chip_sum/pallas_call | solution.py:405
  82.8 9.0 %all-to-all-start.2 = ((bf16[64,112,128]{2,1,0:T(8,128)(2,1)}), bf16[64,112,128]{2,1,0:T(8,128)(2,1)S(1)}, u32[]{:S(2)}, u32[]{:S(2)}) async-start(bf16[64,112,128]{2,1,0:T(8,128)(2,1)} %bitcast.7), calls=%async_computation.2 | async-start | bytes 3670016 | tf_op jit(solution)/shard_map/all_to_all | solution.py:703
  94.2 1.7 %collective-permute-start.11 = (bf16[4,64,256]{2,1,0:T(8,128)(2,1)S(1)}, bf16[4,64,256]{2,1,0:T(8,128)(2,1)S(1)}, u32[]{:S(2)}, u32[]{:S(2)}) collective-permute-start(bf16[4,64,256]{2,1,0:T(8,128)(2,1)S(1)} %copy-done.32), channel_id=1, source_target_pairs={{0,16},{16,32},{32,48},{48,64},{64,80},{80,96},{96,112},{112,0},{1... | collective-permute-start | bytes 393224 | tf_op jit(solution)/shard_map/ppermute | solution.py:20
  95.9 4.9 %collective-permute-start.12 = (bf16[4,64,256]{2,1,0:T(8,128)(2,1)S(1)}, bf16[4,64,256]{2,1,0:T(8,128)(2,1)S(1)}, u32[]{:S(2)}, u32[]{:S(2)}) collective-permute-start(bf16[4,64,256]{2,1,0:T(8,128)(2,1)S(1)} %copy-done.30), channel_id=1, source_target_pairs={{0,1},{1,2},{2,3},{3,4},{4,5},{5,6},{6,7},{7,8},{8,9},{9,10},{10,1... | collective-permute-start | bytes 393224 | tf_op jit(solution)/shard_map/ppermute | solution.py:31
  100.8 12.8 %collective-permute-done.10.r0 = bf16[4,64,256]{2,1,0:T(8,128)(2,1)S(1)} collective-permute-done((bf16[4,64,256]{2,1,0:T(8,128)(2,1)S(1)}, bf16[4,64,256]{2,1,0:T(8,128)(2,1)S(1)}, u32[]{:S(2)}, u32[]{:S(2)}) %collective-permute-start.10) | collective-permute-done | bytes 131104 | tf_op jit(solution)/shard_map/ppermute | solution.py:20
  114.9 4.1 %collective-permute-done.13.rb = bf16[4,64,256]{2,1,0:T(8,128)(2,1)S(1)} collective-permute-done((bf16[4,64,256]{2,1,0:T(8,128)(2,1)S(1)}, bf16[4,64,256]{2,1,0:T(8,128)(2,1)S(1)}, u32[]{:S(2)}, u32[]{:S(2)}) %collective-permute-start.13) | collective-permute-done | bytes 131104 | tf_op jit(solution)/shard_map/ppermute | solution.py:31
  122.2 5.8 %all-to-all-start.3 = ((bf16[64,112,128]{2,1,0:T(8,128)(2,1)}), bf16[64,112,128]{2,1,0:T(8,128)(2,1)S(1)}, u32[]{:S(2)}, u32[]{:S(2)}) async-start(bf16[64,112,128]{2,1,0:T(8,128)(2,1)} %total.1.after_ref), calls=%async_computation.3 | async-start | bytes 3670016 | tf_op jit(solution)/shard_map/all_to_all | solution.py:703
  128.0 5.1 %input_gradient.1 = bf16[4,512,256]{2,1,0:T(8,128)(2,1)} custom-call(s32[1]{0:T(128)} %bitcast.5.core_ref.refs_2_, f32[4,512,256]{2,1,0:T(8,128)} %copy-done, bf16[4,64,256]{2,1,0:T(8,128)(2,1)} %copy-done.35, bf16[4,64,256]{2,1,0:T(8,128)(2,1)} %copy-done.36, bf16[4,64,256]{2,1,0:T(8,128)(2,1)} %copy-done.37, bf16[4,64,256]{2,1,0:T(8,128)(2,1)} %copy-done.38, ...), custom_call_target="tpu_custom_call" | custom-call | bytes 5242880 | tf_op jit(solution)/shard_map/input_gradient/pallas_call | solution.py:632
  133.2 2.2 %collect.1 = bf16[8,512,256]{2,1,0:T(8,128)(2,1)} custom-call(s32[8]{0:T(128)S(1)} %fusion.4.place_ref, bf16[2,512,256]{2,1,0:T(8,128)(2,1)S(1)} %copy-done.3, bf16[2,512,256]{2,1,0:T(8,128)(2,1)S(1)} %get-tuple-element.41.near_ref, bf16[2,512,256]{2,1,0:T(8,128)(2,1)S(1)} %collective-permute-done.7.refs_0_.far_ref, ...), custom_call_target="tpu_custom_call" | custom-call | bytes 4194304 | tf_op jit(solution)/shard_map/collect/pallas_call | solution.py:158
  136.0 16.3 %all-to-all-done.3.refs_0_ = bf16[64,112,128]{2,1,0:T(8,128)(2,1)S(1)} async-done(((bf16[64,112,128]{2,1,0:T(8,128)(2,1)}), bf16[64,112,128]{2,1,0:T(8,128)(2,1)S(1)}, u32[]{:S(2)}, u32[]{:S(2)}) %all-to-all-start.3) | async-done | bytes 1835040 | tf_op jit(solution)/shard_map/all_to_all | solution.py:703
  152.3 3.6 %collective-permute-start.14 = (bf16[28,256,128]{2,1,0:T(8,128)(2,1)S(1)}, bf16[28,256,128]{2,1,0:T(8,128)(2,1)S(1)}, u32[]{:S(2)}, u32[]{:S(2)}) collective-permute-start(bf16[28,256,128]{2,1,0:T(8,128)(2,1)S(1)} %bitcast.25), channel_id=1, source_target_pairs={{0,16},{16,0},{32,48},{48,32},{64,80},{80,64},{96,112},{112,96},{1... | collective-permute-start | bytes 5505032 | tf_op jit(solution)/shard_map/ppermute | solution.py:54
  155.9 2.2 %half.2.refs_0_ = f32[27,256,256]{2,1,0:T(8,128)} custom-call(s32[1]{0:T(128)} %bitcast.5.core_ref.refs_2_, bf16[28,256,128]{2,1,0:T(8,128)(2,1)S(1)} %bitcast.26), custom_call_target="tpu_custom_call" | custom-call | bytes 5308416 | tf_op jit(solution)/shard_map/half/pallas_call | solution.py:446
  159.3 2.2 %half.3 = f32[27,256,256]{2,1,0:T(8,128)} custom-call(s32[1]{0:T(128)} %bitcast.5.core_ref.refs_2_, bf16[28,256,128]{2,1,0:T(8,128)(2,1)S(1)} %collective-permute-done.14.block_ref, f32[27,256,256]{2,1,0:T(8,128)} %half.2.refs_0_), custom_call_target="tpu_custom_call", output_to_operand_aliasing={{}: (2, {})} | custom-call | bytes 5308416 | tf_op jit(solution)/shard_map/half/pallas_call | solution.py:446
  (126 shorter events, 16.8 us)
Async XLA Ops:
  3.7 22.1 %all-to-all-start.1 = ((bf16[8,256,256]{2,1,0:T(8,128)(2,1)}), bf16[8,256,256]{2,1,0:T(8,128)(2,1)S(1)}, u32[]{:S(2)}, u32[]{:S(2)}) async-start(bf16[8,256,256]{2,1,0:T(8,128)(2,1)} %get-tuple-element.51), calls=%async_computation.1 | async-start | bytes 2097152 | tf_op jit(solution)/shard_map/all_to_all | solution.py:676
  10.6 20.0 %copy-start.41 = (s32[4,6]{1,0:T(4,128)S(1)}, s32[4,6]{1,0:T(4,128)}, u32[]{:S(2)}) copy-start(s32[4,6]{1,0:T(4,128)} %param.9) | copy-start | bytes 292
  10.6 20.6 %copy-start.40 = (s32[4,1]{0,1:T(1,128)S(1)}, s32[4,1]{0,1:T(1,128)}, u32[]{:S(2)}) copy-start(s32[4,1]{0,1:T(1,128)} %param.8) | copy-start | bytes 52
  10.7 21.2 %copy-start.7 = (s32[4,1,512]{2,1,0:T(1,128)}, s32[4,1,512]{2,1,0:T(1,128)S(1)}, u32[]{:S(2)}) copy-start(s32[4,1,512]{2,1,0:T(1,128)S(1)} %reshape.35.occ_ref.refs_12_) | copy-start | bytes 24580
  12.8 19.1 %copy-start.17 = (bf16[4,64,256]{2,1,0:T(8,128)(2,1)}, bf16[4,64,256]{2,1,0:T(8,128)(2,1)S(1)}, u32[]{:S(2)}) copy-start(bf16[4,64,256]{2,1,0:T(8,128)(2,1)S(1)} %get-tuple-element.30.l2.refs_6_) | copy-start | bytes 393220
  12.8 19.1 %copy-start.19 = (bf16[4,64,256]{2,1,0:T(8,128)(2,1)}, bf16[4,64,256]{2,1,0:T(8,128)(2,1)S(1)}, u32[]{:S(2)}) copy-start(bf16[4,64,256]{2,1,0:T(8,128)(2,1)S(1)} %get-tuple-element.31.l3.refs_7_) | copy-start | bytes 393220
  12.8 19.0 %collective-permute-start.1 = (bf16[4,64,256]{2,1,0:T(8,128)(2,1)S(1)}, bf16[4,64,256]{2,1,0:T(8,128)(2,1)S(1)}, u32[]{:S(2)}, u32[]{:S(2)}) collective-permute-start(bf16[4,64,256]{2,1,0:T(8,128)(2,1)S(1)} %get-tuple-element.28.l0.refs_4_), channel_id=1, source_target_pairs={{0,112},{16,0},{32,16},{48,32},{64,48},{80,64},{96,80},{112,96},{1... | collective-permute-start | bytes 393224 | tf_op jit(solution)/shard_map/ppermute | solution.py:20
  12.9 18.9 %collective-permute-start = (bf16[4,64,256]{2,1,0:T(8,128)(2,1)S(1)}, bf16[4,64,256]{2,1,0:T(8,128)(2,1)S(1)}, u32[]{:S(2)}, u32[]{:S(2)}) collective-permute-start(bf16[4,64,256]{2,1,0:T(8,128)(2,1)S(1)} %get-tuple-element.29.l1.refs_5_), channel_id=1, source_target_pairs={{0,16},{16,32},{32,48},{48,64},{64,80},{80,96},{96,112},{112,0},{1... | collective-permute-start | bytes 393224 | tf_op jit(solution)/shard_map/ppermute | solution.py:20
  14.6 17.2 %collective-permute-start.2 = (bf16[4,64,256]{2,1,0:T(8,128)(2,1)S(1)}, bf16[4,64,256]{2,1,0:T(8,128)(2,1)S(1)}, u32[]{:S(2)}, u32[]{:S(2)}) collective-permute-start(bf16[4,64,256]{2,1,0:T(8,128)(2,1)S(1)} %get-tuple-element.30.l2.refs_6_), channel_id=1, source_target_pairs={{0,1},{1,2},{2,3},{3,4},{4,5},{5,6},{6,7},{7,8},{8,9},{9,10},{10,1... | collective-permute-start | bytes 393224 | tf_op jit(solution)/shard_map/ppermute | solution.py:31
  19.5 12.3 %collective-permute-start.3 = (bf16[4,64,256]{2,1,0:T(8,128)(2,1)S(1)}, bf16[4,64,256]{2,1,0:T(8,128)(2,1)S(1)}, u32[]{:S(2)}, u32[]{:S(2)}) collective-permute-start(bf16[4,64,256]{2,1,0:T(8,128)(2,1)S(1)} %get-tuple-element.31.l3.refs_7_), channel_id=1, source_target_pairs={{0,15},{1,0},{2,1},{3,2},{4,3},{5,4},{6,5},{7,6},{8,7},{9,8},{10,9... | collective-permute-start | bytes 393224 | tf_op jit(solution)/shard_map/ppermute | solution.py:31
  25.8 19.9 %all-to-all-start = ((bf16[8,256,256]{2,1,0:T(8,128)(2,1)}), bf16[8,256,256]{2,1,0:T(8,128)(2,1)S(1)}, u32[]{:S(2)}, u32[]{:S(2)}) async-start(bf16[8,256,256]{2,1,0:T(8,128)(2,1)} %get-tuple-element.52), calls=%async_computation | async-start | bytes 2097152 | tf_op jit(solution)/shard_map/all_to_all | solution.py:676
  45.8 19.0 %collective-permute-start.4 = (bf16[2,512,256]{2,1,0:T(8,128)(2,1)}, bf16[2,512,256]{2,1,0:T(8,128)(2,1)S(1)}, u32[]{:S(2)}, u32[]{:S(2)}) collective-permute-start(bf16[2,512,256]{2,1,0:T(8,128)(2,1)} %get-tuple-element.36), channel_id=1, source_target_pairs={{0,32},{16,112},{32,64},{48,16},{64,96},{80,48},{96,0},{112,80},{1... | collective-permute-start | bytes 1572872 | tf_op jit(solution)/shard_map/ppermute | solution.py:50
  48.3 17.7 %collective-permute-start.5 = (bf16[2,512,256]{2,1,0:T(8,128)(2,1)}, bf16[2,512,256]{2,1,0:T(8,128)(2,1)S(1)}, u32[]{:S(2)}, u32[]{:S(2)}) collective-permute-start(bf16[2,512,256]{2,1,0:T(8,128)(2,1)} %get-tuple-element.37), channel_id=1, source_target_pairs={{0,32},{16,112},{32,64},{48,16},{64,96},{80,48},{96,0},{112,80},{1... | collective-permute-start | bytes 1572872 | tf_op jit(solution)/shard_map/ppermute | solution.py:50
  48.9 17.1 %collective-permute-start.6 = (bf16[2,512,256]{2,1,0:T(8,128)(2,1)}, bf16[2,512,256]{2,1,0:T(8,128)(2,1)S(1)}, u32[]{:S(2)}, u32[]{:S(2)}) collective-permute-start(bf16[2,512,256]{2,1,0:T(8,128)(2,1)} %get-tuple-element.38), channel_id=1, source_target_pairs={{0,96},{16,48},{32,0},{48,80},{64,32},{80,112},{96,64},{112,16},{1... | collective-permute-start | bytes 1572872 | tf_op jit(solution)/shard_map/ppermute | solution.py:50
  66.0 14.7 %collective-permute-start.9 = (bf16[28,256,128]{2,1,0:T(8,128)(2,1)S(1)}, bf16[28,256,128]{2,1,0:T(8,128)(2,1)S(1)}, u32[]{:S(2)}, u32[]{:S(2)}) collective-permute-start(bf16[28,256,128]{2,1,0:T(8,128)(2,1)S(1)} %get-tuple-element.44), channel_id=1, source_target_pairs={{0,16},{16,0},{32,48},{48,32},{64,80},{80,64},{96,112},{112,96},{1... | collective-permute-start | bytes 5505032 | tf_op jit(solution)/shard_map/ppermute | solution.py:54
  68.6 12.1 %collective-permute-start.7 = (bf16[2,512,256]{2,1,0:T(8,128)(2,1)S(1)}, bf16[2,512,256]{2,1,0:T(8,128)(2,1)S(1)}, u32[]{:S(2)}, u32[]{:S(2)}) collective-permute-start(bf16[2,512,256]{2,1,0:T(8,128)(2,1)S(1)} %get-tuple-element.42), channel_id=1, source_target_pairs={{0,32},{16,112},{32,64},{48,16},{64,96},{80,48},{96,0},{112,80},{1... | collective-permute-start | bytes 1572872 | tf_op jit(solution)/shard_map/ppermute | solution.py:50
  82.8 37.8 %all-to-all-start.2 = ((bf16[64,112,128]{2,1,0:T(8,128)(2,1)}), bf16[64,112,128]{2,1,0:T(8,128)(2,1)S(1)}, u32[]{:S(2)}, u32[]{:S(2)}) async-start(bf16[64,112,128]{2,1,0:T(8,128)(2,1)} %bitcast.7), calls=%async_computation.2 | async-start | bytes 3670016 | tf_op jit(solution)/shard_map/all_to_all | solution.py:703
  93.1 25.9 %collective-permute-start.8 = (bf16[4,512,256]{2,1,0:T(8,128)(2,1)S(1)}, bf16[4,512,256]{2,1,0:T(8,128)(2,1)S(1)}, u32[]{:S(2)}, u32[]{:S(2)}) collective-permute-start(bf16[4,512,256]{2,1,0:T(8,128)(2,1)S(1)} %pad_maximum_fusion), channel_id=1, source_target_pairs={{0,16},{16,0},{32,48},{48,32},{64,80},{80,64},{96,112},{112,96},{1... | collective-permute-start | bytes 3145736 | tf_op jit(solution)/shard_map/ppermute | solution.py:54
  94.2 19.5 %collective-permute-start.10 = (bf16[4,64,256]{2,1,0:T(8,128)(2,1)S(1)}, bf16[4,64,256]{2,1,0:T(8,128)(2,1)S(1)}, u32[]{:S(2)}, u32[]{:S(2)}) collective-permute-start(bf16[4,64,256]{2,1,0:T(8,128)(2,1)S(1)} %copy-done.34), channel_id=1, source_target_pairs={{0,112},{16,0},{32,16},{48,32},{64,48},{80,64},{96,80},{112,96},{1... | collective-permute-start | bytes 393224 | tf_op jit(solution)/shard_map/ppermute | solution.py:20
  94.2 19.4 %collective-permute-start.11 = (bf16[4,64,256]{2,1,0:T(8,128)(2,1)S(1)}, bf16[4,64,256]{2,1,0:T(8,128)(2,1)S(1)}, u32[]{:S(2)}, u32[]{:S(2)}) collective-permute-start(bf16[4,64,256]{2,1,0:T(8,128)(2,1)S(1)} %copy-done.32), channel_id=1, source_target_pairs={{0,16},{16,32},{32,48},{48,64},{64,80},{80,96},{96,112},{112,0},{1... | collective-permute-start | bytes 393224 | tf_op jit(solution)/shard_map/ppermute | solution.py:20
  95.9 19.0 %collective-permute-start.12 = (bf16[4,64,256]{2,1,0:T(8,128)(2,1)S(1)}, bf16[4,64,256]{2,1,0:T(8,128)(2,1)S(1)}, u32[]{:S(2)}, u32[]{:S(2)}) collective-permute-start(bf16[4,64,256]{2,1,0:T(8,128)(2,1)S(1)} %copy-done.30), channel_id=1, source_target_pairs={{0,1},{1,2},{2,3},{3,4},{4,5},{5,6},{6,7},{7,8},{8,9},{9,10},{10,1... | collective-permute-start | bytes 393224 | tf_op jit(solution)/shard_map/ppermute | solution.py:31
  100.8 18.2 %collective-permute-start.13 = (bf16[4,64,256]{2,1,0:T(8,128)(2,1)S(1)}, bf16[4,64,256]{2,1,0:T(8,128)(2,1)S(1)}, u32[]{:S(2)}, u32[]{:S(2)}) collective-permute-start(bf16[4,64,256]{2,1,0:T(8,128)(2,1)S(1)} %get-tuple-element.50), channel_id=1, source_target_pairs={{0,15},{1,0},{2,1},{3,2},{4,3},{5,4},{6,5},{7,6},{8,7},{9,8},{10,9... | collective-permute-start | bytes 393224 | tf_op jit(solution)/shard_map/ppermute | solution.py:31
  122.2 30.1 %all-to-all-start.3 = ((bf16[64,112,128]{2,1,0:T(8,128)(2,1)}), bf16[64,112,128]{2,1,0:T(8,128)(2,1)S(1)}, u32[]{:S(2)}, u32[]{:S(2)}) async-start(bf16[64,112,128]{2,1,0:T(8,128)(2,1)} %total.1.after_ref), calls=%async_computation.3 | async-start | bytes 3670016 | tf_op jit(solution)/shard_map/all_to_all | solution.py:703
  152.3 7.0 %collective-permute-start.14 = (bf16[28,256,128]{2,1,0:T(8,128)(2,1)S(1)}, bf16[28,256,128]{2,1,0:T(8,128)(2,1)S(1)}, u32[]{:S(2)}, u32[]{:S(2)}) collective-permute-start(bf16[28,256,128]{2,1,0:T(8,128)(2,1)S(1)} %bitcast.25), channel_id=1, source_target_pairs={{0,16},{16,0},{32,48},{48,32},{64,80},{80,64},{96,112},{112,96},{1... | collective-permute-start | bytes 5505032 | tf_op jit(solution)/shard_map/ppermute | solution.py:54
  (37 other events, 158.1 us)

commit v5 on v4

--- a/solution.py
+++ b/solution.py
@@ -639,7 +639,7 @@
         out_specs=by_brick((V, width)),
         out_shape=jax.ShapeDtypeStruct((listed, V, width), jnp.bfloat16),
         scratch_shapes=[pltpu.VMEM((1, V, width), jnp.float32)],
-        compiler_params=params(56),
+        compiler_params=params(16),
         cost_estimate=pl.CostEstimate(
             flops=0, bytes_accessed=10 * listed * V * width, transcendentals=listed * V * width
         ),

time: 162 us -> 166 us (1.025)
  local copies, waits for them, and re-layouts: 7.75 us -> 17.4 us
  waiting for transfers between devices: 43.2 us -> 38.2 us
    unnamed x85 -> x111, local copies, waits for them, and re-layouts: 3.51 us -> 12.2 us
    all_to_all x2, waiting for transfers between devices: 16.3 us -> 12.2 us  [all_to_all(): lax.all_to_all(pieces, ('gx', 'gy'), 0, 0, axis_index_groups=same_core, t...]
  transfers between devices with their start and end apart: 19 -> 19, of which waited for: 8 -> 8; matrix products, arithmetic and copies ran while one was open for 2% -> 3% of each run, Pallas kernels for 31% -> 29%
where the time goes in v5:
time: 166 us; the launch traced here: 165 us
  Pallas kernels  54 us (33%)
  starting transfers between devices  52.1 us (31%)
  waiting for transfers between devices  38.2 us (23%)
  local copies, waits for them, and re-layouts  17.4 us (10%)
  other arithmetic  2.04 us (1%)
    all_to_all x2, starting transfers between devices, all_to_all(): lax.all_to_all(pieces, ('gx', 'gy'), 0, 0, axis_index_groups=same_core, t...  15.1 us
    pallas_call x1, Pallas kernels, weight_call(): pl.pallas_call(lambda *refs: weight_kernel(*refs, scale=scale), grid=(4,)...  14.8 us
    pallas_call x1, Pallas kernels, forward_call(): pl.pallas_call(forward_kernel, grid=(listed,), in_specs=[smem(), smem(),...  12.9 us
    all_to_all x2, waiting for transfers between devices, all_to_all(): lax.all_to_all(pieces, ('gx', 'gy'), 0, 0, axis_index_groups=same_core, t...  12.2 us
    unnamed x111, local copies, waits for them, and re-layouts  12.2 us
    ppermute x4, waiting for transfers between devices, from_behind(): lax.ppermute(block, 'gx', [(i, (i + distance) % count) for i in range(cou...  11.8 us
    all_to_all x2, starting transfers between devices, body(): lax.all_to_all(part, 'gx', 0, 0, tiled=True)  11.8 us
    pallas_call x1, Pallas kernels, data_call(): pl.pallas_call(data_kernel, grid=(listed,), in_specs=[smem(), smem(), by_...  11.2 us
  transfers between devices with their start and end apart: 19, of which 8 were waited for; matrix products, arithmetic and copies ran while one was open for 3% of the time, Pallas kernels for 29%

profile of v5, /device:TPU:1, one launch (start us, length us, event | category | flops | bytes accessed | tf_op | source)
XLA Modules:
  0.0 164.9 jit_solution(3330141200876460228)
XLA Ops:
  0.6 3.0 %fusion.10 = (bf16[8,256,256]{2,1,0:T(8,128)(2,1)}, bf16[8,256,256]{2,1,0:T(8,128)(2,1)}) fusion(bf16[8,512,256]{2,1,0:T(8,128)(2,1)} %param.11), kind=kLoop, calls=%fused_computation.36 | loop fusion | bytes 4194304 | tf_op jit(solution)/shard_map/slice | solution.py:677
  3.7 6.9 %all-to-all-start.1 = ((bf16[8,256,256]{2,1,0:T(8,128)(2,1)}), bf16[8,256,256]{2,1,0:T(8,128)(2,1)S(1)}, u32[]{:S(2)}, u32[]{:S(2)}) async-start(bf16[8,256,256]{2,1,0:T(8,128)(2,1)} %get-tuple-element.51), calls=%async_computation.1 | async-start | bytes 2097152 | tf_op jit(solution)/shard_map/all_to_all | solution.py:676
  12.9 1.7 %collective-permute-start = (bf16[4,64,256]{2,1,0:T(8,128)(2,1)S(1)}, bf16[4,64,256]{2,1,0:T(8,128)(2,1)S(1)}, u32[]{:S(2)}, u32[]{:S(2)}) collective-permute-start(bf16[4,64,256]{2,1,0:T(8,128)(2,1)S(1)} %get-tuple-element.29.l1.refs_5_), channel_id=1, source_target_pairs={{0,16},{16,32},{32,48},{48,64},{64,80},{80,96},{96,112},{112,0},{1... | collective-permute-start | bytes 393224 | tf_op jit(solution)/shard_map/ppermute | solution.py:20
  14.6 4.9 %collective-permute-start.2 = (bf16[4,64,256]{2,1,0:T(8,128)(2,1)S(1)}, bf16[4,64,256]{2,1,0:T(8,128)(2,1)S(1)}, u32[]{:S(2)}, u32[]{:S(2)}) collective-permute-start(bf16[4,64,256]{2,1,0:T(8,128)(2,1)S(1)} %get-tuple-element.30.l2.refs_6_), channel_id=1, source_target_pairs={{0,1},{1,2},{2,3},{3,4},{4,5},{5,6},{6,7},{7,8},{8,9},{9,10},{10,1... | collective-permute-start | bytes 393224 | tf_op jit(solution)/shard_map/ppermute | solution.py:31
  19.7 6.1 %all-to-all-done.1.refs_4_.refs_15_ = bf16[8,256,256]{2,1,0:T(8,128)(2,1)S(1)} async-done(((bf16[8,256,256]{2,1,0:T(8,128)(2,1)}), bf16[8,256,256]{2,1,0:T(8,128)(2,1)S(1)}, u32[]{:S(2)}, u32[]{:S(2)}) %all-to-all-start.1) | async-done | bytes 1048608 | tf_op jit(solution)/shard_map/all_to_all | solution.py:676
  25.8 4.8 %all-to-all-start = ((bf16[8,256,256]{2,1,0:T(8,128)(2,1)}), bf16[8,256,256]{2,1,0:T(8,128)(2,1)S(1)}, u32[]{:S(2)}, u32[]{:S(2)}) async-start(bf16[8,256,256]{2,1,0:T(8,128)(2,1)} %get-tuple-element.52), calls=%async_computation | async-start | bytes 2097152 | tf_op jit(solution)/shard_map/all_to_all | solution.py:676
  32.7 12.9 %forward.1 = (bf16[2,512,256]{2,1,0:T(8,128)(2,1)}, bf16[2,512,256]{2,1,0:T(8,128)(2,1)}, bf16[2,512,256]{2,1,0:T(8,128)(2,1)}, bf16[2,512,256]{2,1,0:T(8,128)(2,1)}) custom-call(s32[4,6]{1,0:T(4,128)} %or_select_fusion.near_ref.refs_0_, s32[4]{0:T(128)} %fusion.place_ref, s32[1]{0:T(128)} %bitcast.5.core_ref.refs_2_, bf16[4,512,256]{2,1,0:T(8,128)(2,1)} %copy-done.26, ...), custom_call_target="tpu_custom_call" | custom-call | flops 7247757312 | bytes 10485760 | tf_op jit(solution)/shard_map/forward/pallas_call | solution.py:287
  47.6 2.5 %collective-permute-start.4 = (bf16[2,512,256]{2,1,0:T(8,128)(2,1)}, bf16[2,512,256]{2,1,0:T(8,128)(2,1)S(1)}, u32[]{:S(2)}, u32[]{:S(2)}) collective-permute-start(bf16[2,512,256]{2,1,0:T(8,128)(2,1)} %get-tuple-element.36), channel_id=1, source_target_pairs={{0,32},{16,112},{32,64},{48,16},{64,96},{80,48},{96,0},{112,80},{1... | collective-permute-start | bytes 1572872 | tf_op jit(solution)/shard_map/ppermute | solution.py:50
  51.7 14.8 %weight_gradient.1 = (f32[28,256,128]{2,1,0:T(8,128)S(1)}, bf16[28,256,128]{2,1,0:T(8,128)(2,1)S(1)}, bf16[4,512,256]{2,1,0:T(8,128)(2,1)S(1)}) custom-call(s32[4,6]{1,0:T(4,128)S(1)} %copy-done.24, s32[4,1]{1,0:T(4,128)S(1)} %copy.18.refs_1_, s32[1]{0:T(128)} %bitcast.5.core_ref.refs_2_, bf16[4,512,256]{2,1,0:T(8,128)(2,1)S(1)} %copy-done.27, ...), custom_call_target="tpu_custom_call" | custom-call | flops 7247757312 | bytes 10485760 | tf_op jit(solution)/shard_map/weight_gradient/pallas_call | solution.py:370
  67.8 2.6 %collective-permute-start.9 = (bf16[28,256,128]{2,1,0:T(8,128)(2,1)S(1)}, bf16[28,256,128]{2,1,0:T(8,128)(2,1)S(1)}, u32[]{:S(2)}, u32[]{:S(2)}) collective-permute-start(bf16[28,256,128]{2,1,0:T(8,128)(2,1)S(1)} %get-tuple-element.44), channel_id=1, source_target_pairs={{0,16},{16,0},{32,48},{48,32},{64,80},{80,64},{96,112},{112,96},{1... | collective-permute-start | bytes 5505032 | tf_op jit(solution)/shard_map/ppermute | solution.py:54
  71.2 11.2 %data_gradient.1 = (f32[4,512,256]{2,1,0:T(8,128)S(1)}, bf16[4,64,256]{2,1,0:T(8,128)(2,1)S(1)}, bf16[4,64,256]{2,1,0:T(8,128)(2,1)S(1)}, bf16[4,64,256]{2,1,0:T(8,128)(2,1)S(1)}, bf16[4,64,256]{2,1,0:T(8,128)(2,1)S(1)}) custom-call(s32[4,6]{1,0:T(4,128)S(1)} %copy-done.24, s32[1]{0:T(128)} %bitcast.5.core_ref.refs_2_, ...), custom_call_target="tpu_custom_call" | custom-call | flops 8053063680 | bytes 10485760 | tf_op jit(solution)/shard_map/data_gradient/pallas_call | solution.py:590
  82.6 2.1 %chip_sum.1 = bf16[28,256,128]{2,1,0:T(8,128)(2,1)} custom-call(f32[28,256,128]{2,1,0:T(8,128)S(1)} %get-tuple-element.40.refs_4_.mine_ref, bf16[28,256,128]{2,1,0:T(8,128)(2,1)S(1)} %collective-permute-done.9.theirs_ref, bf16[2,512,256]{2,1,0:T(8,128)(2,1)S(1)} %collective-permute-done.7.refs_0_.far_ref, f32[4,512,256]{2,1,0:T(8,128)S(1)} %get-tuple-element.46.refs_1_.grad_ref), custom_call_target="tpu_custom_call" | custom-call | tf_op jit(solution)/shard_map/chip_sum/pallas_call | solution.py:405
  84.7 9.3 %all-to-all-start.2 = ((bf16[64,112,128]{2,1,0:T(8,128)(2,1)}), bf16[64,112,128]{2,1,0:T(8,128)(2,1)S(1)}, u32[]{:S(2)}, u32[]{:S(2)}) async-start(bf16[64,112,128]{2,1,0:T(8,128)(2,1)} %bitcast.7), calls=%async_computation.2 | async-start | bytes 3670016 | tf_op jit(solution)/shard_map/all_to_all | solution.py:703
  97.3 1.7 %collective-permute-start.11 = (bf16[4,64,256]{2,1,0:T(8,128)(2,1)S(1)}, bf16[4,64,256]{2,1,0:T(8,128)(2,1)S(1)}, u32[]{:S(2)}, u32[]{:S(2)}) collective-permute-start(bf16[4,64,256]{2,1,0:T(8,128)(2,1)S(1)} %copy-done.49), channel_id=1, source_target_pairs={{0,16},{16,32},{32,48},{48,64},{64,80},{80,96},{96,112},{112,0},{1... | collective-permute-start | bytes 393224 | tf_op jit(solution)/shard_map/ppermute | solution.py:20
  99.1 4.9 %collective-permute-start.12 = (bf16[4,64,256]{2,1,0:T(8,128)(2,1)S(1)}, bf16[4,64,256]{2,1,0:T(8,128)(2,1)S(1)}, u32[]{:S(2)}, u32[]{:S(2)}) collective-permute-start(bf16[4,64,256]{2,1,0:T(8,128)(2,1)S(1)} %copy-done.47), channel_id=1, source_target_pairs={{0,1},{1,2},{2,3},{3,4},{4,5},{5,6},{6,7},{7,8},{8,9},{9,10},{10,1... | collective-permute-start | bytes 393224 | tf_op jit(solution)/shard_map/ppermute | solution.py:31
  104.0 11.8 %collective-permute-done.10.r0 = bf16[4,64,256]{2,1,0:T(8,128)(2,1)S(1)} collective-permute-done((bf16[4,64,256]{2,1,0:T(8,128)(2,1)S(1)}, bf16[4,64,256]{2,1,0:T(8,128)(2,1)S(1)}, u32[]{:S(2)}, u32[]{:S(2)}) %collective-permute-start.10) | collective-permute-done | bytes 131104 | tf_op jit(solution)/shard_map/ppermute | solution.py:20
  117.1 4.1 %collective-permute-done.13.rb = bf16[4,64,256]{2,1,0:T(8,128)(2,1)S(1)} collective-permute-done((bf16[4,64,256]{2,1,0:T(8,128)(2,1)S(1)}, bf16[4,64,256]{2,1,0:T(8,128)(2,1)S(1)}, u32[]{:S(2)}, u32[]{:S(2)}) %collective-permute-start.13) | collective-permute-done | bytes 131104 | tf_op jit(solution)/shard_map/ppermute | solution.py:31
  125.6 5.8 %all-to-all-start.3 = ((bf16[64,112,128]{2,1,0:T(8,128)(2,1)}), bf16[64,112,128]{2,1,0:T(8,128)(2,1)S(1)}, u32[]{:S(2)}, u32[]{:S(2)}) async-start(bf16[64,112,128]{2,1,0:T(8,128)(2,1)} %total.1.after_ref), calls=%async_computation.3 | async-start | bytes 3670016 | tf_op jit(solution)/shard_map/all_to_all | solution.py:703
  137.1 3.7 %input_gradient.1 = bf16[4,512,256]{2,1,0:T(8,128)(2,1)} custom-call(s32[1]{0:T(128)} %bitcast.5.core_ref.refs_2_, f32[4,512,256]{2,1,0:T(8,128)S(1)} %copy-done.1, bf16[4,64,256]{2,1,0:T(8,128)(2,1)S(1)} %collective-permute-done.10.r0, bf16[4,64,256]{2,1,0:T(8,128)(2,1)S(1)} %copy-done.17, bf16[4,64,256]{2,1,0:T(8,128)(2,1)S(1)} %copy-done.19, ...), custom_call_target="tpu_custom_call" | custom-call | bytes 5242880 | tf_op jit(solution)/shard_map/input_gradient/pallas_call | solution.py:632
  140.8 2.2 %collect.1 = bf16[8,512,256]{2,1,0:T(8,128)(2,1)} custom-call(s32[8]{0:T(128)S(1)} %fusion.4.place_ref, bf16[2,512,256]{2,1,0:T(8,128)(2,1)S(1)} %copy-done.9, bf16[2,512,256]{2,1,0:T(8,128)(2,1)S(1)} %copy-done.5, bf16[2,512,256]{2,1,0:T(8,128)(2,1)S(1)} %collective-permute-done.7.refs_0_.far_ref, bf16[2,512,256]{2,1,0:T(8,128)(2,1)S(1)} %copy-done.7, ...), custom_call_target="tpu_custom_call" | custom-call | bytes 4194304 | tf_op jit(solution)/shard_map/collect/pallas_call | solution.py:158
  143.7 12.2 %all-to-all-done.3.refs_0_ = bf16[64,112,128]{2,1,0:T(8,128)(2,1)S(1)} async-done(((bf16[64,112,128]{2,1,0:T(8,128)(2,1)}), bf16[64,112,128]{2,1,0:T(8,128)(2,1)S(1)}, u32[]{:S(2)}, u32[]{:S(2)}) %all-to-all-start.3) | async-done | bytes 1835040 | tf_op jit(solution)/shard_map/all_to_all | solution.py:703
  155.9 3.4 %collective-permute-start.14 = (bf16[28,256,128]{2,1,0:T(8,128)(2,1)S(1)}, bf16[28,256,128]{2,1,0:T(8,128)(2,1)S(1)}, u32[]{:S(2)}, u32[]{:S(2)}) collective-permute-start(bf16[28,256,128]{2,1,0:T(8,128)(2,1)S(1)} %bitcast.25), channel_id=1, source_target_pairs={{0,16},{16,0},{32,48},{48,32},{64,80},{80,64},{96,112},{112,96},{1... | collective-permute-start | bytes 5505032 | tf_op jit(solution)/shard_map/ppermute | solution.py:54
  159.3 2.2 %half.2.refs_0_ = f32[27,256,256]{2,1,0:T(8,128)} custom-call(s32[1]{0:T(128)} %bitcast.5.core_ref.refs_2_, bf16[28,256,128]{2,1,0:T(8,128)(2,1)S(1)} %bitcast.26), custom_call_target="tpu_custom_call" | custom-call | bytes 5308416 | tf_op jit(solution)/shard_map/half/pallas_call | solution.py:446
  162.7 2.2 %half.3 = f32[27,256,256]{2,1,0:T(8,128)} custom-call(s32[1]{0:T(128)} %bitcast.5.core_ref.refs_2_, bf16[28,256,128]{2,1,0:T(8,128)(2,1)S(1)} %collective-permute-done.14.block_ref, f32[27,256,256]{2,1,0:T(8,128)} %half.2.refs_0_), custom_call_target="tpu_custom_call", output_to_operand_aliasing={{}: (2, {})} | custom-call | bytes 5308416 | tf_op jit(solution)/shard_map/half/pallas_call | solution.py:446
  (152 shorter events, 26.5 us)
Async XLA Ops:
  3.7 22.1 %all-to-all-start.1 = ((bf16[8,256,256]{2,1,0:T(8,128)(2,1)}), bf16[8,256,256]{2,1,0:T(8,128)(2,1)S(1)}, u32[]{:S(2)}, u32[]{:S(2)}) async-start(bf16[8,256,256]{2,1,0:T(8,128)(2,1)} %get-tuple-element.51), calls=%async_computation.1 | async-start | bytes 2097152 | tf_op jit(solution)/shard_map/all_to_all | solution.py:676
  10.6 20.0 %copy-start.54 = (s32[4,6]{1,0:T(4,128)S(1)}, s32[4,6]{1,0:T(4,128)}, u32[]{:S(2)}) copy-start(s32[4,6]{1,0:T(4,128)} %param.9) | copy-start | bytes 292
  10.6 20.5 %copy-start.53 = (s32[4,1]{0,1:T(1,128)S(1)}, s32[4,1]{0,1:T(1,128)}, u32[]{:S(2)}) copy-start(s32[4,1]{0,1:T(1,128)} %param.8) | copy-start | bytes 52
  10.7 21.3 %copy-start.22 = (s32[4,1,512]{2,1,0:T(1,128)}, s32[4,1,512]{2,1,0:T(1,128)S(1)}, u32[]{:S(2)}) copy-start(s32[4,1,512]{2,1,0:T(1,128)S(1)} %reshape.35.occ_ref.refs_12_) | copy-start | bytes 24580
  12.8 19.1 %copy-start.32 = (bf16[4,64,256]{2,1,0:T(8,128)(2,1)}, bf16[4,64,256]{2,1,0:T(8,128)(2,1)S(1)}, u32[]{:S(2)}) copy-start(bf16[4,64,256]{2,1,0:T(8,128)(2,1)S(1)} %get-tuple-element.30.l2.refs_6_) | copy-start | bytes 393220
  12.8 19.0 %collective-permute-start.1 = (bf16[4,64,256]{2,1,0:T(8,128)(2,1)S(1)}, bf16[4,64,256]{2,1,0:T(8,128)(2,1)S(1)}, u32[]{:S(2)}, u32[]{:S(2)}) collective-permute-start(bf16[4,64,256]{2,1,0:T(8,128)(2,1)S(1)} %get-tuple-element.28.l0.refs_4_), channel_id=1, source_target_pairs={{0,112},{16,0},{32,16},{48,32},{64,48},{80,64},{96,80},{112,96},{1... | collective-permute-start | bytes 393224 | tf_op jit(solution)/shard_map/ppermute | solution.py:20
  12.9 19.0 %collective-permute-start = (bf16[4,64,256]{2,1,0:T(8,128)(2,1)S(1)}, bf16[4,64,256]{2,1,0:T(8,128)(2,1)S(1)}, u32[]{:S(2)}, u32[]{:S(2)}) collective-permute-start(bf16[4,64,256]{2,1,0:T(8,128)(2,1)S(1)} %get-tuple-element.29.l1.refs_5_), channel_id=1, source_target_pairs={{0,16},{16,32},{32,48},{48,64},{64,80},{80,96},{96,112},{112,0},{1... | collective-permute-start | bytes 393224 | tf_op jit(solution)/shard_map/ppermute | solution.py:20
  14.6 17.3 %collective-permute-start.2 = (bf16[4,64,256]{2,1,0:T(8,128)(2,1)S(1)}, bf16[4,64,256]{2,1,0:T(8,128)(2,1)S(1)}, u32[]{:S(2)}, u32[]{:S(2)}) collective-permute-start(bf16[4,64,256]{2,1,0:T(8,128)(2,1)S(1)} %get-tuple-element.30.l2.refs_6_), channel_id=1, source_target_pairs={{0,1},{1,2},{2,3},{3,4},{4,5},{5,6},{6,7},{7,8},{8,9},{9,10},{10,1... | collective-permute-start | bytes 393224 | tf_op jit(solution)/shard_map/ppermute | solution.py:31
  19.5 12.4 %collective-permute-start.3 = (bf16[4,64,256]{2,1,0:T(8,128)(2,1)S(1)}, bf16[4,64,256]{2,1,0:T(8,128)(2,1)S(1)}, u32[]{:S(2)}, u32[]{:S(2)}) collective-permute-start(bf16[4,64,256]{2,1,0:T(8,128)(2,1)S(1)} %get-tuple-element.31.l3.refs_7_), channel_id=1, source_target_pairs={{0,15},{1,0},{2,1},{3,2},{4,3},{5,4},{6,5},{7,6},{8,7},{9,8},{10,9... | collective-permute-start | bytes 393224 | tf_op jit(solution)/shard_map/ppermute | solution.py:31
  25.8 19.9 %all-to-all-start = ((bf16[8,256,256]{2,1,0:T(8,128)(2,1)}), bf16[8,256,256]{2,1,0:T(8,128)(2,1)S(1)}, u32[]{:S(2)}, u32[]{:S(2)}) async-start(bf16[8,256,256]{2,1,0:T(8,128)(2,1)} %get-tuple-element.52), calls=%async_computation | async-start | bytes 2097152 | tf_op jit(solution)/shard_map/all_to_all | solution.py:676
  47.6 18.9 %collective-permute-start.4 = (bf16[2,512,256]{2,1,0:T(8,128)(2,1)}, bf16[2,512,256]{2,1,0:T(8,128)(2,1)S(1)}, u32[]{:S(2)}, u32[]{:S(2)}) collective-permute-start(bf16[2,512,256]{2,1,0:T(8,128)(2,1)} %get-tuple-element.36), channel_id=1, source_target_pairs={{0,32},{16,112},{32,64},{48,16},{64,96},{80,48},{96,0},{112,80},{1... | collective-permute-start | bytes 1572872 | tf_op jit(solution)/shard_map/ppermute | solution.py:50
  50.1 17.7 %collective-permute-start.5 = (bf16[2,512,256]{2,1,0:T(8,128)(2,1)}, bf16[2,512,256]{2,1,0:T(8,128)(2,1)S(1)}, u32[]{:S(2)}, u32[]{:S(2)}) collective-permute-start(bf16[2,512,256]{2,1,0:T(8,128)(2,1)} %get-tuple-element.37), channel_id=1, source_target_pairs={{0,32},{16,112},{32,64},{48,16},{64,96},{80,48},{96,0},{112,80},{1... | collective-permute-start | bytes 1572872 | tf_op jit(solution)/shard_map/ppermute | solution.py:50
  50.7 17.1 %collective-permute-start.6 = (bf16[2,512,256]{2,1,0:T(8,128)(2,1)}, bf16[2,512,256]{2,1,0:T(8,128)(2,1)S(1)}, u32[]{:S(2)}, u32[]{:S(2)}) collective-permute-start(bf16[2,512,256]{2,1,0:T(8,128)(2,1)} %copy-done.15), channel_id=1, source_target_pairs={{0,96},{16,48},{32,0},{48,80},{64,32},{80,112},{96,64},{112,16},{1... | collective-permute-start | bytes 1572872 | tf_op jit(solution)/shard_map/ppermute | solution.py:50
  67.8 27.2 %copy-start.4 = (bf16[2,512,256]{2,1,0:T(8,128)(2,1)}, bf16[2,512,256]{2,1,0:T(8,128)(2,1)S(1)}, u32[]{:S(2)}) copy-start(bf16[2,512,256]{2,1,0:T(8,128)(2,1)S(1)} %get-tuple-element.41.near_ref) | copy-start | bytes 1572868
  67.8 14.7 %collective-permute-start.9 = (bf16[28,256,128]{2,1,0:T(8,128)(2,1)S(1)}, bf16[28,256,128]{2,1,0:T(8,128)(2,1)S(1)}, u32[]{:S(2)}, u32[]{:S(2)}) collective-permute-start(bf16[28,256,128]{2,1,0:T(8,128)(2,1)S(1)} %get-tuple-element.44), channel_id=1, source_target_pairs={{0,16},{16,0},{32,48},{48,32},{64,80},{80,64},{96,112},{112,96},{1... | collective-permute-start | bytes 5505032 | tf_op jit(solution)/shard_map/ppermute | solution.py:54
  70.4 12.1 %collective-permute-start.7 = (bf16[2,512,256]{2,1,0:T(8,128)(2,1)S(1)}, bf16[2,512,256]{2,1,0:T(8,128)(2,1)S(1)}, u32[]{:S(2)}, u32[]{:S(2)}) collective-permute-start(bf16[2,512,256]{2,1,0:T(8,128)(2,1)S(1)} %get-tuple-element.42), channel_id=1, source_target_pairs={{0,32},{16,112},{32,64},{48,16},{64,96},{80,48},{96,0},{112,80},{1... | collective-permute-start | bytes 1572872 | tf_op jit(solution)/shard_map/ppermute | solution.py:50
  84.7 39.4 %all-to-all-start.2 = ((bf16[64,112,128]{2,1,0:T(8,128)(2,1)}), bf16[64,112,128]{2,1,0:T(8,128)(2,1)S(1)}, u32[]{:S(2)}, u32[]{:S(2)}) async-start(bf16[64,112,128]{2,1,0:T(8,128)(2,1)} %bitcast.7), calls=%async_computation.2 | async-start | bytes 3670016 | tf_op jit(solution)/shard_map/all_to_all | solution.py:703
  96.2 24.9 %collective-permute-start.8 = (bf16[4,512,256]{2,1,0:T(8,128)(2,1)S(1)}, bf16[4,512,256]{2,1,0:T(8,128)(2,1)S(1)}, u32[]{:S(2)}, u32[]{:S(2)}) collective-permute-start(bf16[4,512,256]{2,1,0:T(8,128)(2,1)S(1)} %pad_maximum_fusion), channel_id=1, source_target_pairs={{0,16},{16,0},{32,48},{48,32},{64,80},{80,64},{96,112},{112,96},{1... | collective-permute-start | bytes 3145736 | tf_op jit(solution)/shard_map/ppermute | solution.py:54
  97.3 18.4 %collective-permute-start.10 = (bf16[4,64,256]{2,1,0:T(8,128)(2,1)S(1)}, bf16[4,64,256]{2,1,0:T(8,128)(2,1)S(1)}, u32[]{:S(2)}, u32[]{:S(2)}) collective-permute-start(bf16[4,64,256]{2,1,0:T(8,128)(2,1)S(1)} %copy-done.51), channel_id=1, source_target_pairs={{0,112},{16,0},{32,16},{48,32},{64,48},{80,64},{96,80},{112,96},{1... | collective-permute-start | bytes 393224 | tf_op jit(solution)/shard_map/ppermute | solution.py:20
  97.3 18.4 %collective-permute-start.11 = (bf16[4,64,256]{2,1,0:T(8,128)(2,1)S(1)}, bf16[4,64,256]{2,1,0:T(8,128)(2,1)S(1)}, u32[]{:S(2)}, u32[]{:S(2)}) collective-permute-start(bf16[4,64,256]{2,1,0:T(8,128)(2,1)S(1)} %copy-done.49), channel_id=1, source_target_pairs={{0,16},{16,32},{32,48},{48,64},{64,80},{80,96},{96,112},{112,0},{1... | collective-permute-start | bytes 393224 | tf_op jit(solution)/shard_map/ppermute | solution.py:20
  99.1 18.0 %collective-permute-start.12 = (bf16[4,64,256]{2,1,0:T(8,128)(2,1)S(1)}, bf16[4,64,256]{2,1,0:T(8,128)(2,1)S(1)}, u32[]{:S(2)}, u32[]{:S(2)}) collective-permute-start(bf16[4,64,256]{2,1,0:T(8,128)(2,1)S(1)} %copy-done.47), channel_id=1, source_target_pairs={{0,1},{1,2},{2,3},{3,4},{4,5},{5,6},{6,7},{7,8},{8,9},{9,10},{10,1... | collective-permute-start | bytes 393224 | tf_op jit(solution)/shard_map/ppermute | solution.py:31
  104.0 17.2 %collective-permute-start.13 = (bf16[4,64,256]{2,1,0:T(8,128)(2,1)S(1)}, bf16[4,64,256]{2,1,0:T(8,128)(2,1)S(1)}, u32[]{:S(2)}, u32[]{:S(2)}) collective-permute-start(bf16[4,64,256]{2,1,0:T(8,128)(2,1)S(1)} %copy-done.45), channel_id=1, source_target_pairs={{0,15},{1,0},{2,1},{3,2},{4,3},{5,4},{6,5},{7,6},{8,7},{9,8},{10,9... | collective-permute-start | bytes 393224 | tf_op jit(solution)/shard_map/ppermute | solution.py:31
  125.6 30.2 %all-to-all-start.3 = ((bf16[64,112,128]{2,1,0:T(8,128)(2,1)}), bf16[64,112,128]{2,1,0:T(8,128)(2,1)S(1)}, u32[]{:S(2)}, u32[]{:S(2)}) async-start(bf16[64,112,128]{2,1,0:T(8,128)(2,1)} %total.1.after_ref), calls=%async_computation.3 | async-start | bytes 3670016 | tf_op jit(solution)/shard_map/all_to_all | solution.py:703
  155.9 6.9 %collective-permute-start.14 = (bf16[28,256,128]{2,1,0:T(8,128)(2,1)S(1)}, bf16[28,256,128]{2,1,0:T(8,128)(2,1)S(1)}, u32[]{:S(2)}, u32[]{:S(2)}) collective-permute-start(bf16[28,256,128]{2,1,0:T(8,128)(2,1)S(1)} %bitcast.25), channel_id=1, source_target_pairs={{0,16},{16,0},{32,48},{48,32},{64,80},{80,64},{96,112},{112,96},{1... | collective-permute-start | bytes 5505032 | tf_op jit(solution)/shard_map/ppermute | solution.py:54
  (50 other events, 224.1 us)

commit v6 on v4

--- a/solution.py
+++ b/solution.py
@@ -161,7 +161,7 @@
         in_specs=[smem()] + [whole(own.shape)] * 4 + [whole(mate.shape)] + glance([after]),
         out_specs=whole(shape),
         out_shape=jax.ShapeDtypeStruct(shape, mate.dtype),
-        compiler_params=params(20),
+        compiler_params=params(56),
         cost_estimate=pl.CostEstimate(
             flops=0, bytes_accessed=4 * shape[0] * shape[1] * shape[2], transcendentals=0
         ),

time: 162 us -> 161 us (level)
    unnamed x85 -> x87, local copies, waits for them, and re-layouts: 3.51 us -> 1.92 us
  transfers between devices with their start and end apart: 19 -> 19, of which waited for: 8 -> 8; matrix products, arithmetic and copies ran while one was open for 2% -> 2% of each run, Pallas kernels for 31% -> 32%
where the time goes in v6:
time: 161 us; the launch traced here: 160 us
  Pallas kernels  56.4 us (35%)
  starting transfers between devices  52.3 us (32%)
  waiting for transfers between devices  41.7 us (26%)
  local copies, waits for them, and re-layouts  6.16 us (4%)
  other arithmetic  2.61 us (2%)
    all_to_all x2, starting transfers between devices, all_to_all(): lax.all_to_all(pieces, ('gx', 'gy'), 0, 0, axis_index_groups=same_core, t...  15.2 us
    pallas_call x1, Pallas kernels, weight_call(): pl.pallas_call(lambda *refs: weight_kernel(*refs, scale=scale), grid=(4,)...  14.8 us
    all_to_all x2, waiting for transfers between devices, all_to_all(): lax.all_to_all(pieces, ('gx', 'gy'), 0, 0, axis_index_groups=same_core, t...  14.7 us
    ppermute x4, waiting for transfers between devices, from_behind(): lax.ppermute(block, 'gx', [(i, (i + distance) % count) for i in range(cou...  12.9 us
    pallas_call x1, Pallas kernels, forward_call(): pl.pallas_call(forward_kernel, grid=(listed,), in_specs=[smem(), smem(),...  12.9 us
    all_to_all x2, starting transfers between devices, body(): lax.all_to_all(part, 'gx', 0, 0, tiled=True)  11.8 us
    pallas_call x1, Pallas kernels, data_call(): pl.pallas_call(data_kernel, grid=(listed,), in_specs=[smem(), smem(), by_...  11.1 us
    ppermute x4, starting transfers between devices, shifted(): return lax.ppermute(block, ('gx', 'gy'), ways)  9.84 us
  transfers between devices with their start and end apart: 19, of which 8 were waited for; matrix products, arithmetic and copies ran while one was open for 2% of the time, Pallas kernels for 32%

profile of v6, /device:TPU:1, one launch (start us, length us, event | category | flops | bytes accessed | tf_op | source)
XLA Modules:
  0.0 160.3 jit_solution(17659963827931727315)
XLA Ops:
  0.6 3.0 %fusion.10 = (bf16[8,256,256]{2,1,0:T(8,128)(2,1)}, bf16[8,256,256]{2,1,0:T(8,128)(2,1)}) fusion(bf16[8,512,256]{2,1,0:T(8,128)(2,1)} %param.11), kind=kLoop, calls=%fused_computation.36 | loop fusion | bytes 4194304 | tf_op jit(solution)/shard_map/slice | solution.py:677
  3.7 6.9 %all-to-all-start.1 = ((bf16[8,256,256]{2,1,0:T(8,128)(2,1)}), bf16[8,256,256]{2,1,0:T(8,128)(2,1)S(1)}, u32[]{:S(2)}, u32[]{:S(2)}) async-start(bf16[8,256,256]{2,1,0:T(8,128)(2,1)} %get-tuple-element.51), calls=%async_computation.1 | async-start | bytes 2097152 | tf_op jit(solution)/shard_map/all_to_all | solution.py:676
  12.9 1.7 %collective-permute-start = (bf16[4,64,256]{2,1,0:T(8,128)(2,1)S(1)}, bf16[4,64,256]{2,1,0:T(8,128)(2,1)S(1)}, u32[]{:S(2)}, u32[]{:S(2)}) collective-permute-start(bf16[4,64,256]{2,1,0:T(8,128)(2,1)S(1)} %get-tuple-element.29.l1.refs_5_), channel_id=1, source_target_pairs={{0,16},{16,32},{32,48},{48,64},{64,80},{80,96},{96,112},{112,0},{1... | collective-permute-start | bytes 393224 | tf_op jit(solution)/shard_map/ppermute | solution.py:20
  14.6 4.9 %collective-permute-start.2 = (bf16[4,64,256]{2,1,0:T(8,128)(2,1)S(1)}, bf16[4,64,256]{2,1,0:T(8,128)(2,1)S(1)}, u32[]{:S(2)}, u32[]{:S(2)}) collective-permute-start(bf16[4,64,256]{2,1,0:T(8,128)(2,1)S(1)} %get-tuple-element.30.l2.refs_6_), channel_id=1, source_target_pairs={{0,1},{1,2},{2,3},{3,4},{4,5},{5,6},{6,7},{7,8},{8,9},{9,10},{10,1... | collective-permute-start | bytes 393224 | tf_op jit(solution)/shard_map/ppermute | solution.py:31
  19.7 6.1 %all-to-all-done.1.refs_4_.refs_15_ = bf16[8,256,256]{2,1,0:T(8,128)(2,1)S(1)} async-done(((bf16[8,256,256]{2,1,0:T(8,128)(2,1)}), bf16[8,256,256]{2,1,0:T(8,128)(2,1)S(1)}, u32[]{:S(2)}, u32[]{:S(2)}) %all-to-all-start.1) | async-done | bytes 1048608 | tf_op jit(solution)/shard_map/all_to_all | solution.py:676
  25.8 4.8 %all-to-all-start = ((bf16[8,256,256]{2,1,0:T(8,128)(2,1)}), bf16[8,256,256]{2,1,0:T(8,128)(2,1)S(1)}, u32[]{:S(2)}, u32[]{:S(2)}) async-start(bf16[8,256,256]{2,1,0:T(8,128)(2,1)} %get-tuple-element.52), calls=%async_computation | async-start | bytes 2097152 | tf_op jit(solution)/shard_map/all_to_all | solution.py:676
  32.7 12.9 %forward.1 = (bf16[2,512,256]{2,1,0:T(8,128)(2,1)}, bf16[2,512,256]{2,1,0:T(8,128)(2,1)}, bf16[2,512,256]{2,1,0:T(8,128)(2,1)}, bf16[2,512,256]{2,1,0:T(8,128)(2,1)}) custom-call(s32[4,6]{1,0:T(4,128)} %or_select_fusion.near_ref.refs_0_, s32[4]{0:T(128)} %fusion.place_ref, s32[1]{0:T(128)} %bitcast.5.core_ref.refs_2_, bf16[4,512,256]{2,1,0:T(8,128)(2,1)} %copy-done.11, ...), custom_call_target="tpu_custom_call" | custom-call | flops 7247757312 | bytes 10485760 | tf_op jit(solution)/shard_map/forward/pallas_call | solution.py:287
  45.8 2.6 %collective-permute-start.4 = (bf16[2,512,256]{2,1,0:T(8,128)(2,1)}, bf16[2,512,256]{2,1,0:T(8,128)(2,1)S(1)}, u32[]{:S(2)}, u32[]{:S(2)}) collective-permute-start(bf16[2,512,256]{2,1,0:T(8,128)(2,1)} %get-tuple-element.36), channel_id=1, source_target_pairs={{0,32},{16,112},{32,64},{48,16},{64,96},{80,48},{96,0},{112,80},{1... | collective-permute-start | bytes 1572872 | tf_op jit(solution)/shard_map/ppermute | solution.py:50
  50.0 14.8 %weight_gradient.1 = (f32[28,256,128]{2,1,0:T(8,128)S(1)}, bf16[28,256,128]{2,1,0:T(8,128)(2,1)S(1)}, bf16[4,512,256]{2,1,0:T(8,128)(2,1)S(1)}) custom-call(s32[4,6]{1,0:T(4,128)S(1)} %copy-done.9, s32[4,1]{1,0:T(4,128)S(1)} %copy.18.refs_1_, s32[1]{0:T(128)} %bitcast.5.core_ref.refs_2_, bf16[4,512,256]{2,1,0:T(8,128)(2,1)S(1)} %copy-done.12, ...), custom_call_target="tpu_custom_call" | custom-call | flops 7247757312 | bytes 10485760 | tf_op jit(solution)/shard_map/weight_gradient/pallas_call | solution.py:370
  66.1 2.6 %collective-permute-start.9 = (bf16[28,256,128]{2,1,0:T(8,128)(2,1)S(1)}, bf16[28,256,128]{2,1,0:T(8,128)(2,1)S(1)}, u32[]{:S(2)}, u32[]{:S(2)}) collective-permute-start(bf16[28,256,128]{2,1,0:T(8,128)(2,1)S(1)} %get-tuple-element.44), channel_id=1, source_target_pairs={{0,16},{16,0},{32,48},{48,32},{64,80},{80,64},{96,112},{112,96},{1... | collective-permute-start | bytes 5505032 | tf_op jit(solution)/shard_map/ppermute | solution.py:54
  69.5 11.1 %data_gradient.1 = (f32[4,512,256]{2,1,0:T(8,128)S(1)}, bf16[4,64,256]{2,1,0:T(8,128)(2,1)S(1)}, bf16[4,64,256]{2,1,0:T(8,128)(2,1)S(1)}, bf16[4,64,256]{2,1,0:T(8,128)(2,1)S(1)}, bf16[4,64,256]{2,1,0:T(8,128)(2,1)S(1)}) custom-call(s32[4,6]{1,0:T(4,128)S(1)} %copy-done.9, s32[1]{0:T(128)} %bitcast.5.core_ref.refs_2_, ...), custom_call_target="tpu_custom_call" | custom-call | flops 8053063680 | bytes 10485760 | tf_op jit(solution)/shard_map/data_gradient/pallas_call | solution.py:590
  80.7 2.1 %chip_sum.1 = bf16[28,256,128]{2,1,0:T(8,128)(2,1)} custom-call(f32[28,256,128]{2,1,0:T(8,128)S(1)} %get-tuple-element.40.refs_4_.mine_ref, bf16[28,256,128]{2,1,0:T(8,128)(2,1)S(1)} %collective-permute-done.9.theirs_ref, bf16[2,512,256]{2,1,0:T(8,128)(2,1)S(1)} %collective-permute-done.7.refs_0_.far_ref, f32[4,512,256]{2,1,0:T(8,128)S(1)} %get-tuple-element.46.refs_1_.grad_ref), custom_call_target="tpu_custom_call" | custom-call | tf_op jit(solution)/shard_map/chip_sum/pallas_call | solution.py:405
  82.8 9.5 %all-to-all-start.2 = ((bf16[64,112,128]{2,1,0:T(8,128)(2,1)}), bf16[64,112,128]{2,1,0:T(8,128)(2,1)S(1)}, u32[]{:S(2)}, u32[]{:S(2)}) async-start(bf16[64,112,128]{2,1,0:T(8,128)(2,1)} %bitcast.7), calls=%async_computation.2 | async-start | bytes 3670016 | tf_op jit(solution)/shard_map/all_to_all | solution.py:703
  94.6 1.7 %collective-permute-start.11 = (bf16[4,64,256]{2,1,0:T(8,128)(2,1)S(1)}, bf16[4,64,256]{2,1,0:T(8,128)(2,1)S(1)}, u32[]{:S(2)}, u32[]{:S(2)}) collective-permute-start(bf16[4,64,256]{2,1,0:T(8,128)(2,1)S(1)} %copy-done.32), channel_id=1, source_target_pairs={{0,16},{16,32},{32,48},{48,64},{64,80},{80,96},{96,112},{112,0},{1... | collective-permute-start | bytes 393224 | tf_op jit(solution)/shard_map/ppermute | solution.py:20
  96.3 4.9 %collective-permute-start.12 = (bf16[4,64,256]{2,1,0:T(8,128)(2,1)S(1)}, bf16[4,64,256]{2,1,0:T(8,128)(2,1)S(1)}, u32[]{:S(2)}, u32[]{:S(2)}) collective-permute-start(bf16[4,64,256]{2,1,0:T(8,128)(2,1)S(1)} %copy-done.30), channel_id=1, source_target_pairs={{0,1},{1,2},{2,3},{3,4},{4,5},{5,6},{6,7},{7,8},{8,9},{9,10},{10,1... | collective-permute-start | bytes 393224 | tf_op jit(solution)/shard_map/ppermute | solution.py:31
  101.2 12.9 %collective-permute-done.10.r0 = bf16[4,64,256]{2,1,0:T(8,128)(2,1)S(1)} collective-permute-done((bf16[4,64,256]{2,1,0:T(8,128)(2,1)S(1)}, bf16[4,64,256]{2,1,0:T(8,128)(2,1)S(1)}, u32[]{:S(2)}, u32[]{:S(2)}) %collective-permute-start.10) | collective-permute-done | bytes 131104 | tf_op jit(solution)/shard_map/ppermute | solution.py:20
  115.5 4.0 %collective-permute-done.13.rb = bf16[4,64,256]{2,1,0:T(8,128)(2,1)S(1)} collective-permute-done((bf16[4,64,256]{2,1,0:T(8,128)(2,1)S(1)}, bf16[4,64,256]{2,1,0:T(8,128)(2,1)S(1)}, u32[]{:S(2)}, u32[]{:S(2)}) %collective-permute-start.13) | collective-permute-done | bytes 131104 | tf_op jit(solution)/shard_map/ppermute | solution.py:31
  121.1 5.8 %all-to-all-start.3 = ((bf16[64,112,128]{2,1,0:T(8,128)(2,1)}), bf16[64,112,128]{2,1,0:T(8,128)(2,1)S(1)}, u32[]{:S(2)}, u32[]{:S(2)}) async-start(bf16[64,112,128]{2,1,0:T(8,128)(2,1)} %total.1.after_ref), calls=%async_computation.3 | async-start | bytes 3670016 | tf_op jit(solution)/shard_map/all_to_all | solution.py:703
  127.4 5.0 %input_gradient.1 = bf16[4,512,256]{2,1,0:T(8,128)(2,1)} custom-call(s32[1]{0:T(128)} %bitcast.5.core_ref.refs_2_, f32[4,512,256]{2,1,0:T(8,128)} %copy-done, bf16[4,64,256]{2,1,0:T(8,128)(2,1)} %copy-done.36, bf16[4,64,256]{2,1,0:T(8,128)(2,1)} %copy-done.37, bf16[4,64,256]{2,1,0:T(8,128)(2,1)} %copy-done.38, bf16[4,64,256]{2,1,0:T(8,128)(2,1)} %copy-done.39, ...), custom_call_target="tpu_custom_call" | custom-call | bytes 5242880 | tf_op jit(solution)/shard_map/input_gradient/pallas_call | solution.py:632
  132.4 3.3 %collect.1 = bf16[8,512,256]{2,1,0:T(8,128)(2,1)} custom-call(s32[8]{0:T(128)} %fusion.4.place_ref, bf16[2,512,256]{2,1,0:T(8,128)(2,1)} %get-tuple-element.32.refs_13_.own_ref, bf16[2,512,256]{2,1,0:T(8,128)(2,1)} %copy-done.3, bf16[2,512,256]{2,1,0:T(8,128)(2,1)} %copy-done.2, bf16[2,512,256]{2,1,0:T(8,128)(2,1)} %copy-done.4, ...), custom_call_target="tpu_custom_call" | custom-call | bytes 4194304 | tf_op jit(solution)/shard_map/collect/pallas_call | solution.py:158
  136.5 14.7 %all-to-all-done.3.refs_0_ = bf16[64,112,128]{2,1,0:T(8,128)(2,1)S(1)} async-done(((bf16[64,112,128]{2,1,0:T(8,128)(2,1)}), bf16[64,112,128]{2,1,0:T(8,128)(2,1)S(1)}, u32[]{:S(2)}, u32[]{:S(2)}) %all-to-all-start.3) | async-done | bytes 1835040 | tf_op jit(solution)/shard_map/all_to_all | solution.py:703
  151.2 3.5 %collective-permute-start.14 = (bf16[28,256,128]{2,1,0:T(8,128)(2,1)S(1)}, bf16[28,256,128]{2,1,0:T(8,128)(2,1)S(1)}, u32[]{:S(2)}, u32[]{:S(2)}) collective-permute-start(bf16[28,256,128]{2,1,0:T(8,128)(2,1)S(1)} %bitcast.25), channel_id=1, source_target_pairs={{0,16},{16,0},{32,48},{48,32},{64,80},{80,64},{96,112},{112,96},{1... | collective-permute-start | bytes 5505032 | tf_op jit(solution)/shard_map/ppermute | solution.py:54
  154.7 2.2 %half.2.refs_0_ = f32[27,256,256]{2,1,0:T(8,128)} custom-call(s32[1]{0:T(128)} %bitcast.5.core_ref.refs_2_, bf16[28,256,128]{2,1,0:T(8,128)(2,1)S(1)} %bitcast.26), custom_call_target="tpu_custom_call" | custom-call | bytes 5308416 | tf_op jit(solution)/shard_map/half/pallas_call | solution.py:446
  158.2 2.2 %half.3 = f32[27,256,256]{2,1,0:T(8,128)} custom-call(s32[1]{0:T(128)} %bitcast.5.core_ref.refs_2_, bf16[28,256,128]{2,1,0:T(8,128)(2,1)S(1)} %collective-permute-done.14.block_ref, f32[27,256,256]{2,1,0:T(8,128)} %half.2.refs_0_), custom_call_target="tpu_custom_call", output_to_operand_aliasing={{}: (2, {})} | custom-call | bytes 5308416 | tf_op jit(solution)/shard_map/half/pallas_call | solution.py:446
  (128 shorter events, 15.8 us)
Async XLA Ops:
  3.7 22.1 %all-to-all-start.1 = ((bf16[8,256,256]{2,1,0:T(8,128)(2,1)}), bf16[8,256,256]{2,1,0:T(8,128)(2,1)S(1)}, u32[]{:S(2)}, u32[]{:S(2)}) async-start(bf16[8,256,256]{2,1,0:T(8,128)(2,1)} %get-tuple-element.51), calls=%async_computation.1 | async-start | bytes 2097152 | tf_op jit(solution)/shard_map/all_to_all | solution.py:676
  10.6 20.0 %copy-start.42 = (s32[4,6]{1,0:T(4,128)S(1)}, s32[4,6]{1,0:T(4,128)}, u32[]{:S(2)}) copy-start(s32[4,6]{1,0:T(4,128)} %param.9) | copy-start | bytes 292
  10.6 20.6 %copy-start.41 = (s32[4,1]{0,1:T(1,128)S(1)}, s32[4,1]{0,1:T(1,128)}, u32[]{:S(2)}) copy-start(s32[4,1]{0,1:T(1,128)} %param.8) | copy-start | bytes 52
  10.7 21.3 %copy-start.7 = (s32[4,1,512]{2,1,0:T(1,128)}, s32[4,1,512]{2,1,0:T(1,128)S(1)}, u32[]{:S(2)}) copy-start(s32[4,1,512]{2,1,0:T(1,128)S(1)} %reshape.35.occ_ref.refs_12_) | copy-start | bytes 24580
  12.8 19.0 %collective-permute-start.1 = (bf16[4,64,256]{2,1,0:T(8,128)(2,1)S(1)}, bf16[4,64,256]{2,1,0:T(8,128)(2,1)S(1)}, u32[]{:S(2)}, u32[]{:S(2)}) collective-permute-start(bf16[4,64,256]{2,1,0:T(8,128)(2,1)S(1)} %get-tuple-element.28.l0.refs_4_), channel_id=1, source_target_pairs={{0,112},{16,0},{32,16},{48,32},{64,48},{80,64},{96,80},{112,96},{1... | collective-permute-start | bytes 393224 | tf_op jit(solution)/shard_map/ppermute | solution.py:20
  12.9 19.0 %collective-permute-start = (bf16[4,64,256]{2,1,0:T(8,128)(2,1)S(1)}, bf16[4,64,256]{2,1,0:T(8,128)(2,1)S(1)}, u32[]{:S(2)}, u32[]{:S(2)}) collective-permute-start(bf16[4,64,256]{2,1,0:T(8,128)(2,1)S(1)} %get-tuple-element.29.l1.refs_5_), channel_id=1, source_target_pairs={{0,16},{16,32},{32,48},{48,64},{64,80},{80,96},{96,112},{112,0},{1... | collective-permute-start | bytes 393224 | tf_op jit(solution)/shard_map/ppermute | solution.py:20
  14.6 17.3 %collective-permute-start.2 = (bf16[4,64,256]{2,1,0:T(8,128)(2,1)S(1)}, bf16[4,64,256]{2,1,0:T(8,128)(2,1)S(1)}, u32[]{:S(2)}, u32[]{:S(2)}) collective-permute-start(bf16[4,64,256]{2,1,0:T(8,128)(2,1)S(1)} %get-tuple-element.30.l2.refs_6_), channel_id=1, source_target_pairs={{0,1},{1,2},{2,3},{3,4},{4,5},{5,6},{6,7},{7,8},{8,9},{9,10},{10,1... | collective-permute-start | bytes 393224 | tf_op jit(solution)/shard_map/ppermute | solution.py:31
  19.5 12.4 %collective-permute-start.3 = (bf16[4,64,256]{2,1,0:T(8,128)(2,1)S(1)}, bf16[4,64,256]{2,1,0:T(8,128)(2,1)S(1)}, u32[]{:S(2)}, u32[]{:S(2)}) collective-permute-start(bf16[4,64,256]{2,1,0:T(8,128)(2,1)S(1)} %get-tuple-element.31.l3.refs_7_), channel_id=1, source_target_pairs={{0,15},{1,0},{2,1},{3,2},{4,3},{5,4},{6,5},{7,6},{8,7},{9,8},{10,9... | collective-permute-start | bytes 393224 | tf_op jit(solution)/shard_map/ppermute | solution.py:31
  25.8 19.9 %all-to-all-start = ((bf16[8,256,256]{2,1,0:T(8,128)(2,1)}), bf16[8,256,256]{2,1,0:T(8,128)(2,1)S(1)}, u32[]{:S(2)}, u32[]{:S(2)}) async-start(bf16[8,256,256]{2,1,0:T(8,128)(2,1)} %get-tuple-element.52), calls=%async_computation | async-start | bytes 2097152 | tf_op jit(solution)/shard_map/all_to_all | solution.py:676
  45.8 19.1 %collective-permute-start.4 = (bf16[2,512,256]{2,1,0:T(8,128)(2,1)}, bf16[2,512,256]{2,1,0:T(8,128)(2,1)S(1)}, u32[]{:S(2)}, u32[]{:S(2)}) collective-permute-start(bf16[2,512,256]{2,1,0:T(8,128)(2,1)} %get-tuple-element.36), channel_id=1, source_target_pairs={{0,32},{16,112},{32,64},{48,16},{64,96},{80,48},{96,0},{112,80},{1... | collective-permute-start | bytes 1572872 | tf_op jit(solution)/shard_map/ppermute | solution.py:50
  48.4 17.7 %collective-permute-start.5 = (bf16[2,512,256]{2,1,0:T(8,128)(2,1)}, bf16[2,512,256]{2,1,0:T(8,128)(2,1)S(1)}, u32[]{:S(2)}, u32[]{:S(2)}) collective-permute-start(bf16[2,512,256]{2,1,0:T(8,128)(2,1)} %get-tuple-element.37), channel_id=1, source_target_pairs={{0,32},{16,112},{32,64},{48,16},{64,96},{80,48},{96,0},{112,80},{1... | collective-permute-start | bytes 1572872 | tf_op jit(solution)/shard_map/ppermute | solution.py:50
  49.0 17.1 %collective-permute-start.6 = (bf16[2,512,256]{2,1,0:T(8,128)(2,1)}, bf16[2,512,256]{2,1,0:T(8,128)(2,1)S(1)}, u32[]{:S(2)}, u32[]{:S(2)}) collective-permute-start(bf16[2,512,256]{2,1,0:T(8,128)(2,1)} %get-tuple-element.38), channel_id=1, source_target_pairs={{0,96},{16,48},{32,0},{48,80},{64,32},{80,112},{96,64},{112,16},{1... | collective-permute-start | bytes 1572872 | tf_op jit(solution)/shard_map/ppermute | solution.py:50
  66.1 27.3 %copy-start.3 = (bf16[2,512,256]{2,1,0:T(8,128)(2,1)}, bf16[2,512,256]{2,1,0:T(8,128)(2,1)S(1)}, u32[]{:S(2)}) copy-start(bf16[2,512,256]{2,1,0:T(8,128)(2,1)S(1)} %get-tuple-element.41.near_ref) | copy-start | bytes 1572868
  66.1 27.3 %copy-start.4 = (bf16[2,512,256]{2,1,0:T(8,128)(2,1)}, bf16[2,512,256]{2,1,0:T(8,128)(2,1)S(1)}, u32[]{:S(2)}) copy-start(bf16[2,512,256]{2,1,0:T(8,128)(2,1)S(1)} %get-tuple-element.43.back_ref) | copy-start | bytes 1572868
  66.1 14.6 %collective-permute-start.9 = (bf16[28,256,128]{2,1,0:T(8,128)(2,1)S(1)}, bf16[28,256,128]{2,1,0:T(8,128)(2,1)S(1)}, u32[]{:S(2)}, u32[]{:S(2)}) collective-permute-start(bf16[28,256,128]{2,1,0:T(8,128)(2,1)S(1)} %get-tuple-element.44), channel_id=1, source_target_pairs={{0,16},{16,0},{32,48},{48,32},{64,80},{80,64},{96,112},{112,96},{1... | collective-permute-start | bytes 5505032 | tf_op jit(solution)/shard_map/ppermute | solution.py:54
  68.6 12.0 %collective-permute-start.7 = (bf16[2,512,256]{2,1,0:T(8,128)(2,1)S(1)}, bf16[2,512,256]{2,1,0:T(8,128)(2,1)S(1)}, u32[]{:S(2)}, u32[]{:S(2)}) collective-permute-start(bf16[2,512,256]{2,1,0:T(8,128)(2,1)S(1)} %get-tuple-element.42), channel_id=1, source_target_pairs={{0,32},{16,112},{32,64},{48,16},{64,96},{80,48},{96,0},{112,80},{1... | collective-permute-start | bytes 1572872 | tf_op jit(solution)/shard_map/ppermute | solution.py:50
  82.8 36.6 %all-to-all-start.2 = ((bf16[64,112,128]{2,1,0:T(8,128)(2,1)}), bf16[64,112,128]{2,1,0:T(8,128)(2,1)S(1)}, u32[]{:S(2)}, u32[]{:S(2)}) async-start(bf16[64,112,128]{2,1,0:T(8,128)(2,1)} %bitcast.7), calls=%async_computation.2 | async-start | bytes 3670016 | tf_op jit(solution)/shard_map/all_to_all | solution.py:703
  93.6 25.8 %collective-permute-start.8 = (bf16[4,512,256]{2,1,0:T(8,128)(2,1)S(1)}, bf16[4,512,256]{2,1,0:T(8,128)(2,1)S(1)}, u32[]{:S(2)}, u32[]{:S(2)}) collective-permute-start(bf16[4,512,256]{2,1,0:T(8,128)(2,1)S(1)} %pad_maximum_fusion), channel_id=1, source_target_pairs={{0,16},{16,0},{32,48},{48,32},{64,80},{80,64},{96,112},{112,96},{1... | collective-permute-start | bytes 3145736 | tf_op jit(solution)/shard_map/ppermute | solution.py:54
  94.6 19.5 %collective-permute-start.10 = (bf16[4,64,256]{2,1,0:T(8,128)(2,1)S(1)}, bf16[4,64,256]{2,1,0:T(8,128)(2,1)S(1)}, u32[]{:S(2)}, u32[]{:S(2)}) collective-permute-start(bf16[4,64,256]{2,1,0:T(8,128)(2,1)S(1)} %copy-done.34), channel_id=1, source_target_pairs={{0,112},{16,0},{32,16},{48,32},{64,48},{80,64},{96,80},{112,96},{1... | collective-permute-start | bytes 393224 | tf_op jit(solution)/shard_map/ppermute | solution.py:20
  94.6 19.5 %collective-permute-start.11 = (bf16[4,64,256]{2,1,0:T(8,128)(2,1)S(1)}, bf16[4,64,256]{2,1,0:T(8,128)(2,1)S(1)}, u32[]{:S(2)}, u32[]{:S(2)}) collective-permute-start(bf16[4,64,256]{2,1,0:T(8,128)(2,1)S(1)} %copy-done.32), channel_id=1, source_target_pairs={{0,16},{16,32},{32,48},{48,64},{64,80},{80,96},{96,112},{112,0},{1... | collective-permute-start | bytes 393224 | tf_op jit(solution)/shard_map/ppermute | solution.py:20
  96.3 19.1 %collective-permute-start.12 = (bf16[4,64,256]{2,1,0:T(8,128)(2,1)S(1)}, bf16[4,64,256]{2,1,0:T(8,128)(2,1)S(1)}, u32[]{:S(2)}, u32[]{:S(2)}) collective-permute-start(bf16[4,64,256]{2,1,0:T(8,128)(2,1)S(1)} %copy-done.30), channel_id=1, source_target_pairs={{0,1},{1,2},{2,3},{3,4},{4,5},{5,6},{6,7},{7,8},{8,9},{9,10},{10,1... | collective-permute-start | bytes 393224 | tf_op jit(solution)/shard_map/ppermute | solution.py:31
  101.2 18.2 %collective-permute-start.13 = (bf16[4,64,256]{2,1,0:T(8,128)(2,1)S(1)}, bf16[4,64,256]{2,1,0:T(8,128)(2,1)S(1)}, u32[]{:S(2)}, u32[]{:S(2)}) collective-permute-start(bf16[4,64,256]{2,1,0:T(8,128)(2,1)S(1)} %get-tuple-element.50), channel_id=1, source_target_pairs={{0,15},{1,0},{2,1},{3,2},{4,3},{5,4},{6,5},{7,6},{8,7},{9,8},{10,9... | collective-permute-start | bytes 393224 | tf_op jit(solution)/shard_map/ppermute | solution.py:31
  121.1 30.1 %all-to-all-start.3 = ((bf16[64,112,128]{2,1,0:T(8,128)(2,1)}), bf16[64,112,128]{2,1,0:T(8,128)(2,1)S(1)}, u32[]{:S(2)}, u32[]{:S(2)}) async-start(bf16[64,112,128]{2,1,0:T(8,128)(2,1)} %total.1.after_ref), calls=%async_computation.3 | async-start | bytes 3670016 | tf_op jit(solution)/shard_map/all_to_all | solution.py:703
  151.2 6.9 %collective-permute-start.14 = (bf16[28,256,128]{2,1,0:T(8,128)(2,1)S(1)}, bf16[28,256,128]{2,1,0:T(8,128)(2,1)S(1)}, u32[]{:S(2)}, u32[]{:S(2)}) collective-permute-start(bf16[28,256,128]{2,1,0:T(8,128)(2,1)S(1)} %bitcast.25), channel_id=1, source_target_pairs={{0,16},{16,0},{32,48},{48,32},{64,80},{80,64},{96,112},{112,96},{1... | collective-permute-start | bytes 5505032 | tf_op jit(solution)/shard_map/ppermute | solution.py:54
  (38 other events, 206.1 us)
